TPU v7x, 256 devices: a whole 4x4x8 slice. The times are simulated.
256 devices in a mesh: depth: 8 (over x, y_lo), tile: 32 (over y_hi, z, core).
Axes of the slice: x: 4, y: 4 (y_hi: 2, y_lo: 2; y = y_hi * 2 + y_lo), z: 8, core: 2. Of those that a mesh axis runs over, the one named last changes fastest.
Arguments:
- scene_layers: bfloat16 [8, 4096, 256], P('depth', 'tile'), may hold values from -6 to 6
- sensor_grad: bfloat16 [4096, 256], P('tile'), may hold values from -0.0059814453 to 0.0059814453
- pupil_phase: float32 [1024, 1024], P('tile', 'depth'), may hold values from -3.140625 to 3.140625
- defocus_index: int32 [8], P('depth'), may hold values from -6 to 6
Outputs:
- phase_grad: float32 [1024, 1024], P('tile', 'depth')
All inputs are finite; a program needn't handle non-finite values.
Results may differ from a plain program's by a relative error of at most 0.0003.
Values may be sent and summed in bfloat16 or wider, within the bound.
No kernel may reach another device: no remote copies, remote signals or barrier semaphores. Data moves between devices by JAX's collectives and lax.ppermute only.
A program may use at most 64 MiB of HBM per device.

v0:
```python
import jax
import jax.numpy as jnp
from jax import lax
from jax.sharding import PartitionSpec as P

PUPIL = 1024
HALF = 128


two_pi = 6.283185307179586
defocus_step = 0.5
row_block = 8


def with_halo(x, sides, width):
    for axis, dim in sides:
        devices, length = (lax.axis_size(axis), x.shape[dim])
        up = [(i, (i + 1) % devices) for i in range(devices - 1)]
        down = [(j, i) for i, j in up]
        last = lax.slice_in_dim(x, length - width, length, axis=dim)
        leading = lax.slice_in_dim(x, 0, width, axis=dim)
        before = lax.ppermute(last, axis, up)
        after = lax.ppermute(leading, axis, down)
        x = jnp.concatenate([before, x, after], axis=dim)
    return x


def freq_tables(first_row, row_count, pupil_size, half_width):
    wave_index = (jnp.arange(2 * half_width, dtype=jnp.int32) - half_width)[:, None]
    pupil_index = (jnp.arange(row_count, dtype=jnp.int32) + first_row)[None, :]
    phase_angle = jnp.mod(wave_index * pupil_index, pupil_size).astype(jnp.float32) * (
        two_pi / pupil_size
    )
    unit_scale = pupil_size ** (-0.5)
    return (jnp.cos(phase_angle) * unit_scale, -jnp.sin(phase_angle) * unit_scale)


def pupil_terms(first_row, row_count, pupil_size):
    pupil_rows = (jnp.arange(row_count, dtype=jnp.int32) + first_row).astype(jnp.float32)[:, None]
    pupil_cols = jnp.arange(pupil_size, dtype=jnp.int32).astype(jnp.float32)[None, :]
    centre = (pupil_size - 1) / 2.0
    radius = (pupil_rows - centre) ** 2 + (pupil_cols - centre) ** 2
    limit = (pupil_size / 2.0) ** 2
    inside = (radius <= limit).astype(jnp.float32)
    return (inside, radius / limit)


def highest(left, right):
    return jnp.dot(left, right, precision=lax.Precision.HIGHEST)


def correlate(extended, sensor_tile):
    grad_rows, grad_cols = sensor_tile.shape
    out_rows = extended.shape[0] - grad_rows + 1
    width = extended.shape[1]
    period = width + out_rows - 1

    def window_at(offset):
        return lax.dynamic_slice_in_dim(extended, offset, out_rows, 0)

    def one_block(step, total):
        start = step * row_block
        offsets = start + jnp.arange(row_block, dtype=jnp.int32)
        windows = jax.vmap(window_at)(offsets)
        block_rows = lax.dynamic_slice_in_dim(sensor_tile, start, row_block, 0)
        padded = jnp.pad(block_rows, ((0, 0), (0, period - grad_cols)))
        repeated = jnp.tile(padded, (1, out_rows))[:, : out_rows * (period - 1)]
        toeplitz = repeated.reshape(row_block, out_rows, period - 1)[:, :, :width]
        return total + jnp.einsum(
            "bic,bjc->ij", windows, toeplitz, preferred_element_type=jnp.float32
        )

    start_total = jnp.zeros((out_rows, out_rows), jnp.float32)
    return lax.fori_loop(0, grad_rows // row_block, one_block, start_total)


def body(scene_layers, sensor_grad, pupil_phase, defocus_index):
    tile_rows = scene_layers.shape[1]
    row_count = pupil_phase.shape[0]
    first_row = lax.axis_index("tile") * row_count
    full_rows = lax.all_gather(pupil_phase, "depth", axis=1, tiled=True)
    cos_table, sin_table = freq_tables(first_row, row_count, PUPIL, HALF)
    column_cos, column_sin = freq_tables(0, PUPIL, PUPIL, HALF)
    inside, defocus_map = pupil_terms(first_row, row_count, PUPIL)
    extended_all = with_halo(scene_layers, (("tile", 1),), HALF)
    theta = full_rows + defocus_index[0].astype(jnp.float32) * defocus_step * defocus_map
    field_re = inside * jnp.cos(theta)
    field_im = inside * jnp.sin(theta)
    z_re = highest(field_re, column_cos.T) - highest(field_im, column_sin.T)
    z_im = highest(field_re, column_sin.T) + highest(field_im, column_cos.T)
    part_re = highest(cos_table, z_re) - highest(sin_table, z_im)
    part_im = highest(cos_table, z_im) + highest(sin_table, z_re)
    extended = jnp.pad(extended_all[0, : tile_rows + 2 * HALF - 1], ((0, 0), (HALF, HALF - 1)))
    kernel_part_local = correlate(extended, sensor_grad)
    y_re, y_im = lax.psum((part_re, part_im), "tile")
    kernel_grad = lax.psum(kernel_part_local, "tile")
    gy_re = 2.0 * kernel_grad * y_re
    gy_im = 2.0 * kernel_grad * y_im
    gz_re = highest(cos_table.T, gy_re) + highest(sin_table.T, gy_im)
    gz_im = highest(cos_table.T, gy_im) - highest(sin_table.T, gy_re)
    ge_re = highest(gz_re, column_cos) + highest(gz_im, column_sin)
    ge_im = highest(gz_im, column_cos) - highest(gz_re, column_sin)
    phase_total = field_re * ge_im - field_im * ge_re
    return lax.psum_scatter(phase_total, "depth", scatter_dimension=1, tiled=True)


def solution(mesh):
    placed = (P("depth", "tile", None), P("tile", None), P("tile", "depth"), P("depth"))
    return jax.shard_map(
        body, mesh=mesh, in_specs=placed, out_specs=P("tile", "depth"), check_vma=False
    )
```

profile of v0, /device:TPU:16, one launch (start us, length us, event | category | flops | bytes accessed | tf_op | source)
XLA Modules:
  0.0 1126.6 jit_solution(8230766685340689897)
XLA Ops:
  15.8 28.5 %all_gather.3 = f32[32,1024]{1,0:T(8,128)S(1)} all-gather(f32[32,128]{1,0:T(8,128)} %param.8), channel_id=1, replica_groups=mesh['depth'=8,'tile'=32] {'depth'}, dimensions={1}, use_global_device_ids=true | all-gather | bytes 147456 | tf_op jit(solution)/shard_map/all_gather | solution.py:81
  71.0 716.2 %while.20 = (s32[]{:T(128)}, f32[256,256]{1,0:T(8,128)}, bf16[383,511]{1,0:T(8,128)(2,1)S(1)}, bf16[128,256]{1,0:T(8,128)(2,1)}, s32[]{:T(128)}, /*index=5*/s32[...) while((s32[]{:T(128)}, f32[256,256]{1,0:T(8,128)}, bf16[383,511]{1,0:T(8,128)(2,1)S(1)}, ...), condition=%wide.region_1.2_spmd.clone, body=%wide.region_0.1_spmd.clone.sunk | while | flops 535953440 | bytes 41861552 | solution.py:74
  72.1 8.0 reshape.86
  93.6 8.7 reshape.88
  102.3 10.4 while.21
  116.8 8.0 reshape.86
  138.3 8.7 reshape.88
  147.0 10.4 while.21
  161.5 8.0 reshape.86
  183.1 8.7 reshape.88
  191.8 10.4 while.21
  206.3 8.0 reshape.86
  227.8 8.7 reshape.88
  236.5 10.4 while.21
  251.0 8.0 reshape.86
  272.5 8.7 reshape.88
  281.2 10.4 while.21
  295.7 8.0 reshape.86
  317.2 8.7 reshape.88
  325.9 10.4 while.21
  340.4 8.0 reshape.86
  362.0 8.7 reshape.88
  370.7 10.4 while.21
  385.1 8.0 reshape.86
  406.7 8.7 reshape.88
  415.4 10.4 while.21
  451.4 8.7 reshape.88
  460.1 10.4 while.21
  474.6 8.0 reshape.86
  496.1 8.7 reshape.88
  504.8 10.4 while.21
  540.9 8.7 reshape.88
  549.6 10.4 while.21
  564.0 8.0 reshape.86
  585.6 8.7 reshape.88
  594.3 10.4 while.21
  630.3 8.7 reshape.88
  639.0 10.4 while.21
  653.5 8.0 reshape.86
  675.0 8.7 reshape.88
  683.7 10.4 while.21
  719.7 8.7 reshape.88
  728.5 10.4 while.21
  742.9 8.0 reshape.86
  764.5 8.7 reshape.88
  773.2 10.4 while.21
  787.2 266.9 %all-reduce.6.cloned.1.call-done = (f32[256,256]{1,0:T(8,128)}, f32[256,256]{1,0:T(8,128)}, f32[256,256]{1,0:T(8,128)}) async-done(((f32[256,256]{1,0:T(8,128)}, f32[256,256]{1,0:T(8,128)}, f32[256,256]{1,0:T(8,128)}), (f32[256,256]{1,0:T(8,128)}, f32[256,256]{1,0:T(8,128)}, f32[256,256]{1,0:T(8,128)})) %all-reduce.6.cloned.1.call-update) | async-done | bytes 786448 | tf_op jit(solution)/shard_map/psum | solution.py:95
  1081.0 38.6 %reduce-scatter.2.cloned.1.call-done = f32[32,128]{1,0:T(8,128)} async-done(((f32[32,1024]{1,0:T(8,128)}), f32[32,128]{1,0:T(8,128)}) %reduce-scatter.2.cloned.1.call-update) | async-done | bytes 16400 | tf_op jit(solution)/shard_map/reduce_scatter | solution.py:104
  (653 shorter events, 538.9 us)
Async XLA Ops:
  6.5 1047.5 %all-reduce.6.cloned.1.call-start = ((), (), s32[]{:S(2)}) async-start(), calls=%async_computation.2 | async-start | bytes 1572864 | tf_op jit(solution)/shard_map/psum | solution.py:95
  6.5 64.4 %collective-permute-start = (bf16[1,128,256]{2,1,0:T(8,128)(2,1)}, bf16[1,128,256]{2,1,0:T(8,128)(2,1)S(1)}, u32[]{:S(2)}, u32[]{:S(2)}) collective-permute-start(bf16[1,128,256]{2,1,0:T(8,128)(2,1)} %param.6), channel_id=1, source_target_pairs={{0,1},{1,2},{2,3},{3,4},{4,5},{5,6},{6,7},{7,8},{8,9},{9,10},{10,1... | collective-permute-start | bytes 196616 | tf_op jit(solution)/shard_map/ppermute | solution.py:22
  8.5 62.4 %collective-permute-start.1 = (bf16[1,128,256]{2,1,0:T(8,128)(2,1)}, bf16[1,128,256]{2,1,0:T(8,128)(2,1)S(1)}, u32[]{:S(2)}, u32[]{:S(2)}) collective-permute-start(bf16[1,128,256]{2,1,0:T(8,128)(2,1)} %param.6), channel_id=1, source_target_pairs={{1,0},{2,1},{3,2},{4,3},{5,4},{6,5},{7,6},{8,7},{9,8},{10,9},{11,1... | collective-permute-start | bytes 196616 | tf_op jit(solution)/shard_map/ppermute | solution.py:23
  44.2 16.6 %copy-start.2 = (f32[32,1024]{1,0:T(8,128)}, f32[32,1024]{1,0:T(8,128)S(1)}, u32[]{:S(2)}) copy-start(f32[32,1024]{1,0:T(8,128)S(1)} %all_gather.3) | copy-start | bytes 393220
  66.0 4.9 copy-start.4
  102.3 10.4 copy-start
  115.2 0.7 copy-start.1
  147.0 10.4 copy-start
  159.9 0.7 copy-start.1
  191.7 10.4 copy-start
  204.6 0.7 copy-start.1
  236.5 10.4 copy-start
  249.4 0.7 copy-start.1
  281.2 10.4 copy-start
  294.1 0.7 copy-start.1
  325.9 10.4 copy-start
  338.8 0.7 copy-start.1
  370.6 10.4 copy-start
  383.5 0.7 copy-start.1
  415.4 10.4 copy-start
  428.2 0.7 copy-start.1
  460.1 10.4 copy-start
  473.0 0.7 copy-start.1
  504.8 10.4 copy-start
  517.7 0.7 copy-start.1
  549.5 10.4 copy-start
  562.4 0.7 copy-start.1
  594.3 10.4 copy-start
  607.1 0.7 copy-start.1
  639.0 10.4 copy-start
  651.9 0.7 copy-start.1
  683.7 10.4 copy-start
  696.6 0.7 copy-start.1
  728.4 10.4 copy-start
  741.3 0.7 copy-start.1
  773.2 10.4 copy-start
  786.0 0.7 copy-start.1
  787.2 332.4 %reduce-scatter.2.cloned.1.call-start = ((), (), s32[]{:S(2)}) async-start(), calls=%async_computation.1 | async-start | bytes 147456 | tf_op jit(solution)/shard_map/reduce_scatter | solution.py:104
  1059.9 4.6 copy-start.5
  1059.9 4.6 copy-start.6
  1065.5 4.8 copy-start.3
Sparse Core Ops, SparseCore 0:
  787.3 266.7 all-reduce.5
  1081.1 38.4 reduce-scatter.1
where the time goes:
time: 1140 us; the launch traced here: 1130 us
  local copies, waits for them, and re-layouts  673 us (59%)
  waiting for transfers between devices  306 us (27%)
  matrix products  91.7 us (8%)
  blocking collectives  28.5 us (2%)
  between operations  14.5 us (1%)
    psum x1, waiting for transfers between devices, body(): y_re, y_im = lax.psum((part_re, part_im), 'tile')  267 us
    while x96, local copies, waits for them, and re-layouts  244 us
    gather x384, local copies, waits for them, and re-layouts  163 us
    reshape x16, local copies, waits for them, and re-layouts, one_block(): toeplitz = repeated.reshape(row_block, out_rows, period - 1)[:, :, :width]  139 us
    another operation x32, local copies, waits for them, and re-layouts, one_block(): repeated = jnp.tile(padded, (1, out_rows))[:, :out_rows * (period - 1)]  87.2 us
    dot_general x16, matrix products, highest(): return jnp.dot(left, right, precision=lax.Precision.HIGHEST)  52.7 us
    dot_general x16, matrix products, one_block(): jnp.einsum('bic,bjc->ij', windows, toeplitz, preferred_element_type=jnp.f...  39 us
    reduce_scatter x1, waiting for transfers between devices, body(): lax.psum_scatter(phase_total, 'depth', scatter_dimension=1, tiled=True)  38.6 us
  transfers between devices with their start and end apart: 4, of which 2 were waited for; matrix products, arithmetic and copies ran while one was open for 2% of the time, Pallas kernels for 0%

commit v1 on v0

v1 whole, which is shorter than its diff:
```python
import numpy as np
import jax
import jax.numpy as jnp
import ml_dtypes
from jax import lax
from jax.experimental import pallas as pl
from jax.experimental.pallas import tpu as pltpu
from jax.sharding import PartitionSpec as P

PUPIL = 1024
HALF = 128
FREQ = 2 * HALF
GROUP = 16
GATHER_MASKS = (0, 2, 1, 3, 6, 4, 7, 5)
EVEN, ODD = (0, 2, 4, 6), (1, 3, 5, 7)
WINDOW = FREQ + GROUP
defocus_step = 0.5


def split_table(table):
    high = table.astype(ml_dtypes.bfloat16)
    return high, (table - high.astype(np.float64)).astype(ml_dtypes.bfloat16)


def freq_tables():
    waves = np.arange(FREQ, dtype=np.int64) - HALF
    angle = (waves[:, None] * np.arange(PUPIL)[None, :]) % PUPIL * (2 * np.pi / PUPIL)
    cos, sin = np.cos(angle) * PUPIL**-0.5, -np.sin(angle) * PUPIL**-0.5
    gather = split_table(np.concatenate([cos.T, sin.T], axis=1))
    spread = split_table(np.concatenate([cos, sin], axis=1))
    half, chip, core, row = np.indices((2, FREQ // GROUP, 2, 4)).reshape(4, -1)
    arrived = 128 * core + 8 * chip + 4 * half + row
    return gather, spread, [part[arrived] for part in spread]


def split(x):
    high = x.astype(jnp.bfloat16)
    return high, (x - high.astype(jnp.float32)).astype(jnp.bfloat16)


def dot(left, right):
    return jnp.dot(left, right, preferred_element_type=jnp.float32)


def dot3(left, high_ref, low_ref):
    rows = left.shape[0]
    high, low = split(left)
    both = dot(jnp.concatenate([high, low], axis=0), high_ref[...])
    return both[:rows] + both[rows:] + dot(high, low_ref[...])


def shift_kernel(grad, shifts):
    tile_rows = shifts.shape[0] * GROUP
    row = lax.broadcasted_iota(jnp.int32, (tile_rows, FREQ), 0)
    lane = lax.broadcasted_iota(jnp.int32, (tile_rows, FREQ), 1)
    lane_bits = lax.broadcasted_iota(jnp.int32, (WINDOW, FREQ), 1)
    below = jnp.zeros((WINDOW - FREQ, FREQ), jnp.float32)
    columns = grad[...].astype(jnp.float32).T.astype(jnp.bfloat16)
    for step in range(tile_rows // GROUP):
        pick = jnp.where(row == GROUP * step + lane // GROUP, 1.0, 0.0).astype(jnp.bfloat16)
        moved = jnp.concatenate([dot(columns, pick), below], axis=0)
        for shift in (8, 4, 2, 1):
            moved = jnp.where(lane_bits & shift != 0, pltpu.roll(moved, shift, 0), moved)
        shifts[step, :HALF] = jnp.zeros((HALF, FREQ), jnp.bfloat16)
        shifts[step, HALF : HALF + WINDOW] = moved.astype(jnp.bfloat16)
        shifts[step, HALF + WINDOW :] = jnp.zeros((HALF - GROUP, FREQ), jnp.bfloat16)


def windows(core, near, far, own, ext, win):
    tile_rows = near.shape[0]
    here = core == 0
    ext[:tile_rows] = jnp.where(here, far[...], near[...])
    ext[tile_rows : 2 * tile_rows] = own[...]
    ext[2 * tile_rows :] = jnp.where(here, near[...], far[...])
    for step in range(tile_rows // GROUP):
        win[:, FREQ * step : FREQ * (step + 1)] = ext[GROUP * step : GROUP * step + WINDOW]


def exchanged(x, lane, width):
    left, right = pltpu.roll(x, HALF - width, 1), pltpu.roll(x, width, 1)
    return jnp.where(lane & width == 0, left, right)


def lags(win, shifts, half, places):
    lane = lax.broadcasted_iota(jnp.int32, (WINDOW - 8, HALF), 1)

    def raw(place):
        first = pl.multiple_of(FREQ - GROUP * place - HALF * half, GROUP)
        taps = shifts[:, pl.ds(first, FREQ), :].reshape(-1, FREQ)
        return dot(win[...], taps)

    def aligned(terms):
        part = terms[: WINDOW - 8, :HALF] + terms[8:, HALF:]
        for shift in (4, 2, 1):
            up = pltpu.roll(part, WINDOW - 8 - shift, 0)
            part = jnp.where(lane & (GROUP * shift) != 0, up, part)
        return part[:FREQ]

    parts, ahead = [], raw(places[0])
    for place in places[1:]:
        terms, ahead = ahead, raw(place)
        parts.append(aligned(terms))
    parts.append(aligned(ahead))
    lane = lax.broadcasted_iota(jnp.int32, (FREQ, HALF), 1)

    def merged(first, second, width):
        low = lane & width == 0
        rest = jnp.where(low, second, first)
        rest = pltpu.roll(rest, width, 1) if width == HALF // 2 else exchanged(rest, lane, width)
        return jnp.where(low, first, second) + rest

    both = merged(merged(parts[0], parts[2], 64), merged(parts[1], parts[3], 64), 32)
    return both + exchanged(both, lane, 16)


def interleaved(even, odd):
    lane = lax.broadcasted_iota(jnp.int32, (FREQ, HALF), 1)
    return jnp.where(lane & GROUP == 0, even, odd)


def by_owner(total):
    flipped = total.T.reshape(HALF // 8, 8, FREQ)
    return jnp.concatenate([flipped[:, :, :HALF], flipped[:, :, HALF:]], axis=1)


def first_kernel(core, far, near, own, shifts, win, even, ext):
    windows(core[0], near, far, own, ext, win)
    even[...] = lags(win, shifts, 1 - core[0], EVEN)


def second_kernel(core, win, shifts, even, out, kept):
    out[...] = by_owner(interleaved(even[...], lags(win, shifts, 1 - core[0], ODD)))
    kept[...] = lags(win, shifts, core[0], EVEN)


def third_kernel(core, win, shifts, kept, keep_z, out):
    out[:, :16] = by_owner(interleaved(kept[...], lags(win, shifts, core[0], ODD)))
    out[:, 16:] = keep_z[...]


def cos_sin(theta):
    turns = jnp.round(theta * (2 / np.pi))
    rest = theta - turns * 1.5703125
    rest = rest - turns * 4.837512969970703e-4
    rest = rest - turns * 7.549789948768648e-8
    square = rest * rest
    sin = rest + rest * square * (
        -1.6666654611e-1 + square * (8.3321608736e-3 + square * -1.9515295891e-4)
    )
    cos = (1.0 - 0.5 * square) + square * square * (
        4.166664568298827e-2 + square * (-1.388731625493765e-3 + square * 2.443315711809948e-5)
    )
    quarter = turns.astype(jnp.int32)
    odd = quarter & 1 != 0
    real, imag = jnp.where(odd, sin, cos), jnp.where(odd, cos, sin)
    real = jnp.where((quarter + 1) & 2 != 0, -real, real)
    imag = jnp.where(quarter & 2 != 0, -imag, imag)
    return real, imag


def field_kernel(
    first, depth, core, defocus, phase, send_k, high, low, keep, send, field_re, field_im, ordered
):
    blocks, rows, width = phase.shape
    for block in range(blocks):
        ordered[depth[0] ^ GATHER_MASKS[block]] = phase[block]
    full = jnp.concatenate([ordered[block] for block in range(blocks)], axis=1)
    centre = (PUPIL - 1) / 2.0
    shape = (rows, PUPIL)
    u = (lax.broadcasted_iota(jnp.int32, shape, 0) + first[0]).astype(jnp.float32)
    v = lax.broadcasted_iota(jnp.int32, shape, 1).astype(jnp.float32)
    radius = (u - centre) ** 2 + (v - centre) ** 2
    limit = (PUPIL / 2.0) ** 2
    inside = radius <= limit
    real, imag = cos_sin(full + defocus[0].astype(jnp.float32) * defocus_step * (radius / limit))
    real, imag = jnp.where(inside, real, 0.0), jnp.where(inside, imag, 0.0)
    field_re[...] = real
    field_im[...] = imag
    terms = dot3(jnp.concatenate([real, imag], axis=0), high, low)
    z_re = terms[:rows, :FREQ] - terms[rows:, FREQ:]
    z_im = terms[:rows, FREQ:] + terms[rows:, :FREQ]
    here = core[0] == 0
    blank = jnp.zeros((rows, FREQ), jnp.float32)
    first_re, second_re = jnp.where(here, z_re, blank), jnp.where(here, blank, z_re)
    first_im, second_im = jnp.where(here, z_im, blank), jnp.where(here, blank, z_im)
    z = jnp.concatenate([first_re, second_re, first_im, second_im], axis=0).T
    z_low, z_high = z[:HALF], z[HALF:]
    keep[...] = jnp.where(here, z_low, z_high).reshape(keep.shape)
    send[:, :16] = send_k[...]
    send[:, 16:] = jnp.where(here, z_high, z_low).reshape(keep.shape)


def middle_kernel(payload, g_high, g_low, s_high, s_low, out):
    chips = payload.shape[0]
    rows = PUPIL // chips
    kernel_grad = payload[0, :16]
    for chip in range(1, chips):
        kernel_grad = kernel_grad + payload[chip, :16]
    kernel_grad = jnp.concatenate([kernel_grad[:8], kernel_grad[8:]], axis=1)
    z_re = jnp.concatenate([payload[chip, 16:, :rows] for chip in range(chips)], axis=1)
    z_im = jnp.concatenate([payload[chip, 16:, rows:] for chip in range(chips)], axis=1)
    terms = dot3(jnp.concatenate([z_re, z_im], axis=0), g_high, g_low)
    y_re = terms[:8, :FREQ] - terms[8:, FREQ:]
    y_im = terms[:8, FREQ:] + terms[8:, :FREQ]
    gy = 2.0 * jnp.concatenate([kernel_grad * y_re, kernel_grad * y_im], axis=0)
    terms = dot3(gy, s_high, s_low)
    gz_re = terms[:8, :PUPIL] + terms[8:, PUPIL:]
    gz_im = terms[8:, :PUPIL] - terms[:8, PUPIL:]
    rows = rows // 2
    for tile in range(2 * chips):
        here = slice(rows * tile, rows * (tile + 1))
        parts = [part[:, here] for part in (gz_re, gz_im)]
        out[tile] = jnp.concatenate([part[half : half + 4] for half in (0, 4) for part in parts], axis=1)


def phase_kernel(payload, field_re, field_im, high, low, out):
    rows = field_re.shape[0]
    gz = payload[...].T
    gz_re = jnp.concatenate([gz[:rows], gz[2 * rows : 3 * rows]], axis=1)
    gz_im = jnp.concatenate([gz[rows : 2 * rows], gz[3 * rows :]], axis=1)
    terms = dot3(jnp.concatenate([gz_re, gz_im], axis=0), high, low)
    ge_re = terms[:rows, :PUPIL] + terms[rows:, PUPIL:]
    ge_im = terms[rows:, :PUPIL] - terms[:rows, PUPIL:]
    phase = field_re[...] * ge_im - field_im[...] * ge_re
    width = out.shape[2]
    for block in range(out.shape[0]):
        out[block] = phase[:, width * block : width * (block + 1)]


def call(kernel, outs, scratch, flops, moved, smem=0):
    def run(*args):
        spaces = [pltpu.SMEM if place < smem else pltpu.VMEM for place in range(len(args))]
        return pl.pallas_call(
            kernel,
            out_shape=outs,
            in_specs=[pl.BlockSpec(memory_space=space) for space in spaces],
            out_specs=jax.tree.map(lambda _: pl.BlockSpec(memory_space=pltpu.VMEM), outs),
            scratch_shapes=scratch,
            compiler_params=pltpu.CompilerParams(vmem_limit_bytes=40 * 2**20),
            cost_estimate=pl.CostEstimate(flops=flops, bytes_accessed=moved, transcendentals=0),
        )(*args)

    return run


def over_depth(x, mask):
    count = lax.axis_size("depth")
    return lax.ppermute(x, "depth", [(i, i ^ mask) for i in range(count)])


def beside(x, tiles):
    pairs = [(i, i + 1) for i in range(1, tiles - 1, 2)]
    return lax.ppermute(x, ("chip", "core"), pairs + [(j, i) for i, j in pairs])


def swap(x):
    return lax.ppermute(x, "core", [(0, 1), (1, 0)])


def body(scene_layers, sensor_grad, pupil_phase, defocus_index):
    chips, depths = lax.axis_size("chip"), lax.axis_size("depth")
    rows, width = pupil_phase.shape
    f32 = jnp.float32
    (g_high, g_low), (s_high, s_low), (r_high, r_low) = freq_tables()
    core, depth, first_row = (
        lax.axis_index(axis).astype(jnp.int32)[None] for axis in ("core", "depth", ("chip", "core"))
    )
    first_row = first_row * rows
    scene = scene_layers[0]
    steps = scene.shape[0] // GROUP
    work = 2 * steps * FREQ * WINDOW * FREQ
    far = beside(scene, 2 * chips)
    other = over_depth(pupil_phase, GATHER_MASKS[1])
    shape, bf16 = jax.ShapeDtypeStruct, jnp.bfloat16
    shifts = call(
        shift_kernel,
        shape((steps, 2 * FREQ, FREQ), bf16),
        [],
        2 * scene.shape[0] * FREQ * FREQ * GROUP,
        2**22,
    )(sensor_grad)
    other, shifts, edge = lax.optimization_barrier((other, shifts, scene))
    near = swap(edge)
    gathered = jnp.stack([pupil_phase, other])
    beyond = over_depth(gathered, GATHER_MASKS[2])
    far, near, shifts = lax.optimization_barrier((far, near, shifts))
    lanes = shape((FREQ, HALF), f32)
    win, even = call(
        first_kernel,
        (shape((WINDOW, steps * FREQ), bf16), lanes),
        [pltpu.VMEM((3 * scene.shape[0], FREQ), bf16)],
        4 * work,
        2**19,
        smem=1,
    )(core, far, near, scene, shifts)
    beyond, win, even = lax.optimization_barrier((beyond, win, even))
    gathered = jnp.concatenate([gathered, beyond], axis=0)
    beyond = over_depth(gathered, GATHER_MASKS[4])
    send_k, even = call(
        second_kernel, (shape((chips, 16, HALF), f32), lanes), [], 8 * work, 2**19, smem=1
    )(core, win, shifts, even)
    beyond, send_k, even = lax.optimization_barrier((beyond, send_k, even))
    gathered = jnp.concatenate([gathered, beyond], axis=0)
    piece, both = shape((chips, 8, HALF), f32), shape((chips, 24, HALF), f32)
    field = shape((rows, PUPIL), f32)
    keep_z, send, field_re, field_im = call(
        field_kernel,
        (piece, both, field, field),
        [pltpu.VMEM((depths, rows, width), f32)],
        2 * 192 * PUPIL * 2 * FREQ,
        3 * 2**20,
        smem=4,
    )(first_row, depth, core, defocus_index, gathered, send_k, g_high, g_low)
    send, win = lax.optimization_barrier((send, win))
    other = swap(send)
    keep = call(third_kernel, both, [], 4 * work, 2**19, smem=1)(core, win, shifts, even, keep_z)
    other, keep = lax.optimization_barrier((other, keep))
    payload = lax.all_to_all(keep + other, "chip", 0, 0, tiled=True)
    payload = call(
        middle_kernel,
        jax.ShapeDtypeStruct((2 * chips, 4, HALF), f32),
        [],
        2 * 96 * PUPIL * 2 * FREQ,
        5 * 2**20,
    )(payload, g_high, g_low, s_high, s_low)
    payload = lax.all_to_all(payload, ("chip", "core"), 0, 0, tiled=True)
    parts = call(
        phase_kernel,
        jax.ShapeDtypeStruct((depths, rows, width), f32),
        [],
        2 * 192 * PUPIL * 2 * FREQ,
        3 * 2**20,
    )(payload.reshape(HALF, HALF), field_re, field_im, r_high, r_low)
    parts = lax.all_to_all(parts, "depth", 0, 0, tiled=True)
    return jnp.sum(parts, axis=0)


def solution(mesh):
    depths, tiles = mesh.devices.shape
    split_mesh = jax.sharding.Mesh(
        mesh.devices.reshape(depths, tiles // 2, 2), ("depth", "chip", "core")
    )
    rows = ("chip", "core")
    placed = (P("depth", rows, None), P(rows, None), P(rows, "depth"), P("depth"))
    return jax.shard_map(
        body, mesh=split_mesh, in_specs=placed, out_specs=P(rows, "depth"), check_vma=False
    )
```

time: 1140 us -> 68 us (0.06)
  the two profiles are of different devices: /device:TPU:16 before, /device:TPU:8 now
where the time goes in v1:
time: 68 us; the launch traced here: 67.7 us
  blocking collectives  45.3 us (67%)
  Pallas kernels  9.47 us (14%)
  starting transfers between devices  8.24 us (12%)
  waiting for transfers between devices  2.36 us (3%)
  local copies, waits for them, and re-layouts  0.87 us (1%)
  between operations  0.81 us (1%)
    all_to_all x1, blocking collectives, body(): payload = lax.all_to_all(keep + other, 'chip', 0, 0, tiled=True)  20 us
    all_to_all x1, blocking collectives, body(): payload = lax.all_to_all(payload, ('chip', 'core'), 0, 0, tiled=True)  15.2 us
    all_to_all x1, blocking collectives, body(): parts = lax.all_to_all(parts, 'depth', 0, 0, tiled=True)  10 us
    pallas_call x7, Pallas kernels, run(): pl.pallas_call(kernel, out_shape=outs, in_specs=[pl.BlockSpec(memory_spac...  9.47 us
    ppermute x3, starting transfers between devices, over_depth(): return lax.ppermute(x, 'depth', [(i, i ^ mask) for i in range(count)])  4.14 us
    ppermute x2, starting transfers between devices, swap(): return lax.ppermute(x, 'core', [(0, 1), (1, 0)])  3.45 us
    ppermute x3, waiting for transfers between devices, over_depth(): return lax.ppermute(x, 'depth', [(i, i ^ mask) for i in range(count)])  1.92 us
  transfers between devices with their start and end apart: 6, of which 3 were waited for; matrix products, arithmetic and copies ran while one was open for 0% of the time, Pallas kernels for 11%

profile of v1, /device:TPU:8, one launch (start us, length us, event | category | flops | bytes accessed | tf_op | source)
XLA Modules:
  0.0 67.7 jit_solution(490675195141167372)
XLA Ops:
  0.0 0.0 copy-start.8
  0.0 1.5 %collective-permute-start = (f32[32,128]{1,0:T(8,128)}, f32[32,128]{1,0:T(8,128)S(1)}, u32[]{:S(2)}, u32[]{:S(2)}) collective-permute-start(f32[32,128]{1,0:T(8,128)} %param.12), channel_id=1, source_target_pairs={{0,64},{32,96},{64,0},{96,32},{128,192},{160,224},{192,128},{224,1... | collective-permute-start | bytes 49160 | tf_op jit(solution)/shard_map/ppermute | solution.py:248
  1.5 0.7 collective-permute-start.2
  2.8 0.0 copy-start.6
  2.8 0.8 %copy-done.6 = bf16[128,256]{1,0:T(8,128)(2,1)S(1)} copy-done((bf16[128,256]{1,0:T(8,128)(2,1)S(1)}, bf16[128,256]{1,0:T(8,128)(2,1)}, u32[]{:S(2)}) %copy-start.6) | copy-done | bytes 65560
  3.6 0.0 copy-start.7
  3.7 1.1 %shard_map.100.shifts = bf16[8,512,256]{2,1,0:T(8,128)(2,1)S(1)} custom-call(bf16[128,256]{1,0:T(8,128)(2,1)S(1)} %copy-done.6), custom_call_target="tpu_custom_call" | custom-call | flops 268435456 | bytes 4194304 | tf_op jit(solution)/shard_map/pallas_call | solution.py:233
  4.8 0.0 collective-permute-done
  4.8 0.0 copy-done.7
  4.8 3.4 %collective-permute-start.3 = (bf16[128,256]{1,0:T(8,128)(2,1)S(1)}, bf16[128,256]{1,0:T(8,128)(2,1)S(1)}, u32[]{:S(2)}, u32[]{:S(2)}) collective-permute-start(bf16[128,256]{1,0:T(8,128)(2,1)S(1)} %bitcast.9), channel_id=1, source_target_pairs={{0,1},{1,0},{2,3},{3,2},{4,5},{5,4},{6,7},{7,6},{8,9},{9,8},{10,11... | collective-permute-start | bytes 196616 | tf_op jit(solution)/shard_map/ppermute | solution.py:257
  8.2 0.0 copy-done.8
  8.2 0.5 collective-permute-start.1
  8.6 0.0 collective-permute-done.2.far
  8.6 0.4 collective-permute-done.3.near
  9.1 1.6 %shard_map.101 = (bf16[272,2048]{1,0:T(8,128)(2,1)S(1)}, f32[256,128]{1,0:T(8,128)S(1)}) custom-call(s32[1]{0:T(128)} %bitcast.2.core, bf16[128,256]{1,0:T(8,128)(2,1)S(1)} %collective-permute-done.2.far, bf16[128,256]{1,0:T(8,128)(2,1)S(1)} %collective-permute-done.3.near, bf16[128,256]{1,0:T(8,128)(2,1)S(1)} %bitcast.10, ...), custom_call_target="tpu_custom_call" | custom-call | flops 1140850688 | bytes 524288 | tf_op jit(solution)/shard_map/pallas_call | solution.py:233
  10.7 1.4 %collective-permute-done.1 = f32[2,32,128]{2,1,0:T(8,128)S(1)} collective-permute-done((f32[2,32,128]{2,1,0:T(8,128)S(1)}, f32[2,32,128]{2,1,0:T(8,128)S(1)}, u32[]{:S(2)}, u32[]{:S(2)}) %collective-permute-start.1) | collective-permute-done | bytes 32800 | tf_op jit(solution)/shard_map/ppermute | solution.py:248
  12.1 0.0 copy-start
  12.1 0.0 copy-start.1
  12.1 2.2 %collective-permute-start.4 = (f32[4,32,128]{2,1,0:T(8,128)S(1)}, f32[4,32,128]{2,1,0:T(8,128)S(1)}, u32[]{:S(2)}, u32[]{:S(2)}) collective-permute-start(f32[4,32,128]{2,1,0:T(8,128)S(1)} %pad_maximum_fusion.1), channel_id=1, source_target_pairs={{0,192},{32,224},{64,128},{96,160},{128,64},{160,96},{192,0},{224,... | collective-permute-start | bytes 196616 | tf_op jit(solution)/shard_map/ppermute | solution.py:248
  14.3 2.9 %shard_map.102 = (f32[16,16,128]{2,1,0:T(8,128)S(1)}, f32[256,128]{1,0:T(8,128)S(1)}) custom-call(s32[1]{0:T(128)} %bitcast.2.core, bf16[272,2048]{1,0:T(8,128)(2,1)S(1)} %get-tuple-element.46.win, bf16[8,512,256]{2,1,0:T(8,128)(2,1)S(1)} %shard_map.100.shifts, f32[256,128]{1,0:T(8,128)S(1)} %get-tuple-element.39.even), custom_call_target="tpu_custom_call" | custom-call | flops 2281701376 | bytes 524288 | tf_op jit(solution)/shard_map/pallas_call | solution.py:233
  17.2 0.5 collective-permute-done.4
  17.7 0.0 copy-done
  17.7 0.0 copy-done.1
  17.7 0.7 %shard_map.103 = (f32[16,8,128]{2,1,0:T(8,128)S(1)}, f32[16,24,128]{2,1,0:T(8,128)S(1)}, f32[32,1024]{1,0:T(8,128)S(1)}, f32[32,1024]{1,0:T(8,128)S(1)}) custom-call(s32[1]{0:T(128)} %bitcast.first, s32[1]{0:T(128)} %bitcast.1.depth, s32[1]{0:T(128)} %bitcast.2.core, s32[1]{0:T(128)S(6)} %copy.11.defocus, f32[8,32,128]{2,1,0:T(8,128)S(1)} %pad_maximum_fusion.phase, ...), custom_call_target="tpu_custom_call" | custom-call | flops 201326592 | bytes 3145728 | tf_op jit(solution)/shard_map/pallas_call | solution.py:233
  18.4 0.1 collective-permute-start.5
  18.5 0.0 copy-start.2
  18.5 0.0 copy-start.3
  18.5 1.7 %shard_map.104 = f32[16,24,128]{2,1,0:T(8,128)S(1)} custom-call(s32[1]{0:T(128)} %bitcast.2.core, bf16[272,2048]{1,0:T(8,128)(2,1)S(1)} %get-tuple-element.46.win, bf16[8,512,256]{2,1,0:T(8,128)(2,1)S(1)} %shard_map.100.shifts, f32[256,128]{1,0:T(8,128)S(1)} %get-tuple-element.47.kept, f32[16,8,128]{2,1,0:T(8,128)S(1)} %get-tuple-element.48.keep_z), custom_call_target="tpu_custom_call" | custom-call | flops 1140850688 | bytes 524288 | tf_op jit(solution)/shard_map/pallas_call | solution.py:233
  20.2 0.0 collective-permute-done.5
  20.3 20.0 %all_to_all.15.payload = f32[16,24,128]{2,1,0:T(8,128)S(1)} all-to-all(f32[16,24,128]{2,1,0:T(8,128)S(1)} %add.7), channel_id=1, replica_groups=mesh['depth'=8,'chip'=16,'core'=2] {'chip'}, dimensions={0} | all-to-all | bytes 393216 | tf_op jit(solution)/shard_map/all_to_all | solution.py:318
  40.3 0.0 copy-done.2
  40.3 0.0 copy-done.3
  40.3 0.0 copy-start.4
  40.3 0.0 copy-start.5
  40.3 1.0 %shard_map.105 = f32[32,4,128]{2,1,0:T(4,128)S(1)} custom-call(f32[16,24,128]{2,1,0:T(8,128)S(1)} %all_to_all.15.payload, bf16[1024,512]{1,0:T(8,128)(2,1)S(1)} %copy-done.1, bf16[1024,512]{1,0:T(8,128)(2,1)S(1)} %copy-done, bf16[256,2048]{1,0:T(8,128)(2,1)S(1)} %copy-done.3, bf16[256,2048]{1,0:T(8,128)(2,1)S(1)} %copy-done.2), custom_call_target="tpu_custom_call" | custom-call | flops 100663296 | bytes 5242880 | tf_op jit(solution)/shard_map/pallas_call | solution.py:233
  41.3 15.2 %all_to_all.16 = f32[32,4,128]{2,1,0:T(4,128)S(1)} all-to-all(f32[32,4,128]{2,1,0:T(4,128)S(1)} %shard_map.105), channel_id=1, replica_groups=mesh['depth'=8,'chip'=16,'core'=2] {'chip','core'}, dimensions={0} | all-to-all | bytes 131072 | tf_op jit(solution)/shard_map/all_to_all | solution.py:326
  56.5 0.0 copy-done.4
  56.5 0.0 copy-done.5
  56.5 0.5 shard_map.106
  57.0 10.0 %all_to_all.17 = f32[8,32,128]{2,1,0:T(8,128)S(1)} all-to-all(f32[8,32,128]{2,1,0:T(8,128)S(1)} %shard_map.106), channel_id=1, replica_groups=mesh['depth'=8,'chip'=16,'core'=2] {'depth'}, dimensions={0} | all-to-all | bytes 262144 | tf_op jit(solution)/shard_map/all_to_all | solution.py:334
  67.1 0.6 reduce_sum.9
  (4 shorter events, 0.0 us)
Async XLA Ops:
  0.0 8.2 %copy-start.8 = (f32[32,128]{1,0:T(8,128)S(1)}, f32[32,128]{1,0:T(8,128)}, u32[]{:S(2)}) copy-start(f32[32,128]{1,0:T(8,128)} %param.12) | copy-start | bytes 49156
  0.0 4.8 %collective-permute-start = (f32[32,128]{1,0:T(8,128)}, f32[32,128]{1,0:T(8,128)S(1)}, u32[]{:S(2)}, u32[]{:S(2)}) collective-permute-start(f32[32,128]{1,0:T(8,128)} %param.12), channel_id=1, source_target_pairs={{0,64},{32,96},{64,0},{96,32},{128,192},{160,224},{192,128},{224,1... | collective-permute-start | bytes 49160 | tf_op jit(solution)/shard_map/ppermute | solution.py:248
  1.5 7.1 %collective-permute-start.2 = (bf16[128,256]{1,0:T(8,128)(2,1)}, bf16[128,256]{1,0:T(8,128)(2,1)S(1)}, u32[]{:S(2)}, u32[]{:S(2)}) collective-permute-start(bf16[128,256]{1,0:T(8,128)(2,1)} %bitcast.8), channel_id=1, source_target_pairs={{1,2},{3,4},{5,6},{7,8},{9,10},{11,12},{13,14},{15,16},{17,18},{19... | collective-permute-start | bytes 196616 | tf_op jit(solution)/shard_map/ppermute | solution.py:253
  2.8 0.8 %copy-start.6 = (bf16[128,256]{1,0:T(8,128)(2,1)S(1)}, bf16[128,256]{1,0:T(8,128)(2,1)}, u32[]{:S(2)}) copy-start(bf16[128,256]{1,0:T(8,128)(2,1)} %grad.1) | copy-start | bytes 196612
  3.6 1.1 %copy-start.7 = (bf16[1,128,256]{2,1,0:T(8,128)(2,1)S(1)}, bf16[1,128,256]{2,1,0:T(8,128)(2,1)}, u32[]{:S(2)}) copy-start(bf16[1,128,256]{2,1,0:T(8,128)(2,1)} %param.10) | copy-start | bytes 196612
  4.8 4.3 %collective-permute-start.3 = (bf16[128,256]{1,0:T(8,128)(2,1)S(1)}, bf16[128,256]{1,0:T(8,128)(2,1)S(1)}, u32[]{:S(2)}, u32[]{:S(2)}) collective-permute-start(bf16[128,256]{1,0:T(8,128)(2,1)S(1)} %bitcast.9), channel_id=1, source_target_pairs={{0,1},{1,0},{2,3},{3,2},{4,5},{5,4},{6,7},{7,6},{8,9},{9,8},{10,11... | collective-permute-start | bytes 196616 | tf_op jit(solution)/shard_map/ppermute | solution.py:257
  8.2 3.9 %collective-permute-start.1 = (f32[2,32,128]{2,1,0:T(8,128)S(1)}, f32[2,32,128]{2,1,0:T(8,128)S(1)}, u32[]{:S(2)}, u32[]{:S(2)}) collective-permute-start(f32[2,32,128]{2,1,0:T(8,128)S(1)} %pad_maximum_fusion.2), channel_id=1, source_target_pairs={{0,32},{32,0},{64,96},{96,64},{128,160},{160,128},{192,224},{224,1... | collective-permute-start | bytes 98312 | tf_op jit(solution)/shard_map/ppermute | solution.py:248
  12.1 5.6 %copy-start = (bf16[1024,512]{1,0:T(8,128)(2,1)S(1)}, bf16[1024,512]{1,0:T(8,128)(2,1)}, u32[]{:S(2)}) copy-start(bf16[1024,512]{1,0:T(8,128)(2,1)} %constant.34.clone.low.g_low) | copy-start | bytes 3145732
  12.1 5.6 %copy-start.1 = (bf16[1024,512]{1,0:T(8,128)(2,1)S(1)}, bf16[1024,512]{1,0:T(8,128)(2,1)}, u32[]{:S(2)}) copy-start(bf16[1024,512]{1,0:T(8,128)(2,1)} %constant.33.clone.high.g_high) | copy-start | bytes 3145732
  12.1 5.6 %collective-permute-start.4 = (f32[4,32,128]{2,1,0:T(8,128)S(1)}, f32[4,32,128]{2,1,0:T(8,128)S(1)}, u32[]{:S(2)}, u32[]{:S(2)}) collective-permute-start(f32[4,32,128]{2,1,0:T(8,128)S(1)} %pad_maximum_fusion.1), channel_id=1, source_target_pairs={{0,192},{32,224},{64,128},{96,160},{128,64},{160,96},{192,0},{224,... | collective-permute-start | bytes 196616 | tf_op jit(solution)/shard_map/ppermute | solution.py:248
  18.4 1.8 %collective-permute-start.5 = (f32[16,24,128]{2,1,0:T(8,128)S(1)}, f32[16,24,128]{2,1,0:T(8,128)S(1)}, u32[]{:S(2)}, u32[]{:S(2)}) collective-permute-start(f32[16,24,128]{2,1,0:T(8,128)S(1)} %get-tuple-element.45), channel_id=1, source_target_pairs={{0,1},{1,0},{2,3},{3,2},{4,5},{5,4},{6,7},{7,6},{8,9},{9,8},{10,11... | collective-permute-start | bytes 589832 | tf_op jit(solution)/shard_map/ppermute | solution.py:257
  18.5 21.8 %copy-start.2 = (bf16[256,2048]{1,0:T(8,128)(2,1)S(1)}, bf16[256,2048]{1,0:T(8,128)(2,1)}, u32[]{:S(2)}) copy-start(bf16[256,2048]{1,0:T(8,128)(2,1)} %constant.36.clone.s_low) | copy-start | bytes 3145732
  18.5 21.8 %copy-start.3 = (bf16[256,2048]{1,0:T(8,128)(2,1)S(1)}, bf16[256,2048]{1,0:T(8,128)(2,1)}, u32[]{:S(2)}) copy-start(bf16[256,2048]{1,0:T(8,128)(2,1)} %constant.35.clone.s_high) | copy-start | bytes 3145732
  40.3 16.2 %copy-start.4 = (bf16[256,2048]{1,0:T(8,128)(2,1)S(1)}, bf16[256,2048]{1,0:T(8,128)(2,1)}, u32[]{:S(2)}) copy-start(bf16[256,2048]{1,0:T(8,128)(2,1)} %constant.38.clone.low) | copy-start | bytes 3145732
  40.3 16.2 %copy-start.5 = (bf16[256,2048]{1,0:T(8,128)(2,1)S(1)}, bf16[256,2048]{1,0:T(8,128)(2,1)}, u32[]{:S(2)}) copy-start(bf16[256,2048]{1,0:T(8,128)(2,1)} %constant.37.clone.high) | copy-start | bytes 3145732

commit v2 on v1

--- a/solution.py
+++ b/solution.py
@@ -29,7 +29,7 @@
     gather = split_table(np.concatenate([cos.T, sin.T], axis=1))
     spread = split_table(np.concatenate([cos, sin], axis=1))
     half, chip, core, row = np.indices((2, FREQ // GROUP, 2, 4)).reshape(4, -1)
-    arrived = 128 * core + 8 * chip + 4 * half + row
+    arrived = 128 * (1 - core) + 8 * chip + 4 * half + row
     return gather, spread, [part[arrived] for part in spread]
 
 
@@ -197,8 +197,9 @@
     for chip in range(1, chips):
         kernel_grad = kernel_grad + payload[chip, :16]
     kernel_grad = jnp.concatenate([kernel_grad[:8], kernel_grad[8:]], axis=1)
-    z_re = jnp.concatenate([payload[chip, 16:, :rows] for chip in range(chips)], axis=1)
-    z_im = jnp.concatenate([payload[chip, 16:, rows:] for chip in range(chips)], axis=1)
+    order = list(reversed(range(chips)))
+    z_re = jnp.concatenate([payload[place, 16:, :rows] for place in order], axis=1)
+    z_im = jnp.concatenate([payload[place, 16:, rows:] for place in order], axis=1)
     terms = dot3(jnp.concatenate([z_re, z_im], axis=0), g_high, g_low)
     y_re = terms[:8, :FREQ] - terms[8:, FREQ:]
     y_im = terms[:8, FREQ:] + terms[8:, :FREQ]
@@ -210,7 +211,8 @@
     for tile in range(2 * chips):
         here = slice(rows * tile, rows * (tile + 1))
         parts = [part[:, here] for part in (gz_re, gz_im)]
-        out[tile] = jnp.concatenate([part[half : half + 4] for half in (0, 4) for part in parts], axis=1)
+        rows_of = [part[half : half + 4] for half in (0, 4) for part in parts]
+        out[2 * chips - 1 - tile] = jnp.concatenate(rows_of, axis=1)
 
 
 def phase_kernel(payload, field_re, field_im, high, low, out):
@@ -224,7 +226,7 @@
     phase = field_re[...] * ge_im - field_im[...] * ge_re
     width = out.shape[2]
     for block in range(out.shape[0]):
-        out[block] = phase[:, width * block : width * (block + 1)]
+        out[out.shape[0] - 1 - block] = phase[:, width * block : width * (block + 1)]
 
 
 def call(kernel, outs, scratch, flops, moved, smem=0):
@@ -251,6 +253,11 @@
 def beside(x, tiles):
     pairs = [(i, i + 1) for i in range(1, tiles - 1, 2)]
     return lax.ppermute(x, ("chip", "core"), pairs + [(j, i) for i, j in pairs])
+
+
+def redistribute(x, axis):
+    order = list(reversed(range(x.shape[0])))
+    return lax.all_to_all(x, axis, 0, 0, tiled=True, axis_index_groups=[order])
 
 
 def swap(x):
@@ -315,7 +322,7 @@
     other = swap(send)
     keep = call(third_kernel, both, [], 4 * work, 2**19, smem=1)(core, win, shifts, even, keep_z)
     other, keep = lax.optimization_barrier((other, keep))
-    payload = lax.all_to_all(keep + other, "chip", 0, 0, tiled=True)
+    payload = redistribute(keep + other, "chip")
     payload = call(
         middle_kernel,
         jax.ShapeDtypeStruct((2 * chips, 4, HALF), f32),
@@ -323,7 +330,7 @@
         2 * 96 * PUPIL * 2 * FREQ,
         5 * 2**20,
     )(payload, g_high, g_low, s_high, s_low)
-    payload = lax.all_to_all(payload, ("chip", "core"), 0, 0, tiled=True)
+    payload = redistribute(payload, ("chip", "core"))
     parts = call(
         phase_kernel,
         jax.ShapeDtypeStruct((depths, rows, width), f32),
@@ -331,7 +338,7 @@
         2 * 192 * PUPIL * 2 * FREQ,
         3 * 2**20,
     )(payload.reshape(HALF, HALF), field_re, field_im, r_high, r_low)
-    parts = lax.all_to_all(parts, "depth", 0, 0, tiled=True)
+    parts = redistribute(parts, "depth")
     return jnp.sum(parts, axis=0)
 
 

time: 68 us -> 64.8 us (0.953)
  the two profiles are of different devices: /device:TPU:8 before, /device:TPU:16 now
where the time goes in v2:
time: 64.8 us; the launch traced here: 64.5 us
  blocking collectives  39 us (60%)
  starting transfers between devices  12.8 us (20%)
  Pallas kernels  9.46 us (15%)
  local copies, waits for them, and re-layouts  0.87 us (1%)
  between operations  0.84 us (1%)
  waiting for transfers between devices  0.83 us (1%)
  other arithmetic  0.66 us (1%)
    all_to_all x3, blocking collectives, redistribute(): return lax.all_to_all(x, axis, 0, 0, tiled=True, axis_index_groups=[order])  39 us
    pallas_call x7, Pallas kernels, run(): pl.pallas_call(kernel, out_shape=outs, in_specs=[pl.BlockSpec(memory_spac...  9.46 us
    ppermute x1, starting transfers between devices, beside(): return lax.ppermute(x, ('chip', 'core'), pairs + [(j, i) for i, j in pairs])  6.68 us
    ppermute x3, starting transfers between devices, over_depth(): return lax.ppermute(x, 'depth', [(i, i ^ mask) for i in range(count)])  5.97 us
  transfers between devices with their start and end apart: 6, of which 2 were waited for; matrix products, arithmetic and copies ran while one was open for 0% of the time, Pallas kernels for 11%

profile of v2, /device:TPU:16, one launch (start us, length us, event | category | flops | bytes accessed | tf_op | source)
XLA Modules:
  0.0 64.5 jit_solution(10044678159409723993)
XLA Ops:
  0.0 0.0 copy-start.8
  0.0 1.5 %collective-permute-start = (f32[32,128]{1,0:T(8,128)}, f32[32,128]{1,0:T(8,128)S(1)}, u32[]{:S(2)}, u32[]{:S(2)}) collective-permute-start(f32[32,128]{1,0:T(8,128)} %param.12), channel_id=1, source_target_pairs={{0,64},{32,96},{64,0},{96,32},{128,192},{160,224},{192,128},{224,1... | collective-permute-start | bytes 49160 | tf_op jit(solution)/shard_map/ppermute | solution.py:250
  1.5 6.7 %collective-permute-start.2 = (bf16[128,256]{1,0:T(8,128)(2,1)}, bf16[128,256]{1,0:T(8,128)(2,1)S(1)}, u32[]{:S(2)}, u32[]{:S(2)}) collective-permute-start(bf16[128,256]{1,0:T(8,128)(2,1)} %bitcast.8), channel_id=1, source_target_pairs={{1,2},{3,4},{5,6},{7,8},{9,10},{11,12},{13,14},{15,16},{17,18},{19... | collective-permute-start | bytes 196616 | tf_op jit(solution)/shard_map/ppermute | solution.py:255
  8.8 0.0 copy-start.6
  8.9 0.8 %copy-done.6 = bf16[128,256]{1,0:T(8,128)(2,1)S(1)} copy-done((bf16[128,256]{1,0:T(8,128)(2,1)S(1)}, bf16[128,256]{1,0:T(8,128)(2,1)}, u32[]{:S(2)}) %copy-start.6) | copy-done | bytes 65560
  9.7 0.0 copy-start.7
  9.7 1.1 %shard_map.100.shifts = bf16[8,512,256]{2,1,0:T(8,128)(2,1)S(1)} custom-call(bf16[128,256]{1,0:T(8,128)(2,1)S(1)} %copy-done.6), custom_call_target="tpu_custom_call" | custom-call | flops 268435456 | bytes 4194304 | tf_op jit(solution)/shard_map/pallas_call | solution.py:235
  10.8 0.0 collective-permute-done
  10.8 0.0 copy-done.7
  10.8 0.1 collective-permute-start.3
  10.9 0.0 copy-done.8
  10.9 2.3 %collective-permute-start.1 = (f32[2,32,128]{2,1,0:T(8,128)S(1)}, f32[2,32,128]{2,1,0:T(8,128)S(1)}, u32[]{:S(2)}, u32[]{:S(2)}) collective-permute-start(f32[2,32,128]{2,1,0:T(8,128)S(1)} %pad_maximum_fusion.2), channel_id=1, source_target_pairs={{0,32},{32,0},{64,96},{96,64},{128,160},{160,128},{192,224},{224,1... | collective-permute-start | bytes 98312 | tf_op jit(solution)/shard_map/ppermute | solution.py:250
  13.2 0.0 collective-permute-done.2.far
  13.2 0.0 collective-permute-done.3.near
  13.3 1.6 %shard_map.101 = (bf16[272,2048]{1,0:T(8,128)(2,1)S(1)}, f32[256,128]{1,0:T(8,128)S(1)}) custom-call(s32[1]{0:T(128)} %bitcast.2.core, bf16[128,256]{1,0:T(8,128)(2,1)S(1)} %collective-permute-done.2.far, bf16[128,256]{1,0:T(8,128)(2,1)S(1)} %collective-permute-done.3.near, bf16[128,256]{1,0:T(8,128)(2,1)S(1)} %bitcast.10, ...), custom_call_target="tpu_custom_call" | custom-call | flops 1140850688 | bytes 524288 | tf_op jit(solution)/shard_map/pallas_call | solution.py:235
  14.9 0.3 collective-permute-done.1
  15.2 0.0 copy-start
  15.2 0.0 copy-start.1
  15.2 2.2 %collective-permute-start.4 = (f32[4,32,128]{2,1,0:T(8,128)S(1)}, f32[4,32,128]{2,1,0:T(8,128)S(1)}, u32[]{:S(2)}, u32[]{:S(2)}) collective-permute-start(f32[4,32,128]{2,1,0:T(8,128)S(1)} %pad_maximum_fusion.1), channel_id=1, source_target_pairs={{0,192},{32,224},{64,128},{96,160},{128,64},{160,96},{192,0},{224,... | collective-permute-start | bytes 196616 | tf_op jit(solution)/shard_map/ppermute | solution.py:250
  17.4 2.9 %shard_map.102 = (f32[16,16,128]{2,1,0:T(8,128)S(1)}, f32[256,128]{1,0:T(8,128)S(1)}) custom-call(s32[1]{0:T(128)} %bitcast.2.core, bf16[272,2048]{1,0:T(8,128)(2,1)S(1)} %get-tuple-element.46.win, bf16[8,512,256]{2,1,0:T(8,128)(2,1)S(1)} %shard_map.100.shifts, f32[256,128]{1,0:T(8,128)S(1)} %get-tuple-element.39.even), custom_call_target="tpu_custom_call" | custom-call | flops 2281701376 | bytes 524288 | tf_op jit(solution)/shard_map/pallas_call | solution.py:235
  20.2 0.5 collective-permute-done.4
  20.8 0.0 copy-done
  20.8 0.0 copy-done.1
  20.8 0.7 %shard_map.103 = (f32[16,8,128]{2,1,0:T(8,128)S(1)}, f32[16,24,128]{2,1,0:T(8,128)S(1)}, f32[32,1024]{1,0:T(8,128)S(1)}, f32[32,1024]{1,0:T(8,128)S(1)}) custom-call(s32[1]{0:T(128)} %bitcast.first, s32[1]{0:T(128)} %bitcast.1.depth, s32[1]{0:T(128)} %bitcast.2.core, s32[1]{0:T(128)S(6)} %copy.11.defocus, f32[8,32,128]{2,1,0:T(8,128)S(1)} %pad_maximum_fusion.phase, ...), custom_call_target="tpu_custom_call" | custom-call | flops 201326592 | bytes 3145728 | tf_op jit(solution)/shard_map/pallas_call | solution.py:235
  21.5 0.1 collective-permute-start.5
  21.6 0.0 copy-start.2
  21.6 0.0 copy-start.3
  21.6 1.7 %shard_map.104 = f32[16,24,128]{2,1,0:T(8,128)S(1)} custom-call(s32[1]{0:T(128)} %bitcast.2.core, bf16[272,2048]{1,0:T(8,128)(2,1)S(1)} %get-tuple-element.46.win, bf16[8,512,256]{2,1,0:T(8,128)(2,1)S(1)} %shard_map.100.shifts, f32[256,128]{1,0:T(8,128)S(1)} %get-tuple-element.47.kept, f32[16,8,128]{2,1,0:T(8,128)S(1)} %get-tuple-element.48.keep_z), custom_call_target="tpu_custom_call" | custom-call | flops 1140850688 | bytes 524288 | tf_op jit(solution)/shard_map/pallas_call | solution.py:235
  23.3 0.0 collective-permute-done.5
  23.4 17.1 %all_to_all.15.payload = f32[16,24,128]{2,1,0:T(8,128)S(1)} all-to-all(f32[16,24,128]{2,1,0:T(8,128)S(1)} %add.7), channel_id=1, replica_groups={{30,28,26,24,22,20,18,16,14,12,10,8,6,4,2,0},{31,29,27,25,23,21,19,17,1..., dimensions={0} | all-to-all | bytes 393216 | tf_op jit(solution)/shard_map/all_to_all | solution.py:260
  40.5 0.0 copy-done.2
  40.5 0.0 copy-done.3
  40.5 0.0 copy-start.4
  40.5 0.0 copy-start.5
  40.5 1.0 %shard_map.105 = f32[32,4,128]{2,1,0:T(4,128)S(1)} custom-call(f32[16,24,128]{2,1,0:T(8,128)S(1)} %all_to_all.15.payload, bf16[1024,512]{1,0:T(8,128)(2,1)S(1)} %copy-done.1, bf16[1024,512]{1,0:T(8,128)(2,1)S(1)} %copy-done, bf16[256,2048]{1,0:T(8,128)(2,1)S(1)} %copy-done.3, bf16[256,2048]{1,0:T(8,128)(2,1)S(1)} %copy-done.2), custom_call_target="tpu_custom_call" | custom-call | flops 100663296 | bytes 5242880 | tf_op jit(solution)/shard_map/pallas_call | solution.py:235
  41.5 12.1 %all_to_all.16 = f32[32,4,128]{2,1,0:T(4,128)S(1)} all-to-all(f32[32,4,128]{2,1,0:T(4,128)S(1)} %shard_map.105), channel_id=1, replica_groups={{31,30,29,28,27,26,25,24,23,22,21,20,19,18,17,16,15,14,13,12,11,10,9,8,..., dimensions={0} | all-to-all | bytes 131072 | tf_op jit(solution)/shard_map/all_to_all | solution.py:260
  53.6 0.0 copy-done.4
  53.6 0.0 copy-done.5
  53.6 0.5 shard_map.106
  54.1 9.8 %all_to_all.17 = f32[8,32,128]{2,1,0:T(8,128)S(1)} all-to-all(f32[8,32,128]{2,1,0:T(8,128)S(1)} %shard_map.106), channel_id=1, replica_groups={{224,192,160,128,96,64,32,0},{225,193,161,129,97,65,33,1},{226,194,162,..., dimensions={0} | all-to-all | bytes 262144 | tf_op jit(solution)/shard_map/all_to_all | solution.py:260
  63.9 0.6 reduce_sum.9
  (4 shorter events, 0.0 us)
Async XLA Ops:
  0.0 10.9 %copy-start.8 = (f32[32,128]{1,0:T(8,128)S(1)}, f32[32,128]{1,0:T(8,128)}, u32[]{:S(2)}) copy-start(f32[32,128]{1,0:T(8,128)} %param.12) | copy-start | bytes 49156
  0.0 10.8 %collective-permute-start = (f32[32,128]{1,0:T(8,128)}, f32[32,128]{1,0:T(8,128)S(1)}, u32[]{:S(2)}, u32[]{:S(2)}) collective-permute-start(f32[32,128]{1,0:T(8,128)} %param.12), channel_id=1, source_target_pairs={{0,64},{32,96},{64,0},{96,32},{128,192},{160,224},{192,128},{224,1... | collective-permute-start | bytes 49160 | tf_op jit(solution)/shard_map/ppermute | solution.py:250
  1.5 11.8 %collective-permute-start.2 = (bf16[128,256]{1,0:T(8,128)(2,1)}, bf16[128,256]{1,0:T(8,128)(2,1)S(1)}, u32[]{:S(2)}, u32[]{:S(2)}) collective-permute-start(bf16[128,256]{1,0:T(8,128)(2,1)} %bitcast.8), channel_id=1, source_target_pairs={{1,2},{3,4},{5,6},{7,8},{9,10},{11,12},{13,14},{15,16},{17,18},{19... | collective-permute-start | bytes 196616 | tf_op jit(solution)/shard_map/ppermute | solution.py:255
  8.8 0.8 %copy-start.6 = (bf16[128,256]{1,0:T(8,128)(2,1)S(1)}, bf16[128,256]{1,0:T(8,128)(2,1)}, u32[]{:S(2)}) copy-start(bf16[128,256]{1,0:T(8,128)(2,1)} %grad.1) | copy-start | bytes 196612
  9.7 1.1 %copy-start.7 = (bf16[1,128,256]{2,1,0:T(8,128)(2,1)S(1)}, bf16[1,128,256]{2,1,0:T(8,128)(2,1)}, u32[]{:S(2)}) copy-start(bf16[1,128,256]{2,1,0:T(8,128)(2,1)} %param.10) | copy-start | bytes 196612
  10.8 2.4 %collective-permute-start.3 = (bf16[128,256]{1,0:T(8,128)(2,1)S(1)}, bf16[128,256]{1,0:T(8,128)(2,1)S(1)}, u32[]{:S(2)}, u32[]{:S(2)}) collective-permute-start(bf16[128,256]{1,0:T(8,128)(2,1)S(1)} %bitcast.9), channel_id=1, source_target_pairs={{0,1},{1,0},{2,3},{3,2},{4,5},{5,4},{6,7},{7,6},{8,9},{9,8},{10,11... | collective-permute-start | bytes 196616 | tf_op jit(solution)/shard_map/ppermute | solution.py:264
  10.9 4.2 %collective-permute-start.1 = (f32[2,32,128]{2,1,0:T(8,128)S(1)}, f32[2,32,128]{2,1,0:T(8,128)S(1)}, u32[]{:S(2)}, u32[]{:S(2)}) collective-permute-start(f32[2,32,128]{2,1,0:T(8,128)S(1)} %pad_maximum_fusion.2), channel_id=1, source_target_pairs={{0,32},{32,0},{64,96},{96,64},{128,160},{160,128},{192,224},{224,1... | collective-permute-start | bytes 98312 | tf_op jit(solution)/shard_map/ppermute | solution.py:250
  15.2 5.6 %copy-start = (bf16[1024,512]{1,0:T(8,128)(2,1)S(1)}, bf16[1024,512]{1,0:T(8,128)(2,1)}, u32[]{:S(2)}) copy-start(bf16[1024,512]{1,0:T(8,128)(2,1)} %constant.34.clone.low.g_low) | copy-start | bytes 3145732
  15.2 5.6 %copy-start.1 = (bf16[1024,512]{1,0:T(8,128)(2,1)S(1)}, bf16[1024,512]{1,0:T(8,128)(2,1)}, u32[]{:S(2)}) copy-start(bf16[1024,512]{1,0:T(8,128)(2,1)} %constant.33.clone.high.g_high) | copy-start | bytes 3145732
  15.2 5.6 %collective-permute-start.4 = (f32[4,32,128]{2,1,0:T(8,128)S(1)}, f32[4,32,128]{2,1,0:T(8,128)S(1)}, u32[]{:S(2)}, u32[]{:S(2)}) collective-permute-start(f32[4,32,128]{2,1,0:T(8,128)S(1)} %pad_maximum_fusion.1), channel_id=1, source_target_pairs={{0,192},{32,224},{64,128},{96,160},{128,64},{160,96},{192,0},{224,... | collective-permute-start | bytes 196616 | tf_op jit(solution)/shard_map/ppermute | solution.py:250
  21.5 1.8 %collective-permute-start.5 = (f32[16,24,128]{2,1,0:T(8,128)S(1)}, f32[16,24,128]{2,1,0:T(8,128)S(1)}, u32[]{:S(2)}, u32[]{:S(2)}) collective-permute-start(f32[16,24,128]{2,1,0:T(8,128)S(1)} %get-tuple-element.45), channel_id=1, source_target_pairs={{0,1},{1,0},{2,3},{3,2},{4,5},{5,4},{6,7},{7,6},{8,9},{9,8},{10,11... | collective-permute-start | bytes 589832 | tf_op jit(solution)/shard_map/ppermute | solution.py:264
  21.6 18.9 %copy-start.2 = (bf16[256,2048]{1,0:T(8,128)(2,1)S(1)}, bf16[256,2048]{1,0:T(8,128)(2,1)}, u32[]{:S(2)}) copy-start(bf16[256,2048]{1,0:T(8,128)(2,1)} %constant.36.clone.s_low) | copy-start | bytes 3145732
  21.6 18.9 %copy-start.3 = (bf16[256,2048]{1,0:T(8,128)(2,1)S(1)}, bf16[256,2048]{1,0:T(8,128)(2,1)}, u32[]{:S(2)}) copy-start(bf16[256,2048]{1,0:T(8,128)(2,1)} %constant.35.clone.s_high) | copy-start | bytes 3145732
  40.5 13.1 %copy-start.4 = (bf16[256,2048]{1,0:T(8,128)(2,1)S(1)}, bf16[256,2048]{1,0:T(8,128)(2,1)}, u32[]{:S(2)}) copy-start(bf16[256,2048]{1,0:T(8,128)(2,1)} %constant.38.clone.low) | copy-start | bytes 3145732
  40.5 13.1 %copy-start.5 = (bf16[256,2048]{1,0:T(8,128)(2,1)S(1)}, bf16[256,2048]{1,0:T(8,128)(2,1)}, u32[]{:S(2)}) copy-start(bf16[256,2048]{1,0:T(8,128)(2,1)} %constant.37.clone.high) | copy-start | bytes 3145732

commit v3 on v2

--- a/solution.py
+++ b/solution.py
@@ -12,6 +12,9 @@
 FREQ = 2 * HALF
 GROUP = 16
 GATHER_MASKS = (0, 2, 1, 3, 6, 4, 7, 5)
+CHIP_ORDER = tuple(8 * y + z for z in reversed(range(8)) for y in (1, 0))
+TILE_ORDER = tuple(2 * chip + core for chip in CHIP_ORDER for core in (1, 0))
+DEPTH_ORDER = tuple(reversed(range(8)))
 EVEN, ODD = (0, 2, 4, 6), (1, 3, 5, 7)
 WINDOW = FREQ + GROUP
 defocus_step = 0.5
@@ -28,8 +31,9 @@
     cos, sin = np.cos(angle) * PUPIL**-0.5, -np.sin(angle) * PUPIL**-0.5
     gather = split_table(np.concatenate([cos.T, sin.T], axis=1))
     spread = split_table(np.concatenate([cos, sin], axis=1))
-    half, chip, core, row = np.indices((2, FREQ // GROUP, 2, 4)).reshape(4, -1)
-    arrived = 128 * (1 - core) + 8 * chip + 4 * half + row
+    half, place, row = np.indices((2, len(TILE_ORDER), 4)).reshape(3, -1)
+    tile = np.array(TILE_ORDER)[place]
+    arrived = 128 * (tile % 2) + 8 * np.argsort(CHIP_ORDER)[tile // 2] + 4 * half + row
     return gather, spread, [part[arrived] for part in spread]
 
 
@@ -197,7 +201,7 @@
     for chip in range(1, chips):
         kernel_grad = kernel_grad + payload[chip, :16]
     kernel_grad = jnp.concatenate([kernel_grad[:8], kernel_grad[8:]], axis=1)
-    order = list(reversed(range(chips)))
+    order = [CHIP_ORDER.index(chip) for chip in range(chips)]
     z_re = jnp.concatenate([payload[place, 16:, :rows] for place in order], axis=1)
     z_im = jnp.concatenate([payload[place, 16:, rows:] for place in order], axis=1)
     terms = dot3(jnp.concatenate([z_re, z_im], axis=0), g_high, g_low)
@@ -212,7 +216,7 @@
         here = slice(rows * tile, rows * (tile + 1))
         parts = [part[:, here] for part in (gz_re, gz_im)]
         rows_of = [part[half : half + 4] for half in (0, 4) for part in parts]
-        out[2 * chips - 1 - tile] = jnp.concatenate(rows_of, axis=1)
+        out[TILE_ORDER.index(tile)] = jnp.concatenate(rows_of, axis=1)
 
 
 def phase_kernel(payload, field_re, field_im, high, low, out):
@@ -226,7 +230,7 @@
     phase = field_re[...] * ge_im - field_im[...] * ge_re
     width = out.shape[2]
     for block in range(out.shape[0]):
-        out[out.shape[0] - 1 - block] = phase[:, width * block : width * (block + 1)]
+        out[DEPTH_ORDER.index(block)] = phase[:, width * block : width * (block + 1)]
 
 
 def call(kernel, outs, scratch, flops, moved, smem=0):
@@ -255,9 +259,8 @@
     return lax.ppermute(x, ("chip", "core"), pairs + [(j, i) for i, j in pairs])
 
 
-def redistribute(x, axis):
-    order = list(reversed(range(x.shape[0])))
-    return lax.all_to_all(x, axis, 0, 0, tiled=True, axis_index_groups=[order])
+def redistribute(x, axis, order):
+    return lax.all_to_all(x, axis, 0, 0, tiled=True, axis_index_groups=[list(order)])
 
 
 def swap(x):
@@ -322,7 +325,7 @@
     other = swap(send)
     keep = call(third_kernel, both, [], 4 * work, 2**19, smem=1)(core, win, shifts, even, keep_z)
     other, keep = lax.optimization_barrier((other, keep))
-    payload = redistribute(keep + other, "chip")
+    payload = redistribute(keep + other, "chip", CHIP_ORDER)
     payload = call(
         middle_kernel,
         jax.ShapeDtypeStruct((2 * chips, 4, HALF), f32),
@@ -330,7 +333,7 @@
         2 * 96 * PUPIL * 2 * FREQ,
         5 * 2**20,
     )(payload, g_high, g_low, s_high, s_low)
-    payload = redistribute(payload, ("chip", "core"))
+    payload = redistribute(payload, ("chip", "core"), TILE_ORDER)
     parts = call(
         phase_kernel,
         jax.ShapeDtypeStruct((depths, rows, width), f32),
@@ -338,7 +341,7 @@
         2 * 192 * PUPIL * 2 * FREQ,
         3 * 2**20,
     )(payload.reshape(HALF, HALF), field_re, field_im, r_high, r_low)
-    parts = redistribute(parts, "depth")
+    parts = redistribute(parts, "depth", DEPTH_ORDER)
     return jnp.sum(parts, axis=0)
 
 

time: 64.8 us -> 64.9 us (level)
  no operation moved by 1% of the time
where the time goes in v3:
time: 64.9 us; the launch traced here: 64.6 us
  blocking collectives  39.1 us (60%)
  starting transfers between devices  12.8 us (20%)
  Pallas kernels  9.45 us (15%)
  local copies, waits for them, and re-layouts  0.87 us (1%)
  between operations  0.84 us (1%)
  waiting for transfers between devices  0.83 us (1%)
  other arithmetic  0.66 us (1%)
    all_to_all x3, blocking collectives, redistribute(): lax.all_to_all(x, axis, 0, 0, tiled=True, axis_index_groups=[list(order)])  39.1 us
    pallas_call x7, Pallas kernels, run(): pl.pallas_call(kernel, out_shape=outs, in_specs=[pl.BlockSpec(memory_spac...  9.45 us
    ppermute x1, starting transfers between devices, beside(): return lax.ppermute(x, ('chip', 'core'), pairs + [(j, i) for i, j in pairs])  6.68 us
    ppermute x3, starting transfers between devices, over_depth(): return lax.ppermute(x, 'depth', [(i, i ^ mask) for i in range(count)])  5.97 us
  transfers between devices with their start and end apart: 6, of which 2 were waited for; matrix products, arithmetic and copies ran while one was open for 0% of the time, Pallas kernels for 11%

profile of v3, /device:TPU:16, one launch (start us, length us, event | category | flops | bytes accessed | tf_op | source)
XLA Modules:
  0.0 64.6 jit_solution(15140980954086773788)
XLA Ops:
  0.0 0.0 copy-start.8
  0.0 1.5 %collective-permute-start = (f32[32,128]{1,0:T(8,128)}, f32[32,128]{1,0:T(8,128)S(1)}, u32[]{:S(2)}, u32[]{:S(2)}) collective-permute-start(f32[32,128]{1,0:T(8,128)} %param.12), channel_id=1, source_target_pairs={{0,64},{32,96},{64,0},{96,32},{128,192},{160,224},{192,128},{224,1... | collective-permute-start | bytes 49160 | tf_op jit(solution)/shard_map/ppermute | solution.py:254
  1.5 6.7 %collective-permute-start.2 = (bf16[128,256]{1,0:T(8,128)(2,1)}, bf16[128,256]{1,0:T(8,128)(2,1)S(1)}, u32[]{:S(2)}, u32[]{:S(2)}) collective-permute-start(bf16[128,256]{1,0:T(8,128)(2,1)} %bitcast.8), channel_id=1, source_target_pairs={{1,2},{3,4},{5,6},{7,8},{9,10},{11,12},{13,14},{15,16},{17,18},{19... | collective-permute-start | bytes 196616 | tf_op jit(solution)/shard_map/ppermute | solution.py:259
  8.8 0.0 copy-start.6
  8.9 0.8 %copy-done.6 = bf16[128,256]{1,0:T(8,128)(2,1)S(1)} copy-done((bf16[128,256]{1,0:T(8,128)(2,1)S(1)}, bf16[128,256]{1,0:T(8,128)(2,1)}, u32[]{:S(2)}) %copy-start.6) | copy-done | bytes 65560
  9.7 0.0 copy-start.7
  9.7 1.1 %shard_map.100.shifts = bf16[8,512,256]{2,1,0:T(8,128)(2,1)S(1)} custom-call(bf16[128,256]{1,0:T(8,128)(2,1)S(1)} %copy-done.6), custom_call_target="tpu_custom_call" | custom-call | flops 268435456 | bytes 4194304 | tf_op jit(solution)/shard_map/pallas_call | solution.py:239
  10.8 0.0 collective-permute-done
  10.8 0.0 copy-done.7
  10.8 0.1 collective-permute-start.3
  10.9 0.0 copy-done.8
  10.9 2.3 %collective-permute-start.1 = (f32[2,32,128]{2,1,0:T(8,128)S(1)}, f32[2,32,128]{2,1,0:T(8,128)S(1)}, u32[]{:S(2)}, u32[]{:S(2)}) collective-permute-start(f32[2,32,128]{2,1,0:T(8,128)S(1)} %pad_maximum_fusion.2), channel_id=1, source_target_pairs={{0,32},{32,0},{64,96},{96,64},{128,160},{160,128},{192,224},{224,1... | collective-permute-start | bytes 98312 | tf_op jit(solution)/shard_map/ppermute | solution.py:254
  13.2 0.0 collective-permute-done.2.far
  13.2 0.0 collective-permute-done.3.near
  13.3 1.6 %shard_map.101 = (bf16[272,2048]{1,0:T(8,128)(2,1)S(1)}, f32[256,128]{1,0:T(8,128)S(1)}) custom-call(s32[1]{0:T(128)} %bitcast.2.core, bf16[128,256]{1,0:T(8,128)(2,1)S(1)} %collective-permute-done.2.far, bf16[128,256]{1,0:T(8,128)(2,1)S(1)} %collective-permute-done.3.near, bf16[128,256]{1,0:T(8,128)(2,1)S(1)} %bitcast.10, ...), custom_call_target="tpu_custom_call" | custom-call | flops 1140850688 | bytes 524288 | tf_op jit(solution)/shard_map/pallas_call | solution.py:239
  14.9 0.3 collective-permute-done.1
  15.2 0.0 copy-start
  15.2 0.0 copy-start.1
  15.2 2.2 %collective-permute-start.4 = (f32[4,32,128]{2,1,0:T(8,128)S(1)}, f32[4,32,128]{2,1,0:T(8,128)S(1)}, u32[]{:S(2)}, u32[]{:S(2)}) collective-permute-start(f32[4,32,128]{2,1,0:T(8,128)S(1)} %pad_maximum_fusion.1), channel_id=1, source_target_pairs={{0,192},{32,224},{64,128},{96,160},{128,64},{160,96},{192,0},{224,... | collective-permute-start | bytes 196616 | tf_op jit(solution)/shard_map/ppermute | solution.py:254
  17.4 2.9 %shard_map.102 = (f32[16,16,128]{2,1,0:T(8,128)S(1)}, f32[256,128]{1,0:T(8,128)S(1)}) custom-call(s32[1]{0:T(128)} %bitcast.2.core, bf16[272,2048]{1,0:T(8,128)(2,1)S(1)} %get-tuple-element.46.win, bf16[8,512,256]{2,1,0:T(8,128)(2,1)S(1)} %shard_map.100.shifts, f32[256,128]{1,0:T(8,128)S(1)} %get-tuple-element.39.even), custom_call_target="tpu_custom_call" | custom-call | flops 2281701376 | bytes 524288 | tf_op jit(solution)/shard_map/pallas_call | solution.py:239
  20.2 0.5 collective-permute-done.4
  20.8 0.0 copy-done
  20.8 0.0 copy-done.1
  20.8 0.7 %shard_map.103 = (f32[16,8,128]{2,1,0:T(8,128)S(1)}, f32[16,24,128]{2,1,0:T(8,128)S(1)}, f32[32,1024]{1,0:T(8,128)S(1)}, f32[32,1024]{1,0:T(8,128)S(1)}) custom-call(s32[1]{0:T(128)} %bitcast.first, s32[1]{0:T(128)} %bitcast.1.depth, s32[1]{0:T(128)} %bitcast.2.core, s32[1]{0:T(128)S(6)} %copy.11.defocus, f32[8,32,128]{2,1,0:T(8,128)S(1)} %pad_maximum_fusion.phase, ...), custom_call_target="tpu_custom_call" | custom-call | flops 201326592 | bytes 3145728 | tf_op jit(solution)/shard_map/pallas_call | solution.py:239
  21.5 0.1 collective-permute-start.5
  21.6 0.0 copy-start.2
  21.6 0.0 copy-start.3
  21.6 1.7 %shard_map.104 = f32[16,24,128]{2,1,0:T(8,128)S(1)} custom-call(s32[1]{0:T(128)} %bitcast.2.core, bf16[272,2048]{1,0:T(8,128)(2,1)S(1)} %get-tuple-element.46.win, bf16[8,512,256]{2,1,0:T(8,128)(2,1)S(1)} %shard_map.100.shifts, f32[256,128]{1,0:T(8,128)S(1)} %get-tuple-element.47.kept, f32[16,8,128]{2,1,0:T(8,128)S(1)} %get-tuple-element.48.keep_z), custom_call_target="tpu_custom_call" | custom-call | flops 1140850688 | bytes 524288 | tf_op jit(solution)/shard_map/pallas_call | solution.py:239
  23.3 0.0 collective-permute-done.5
  23.4 16.5 %all_to_all.15.payload = f32[16,24,128]{2,1,0:T(8,128)S(1)} all-to-all(f32[16,24,128]{2,1,0:T(8,128)S(1)} %add.7), channel_id=1, replica_groups={{30,14,28,12,26,10,24,8,22,6,20,4,18,2,16,0},{31,15,29,13,27,11,25,9,23..., dimensions={0} | all-to-all | bytes 393216 | tf_op jit(solution)/shard_map/all_to_all | solution.py:263
  39.9 0.0 copy-done.2
  39.9 0.0 copy-done.3
  39.9 0.0 copy-start.4
  39.9 0.0 copy-start.5
  39.9 1.0 %shard_map.105 = f32[32,4,128]{2,1,0:T(4,128)S(1)} custom-call(f32[16,24,128]{2,1,0:T(8,128)S(1)} %all_to_all.15.payload, bf16[1024,512]{1,0:T(8,128)(2,1)S(1)} %copy-done.1, bf16[1024,512]{1,0:T(8,128)(2,1)S(1)} %copy-done, bf16[256,2048]{1,0:T(8,128)(2,1)S(1)} %copy-done.3, bf16[256,2048]{1,0:T(8,128)(2,1)S(1)} %copy-done.2), custom_call_target="tpu_custom_call" | custom-call | flops 100663296 | bytes 5242880 | tf_op jit(solution)/shard_map/pallas_call | solution.py:239
  40.9 12.8 %all_to_all.16 = f32[32,4,128]{2,1,0:T(4,128)S(1)} all-to-all(f32[32,4,128]{2,1,0:T(4,128)S(1)} %shard_map.105), channel_id=1, replica_groups={{31,30,15,14,29,28,13,12,27,26,11,10,25,24,9,8,23,22,7,6,21,20,5,4,19,1..., dimensions={0} | all-to-all | bytes 131072 | tf_op jit(solution)/shard_map/all_to_all | solution.py:263
  53.7 0.0 copy-done.4
  53.7 0.0 copy-done.5
  53.7 0.5 shard_map.106
  54.2 9.8 %all_to_all.17 = f32[8,32,128]{2,1,0:T(8,128)S(1)} all-to-all(f32[8,32,128]{2,1,0:T(8,128)S(1)} %shard_map.106), channel_id=1, replica_groups={{224,192,160,128,96,64,32,0},{225,193,161,129,97,65,33,1},{226,194,162,..., dimensions={0} | all-to-all | bytes 262144 | tf_op jit(solution)/shard_map/all_to_all | solution.py:263
  64.0 0.6 reduce_sum.9
  (4 shorter events, 0.0 us)
Async XLA Ops:
  0.0 10.9 %copy-start.8 = (f32[32,128]{1,0:T(8,128)S(1)}, f32[32,128]{1,0:T(8,128)}, u32[]{:S(2)}) copy-start(f32[32,128]{1,0:T(8,128)} %param.12) | copy-start | bytes 49156
  0.0 10.8 %collective-permute-start = (f32[32,128]{1,0:T(8,128)}, f32[32,128]{1,0:T(8,128)S(1)}, u32[]{:S(2)}, u32[]{:S(2)}) collective-permute-start(f32[32,128]{1,0:T(8,128)} %param.12), channel_id=1, source_target_pairs={{0,64},{32,96},{64,0},{96,32},{128,192},{160,224},{192,128},{224,1... | collective-permute-start | bytes 49160 | tf_op jit(solution)/shard_map/ppermute | solution.py:254
  1.5 11.8 %collective-permute-start.2 = (bf16[128,256]{1,0:T(8,128)(2,1)}, bf16[128,256]{1,0:T(8,128)(2,1)S(1)}, u32[]{:S(2)}, u32[]{:S(2)}) collective-permute-start(bf16[128,256]{1,0:T(8,128)(2,1)} %bitcast.8), channel_id=1, source_target_pairs={{1,2},{3,4},{5,6},{7,8},{9,10},{11,12},{13,14},{15,16},{17,18},{19... | collective-permute-start | bytes 196616 | tf_op jit(solution)/shard_map/ppermute | solution.py:259
  8.8 0.8 %copy-start.6 = (bf16[128,256]{1,0:T(8,128)(2,1)S(1)}, bf16[128,256]{1,0:T(8,128)(2,1)}, u32[]{:S(2)}) copy-start(bf16[128,256]{1,0:T(8,128)(2,1)} %grad.1) | copy-start | bytes 196612
  9.7 1.1 %copy-start.7 = (bf16[1,128,256]{2,1,0:T(8,128)(2,1)S(1)}, bf16[1,128,256]{2,1,0:T(8,128)(2,1)}, u32[]{:S(2)}) copy-start(bf16[1,128,256]{2,1,0:T(8,128)(2,1)} %param.10) | copy-start | bytes 196612
  10.8 2.4 %collective-permute-start.3 = (bf16[128,256]{1,0:T(8,128)(2,1)S(1)}, bf16[128,256]{1,0:T(8,128)(2,1)S(1)}, u32[]{:S(2)}, u32[]{:S(2)}) collective-permute-start(bf16[128,256]{1,0:T(8,128)(2,1)S(1)} %bitcast.9), channel_id=1, source_target_pairs={{0,1},{1,0},{2,3},{3,2},{4,5},{5,4},{6,7},{7,6},{8,9},{9,8},{10,11... | collective-permute-start | bytes 196616 | tf_op jit(solution)/shard_map/ppermute | solution.py:267
  10.9 4.2 %collective-permute-start.1 = (f32[2,32,128]{2,1,0:T(8,128)S(1)}, f32[2,32,128]{2,1,0:T(8,128)S(1)}, u32[]{:S(2)}, u32[]{:S(2)}) collective-permute-start(f32[2,32,128]{2,1,0:T(8,128)S(1)} %pad_maximum_fusion.2), channel_id=1, source_target_pairs={{0,32},{32,0},{64,96},{96,64},{128,160},{160,128},{192,224},{224,1... | collective-permute-start | bytes 98312 | tf_op jit(solution)/shard_map/ppermute | solution.py:254
  15.2 5.6 %copy-start = (bf16[1024,512]{1,0:T(8,128)(2,1)S(1)}, bf16[1024,512]{1,0:T(8,128)(2,1)}, u32[]{:S(2)}) copy-start(bf16[1024,512]{1,0:T(8,128)(2,1)} %constant.34.clone.low.g_low) | copy-start | bytes 3145732
  15.2 5.6 %copy-start.1 = (bf16[1024,512]{1,0:T(8,128)(2,1)S(1)}, bf16[1024,512]{1,0:T(8,128)(2,1)}, u32[]{:S(2)}) copy-start(bf16[1024,512]{1,0:T(8,128)(2,1)} %constant.33.clone.high.g_high) | copy-start | bytes 3145732
  15.2 5.6 %collective-permute-start.4 = (f32[4,32,128]{2,1,0:T(8,128)S(1)}, f32[4,32,128]{2,1,0:T(8,128)S(1)}, u32[]{:S(2)}, u32[]{:S(2)}) collective-permute-start(f32[4,32,128]{2,1,0:T(8,128)S(1)} %pad_maximum_fusion.1), channel_id=1, source_target_pairs={{0,192},{32,224},{64,128},{96,160},{128,64},{160,96},{192,0},{224,... | collective-permute-start | bytes 196616 | tf_op jit(solution)/shard_map/ppermute | solution.py:254
  21.5 1.8 %collective-permute-start.5 = (f32[16,24,128]{2,1,0:T(8,128)S(1)}, f32[16,24,128]{2,1,0:T(8,128)S(1)}, u32[]{:S(2)}, u32[]{:S(2)}) collective-permute-start(f32[16,24,128]{2,1,0:T(8,128)S(1)} %get-tuple-element.45), channel_id=1, source_target_pairs={{0,1},{1,0},{2,3},{3,2},{4,5},{5,4},{6,7},{7,6},{8,9},{9,8},{10,11... | collective-permute-start | bytes 589832 | tf_op jit(solution)/shard_map/ppermute | solution.py:267
  21.6 18.3 %copy-start.2 = (bf16[256,2048]{1,0:T(8,128)(2,1)S(1)}, bf16[256,2048]{1,0:T(8,128)(2,1)}, u32[]{:S(2)}) copy-start(bf16[256,2048]{1,0:T(8,128)(2,1)} %constant.36.clone.s_low) | copy-start | bytes 3145732
  21.6 18.3 %copy-start.3 = (bf16[256,2048]{1,0:T(8,128)(2,1)S(1)}, bf16[256,2048]{1,0:T(8,128)(2,1)}, u32[]{:S(2)}) copy-start(bf16[256,2048]{1,0:T(8,128)(2,1)} %constant.35.clone.s_high) | copy-start | bytes 3145732
  39.9 13.8 %copy-start.4 = (bf16[256,2048]{1,0:T(8,128)(2,1)S(1)}, bf16[256,2048]{1,0:T(8,128)(2,1)}, u32[]{:S(2)}) copy-start(bf16[256,2048]{1,0:T(8,128)(2,1)} %constant.38.clone.low) | copy-start | bytes 3145732
  39.9 13.8 %copy-start.5 = (bf16[256,2048]{1,0:T(8,128)(2,1)S(1)}, bf16[256,2048]{1,0:T(8,128)(2,1)}, u32[]{:S(2)}) copy-start(bf16[256,2048]{1,0:T(8,128)(2,1)} %constant.37.clone.high) | copy-start | bytes 3145732

commit v4 on v3

--- a/solution.py
+++ b/solution.py
@@ -12,9 +12,15 @@
 FREQ = 2 * HALF
 GROUP = 16
 GATHER_MASKS = (0, 2, 1, 3, 6, 4, 7, 5)
-CHIP_ORDER = tuple(8 * y + z for z in reversed(range(8)) for y in (1, 0))
-TILE_ORDER = tuple(2 * chip + core for chip in CHIP_ORDER for core in (1, 0))
-DEPTH_ORDER = tuple(reversed(range(8)))
+CHIPS = tuple(8 * y + z for z in reversed(range(8)) for y in (1, 0))
+CHIP_ORDERS = (CHIPS, CHIPS[8:] + CHIPS[:8])
+TILE_ORDER = tuple(
+    16 * y + 2 * z + core
+    for _, z, y, core in sorted(
+        ((z + 1.5 * (y ^ core), z, y, core) for z in range(8) for y in (0, 1) for core in (0, 1)),
+        reverse=True,
+    )
+)
 EVEN, ODD = (0, 2, 4, 6), (1, 3, 5, 7)
 WINDOW = FREQ + GROUP
 defocus_step = 0.5
@@ -33,7 +39,8 @@
     spread = split_table(np.concatenate([cos, sin], axis=1))
     half, place, row = np.indices((2, len(TILE_ORDER), 4)).reshape(3, -1)
     tile = np.array(TILE_ORDER)[place]
-    arrived = 128 * (tile % 2) + 8 * np.argsort(CHIP_ORDER)[tile // 2] + 4 * half + row
+    owned = np.argsort(CHIP_ORDERS, axis=1)[tile % 2, tile // 2]
+    arrived = 128 * (tile % 2) + 8 * owned + 4 * half + row
     return gather, spread, [part[arrived] for part in spread]
 
 
@@ -194,16 +201,17 @@
     send[:, 16:] = jnp.where(here, z_high, z_low).reshape(keep.shape)
 
 
-def middle_kernel(payload, g_high, g_low, s_high, s_low, out):
+def middle_kernel(core, payload, g_high, g_low, s_high, s_low, out):
     chips = payload.shape[0]
     rows = PUPIL // chips
     kernel_grad = payload[0, :16]
     for chip in range(1, chips):
         kernel_grad = kernel_grad + payload[chip, :16]
     kernel_grad = jnp.concatenate([kernel_grad[:8], kernel_grad[8:]], axis=1)
-    order = [CHIP_ORDER.index(chip) for chip in range(chips)]
-    z_re = jnp.concatenate([payload[place, 16:, :rows] for place in order], axis=1)
-    z_im = jnp.concatenate([payload[place, 16:, rows:] for place in order], axis=1)
+    blocks = [[payload[order.index(chip), 16:] for order in CHIP_ORDERS] for chip in range(chips)]
+    blocks = [jnp.where(core[0] == 0, *pair) for pair in blocks]
+    z_re = jnp.concatenate([block[:, :rows] for block in blocks], axis=1)
+    z_im = jnp.concatenate([block[:, rows:] for block in blocks], axis=1)
     terms = dot3(jnp.concatenate([z_re, z_im], axis=0), g_high, g_low)
     y_re = terms[:8, :FREQ] - terms[8:, FREQ:]
     y_im = terms[:8, FREQ:] + terms[8:, :FREQ]
@@ -219,7 +227,7 @@
         out[TILE_ORDER.index(tile)] = jnp.concatenate(rows_of, axis=1)
 
 
-def phase_kernel(payload, field_re, field_im, high, low, out):
+def phase_kernel(core, payload, field_re, field_im, high, low, out):
     rows = field_re.shape[0]
     gz = payload[...].T
     gz_re = jnp.concatenate([gz[:rows], gz[2 * rows : 3 * rows]], axis=1)
@@ -230,7 +238,8 @@
     phase = field_re[...] * ge_im - field_im[...] * ge_re
     width = out.shape[2]
     for block in range(out.shape[0]):
-        out[DEPTH_ORDER.index(block)] = phase[:, width * block : width * (block + 1)]
+        place = (out.shape[0] - 1 - block + 4 * core[0]) & (out.shape[0] - 1)
+        out[place] = phase[:, width * block : width * (block + 1)]
 
 
 def call(kernel, outs, scratch, flops, moved, smem=0):
@@ -259,8 +268,8 @@
     return lax.ppermute(x, ("chip", "core"), pairs + [(j, i) for i, j in pairs])
 
 
-def redistribute(x, axis, order):
-    return lax.all_to_all(x, axis, 0, 0, tiled=True, axis_index_groups=[list(order)])
+def redistribute(x, axis, groups):
+    return lax.all_to_all(x, axis, 0, 0, tiled=True, axis_index_groups=groups)
 
 
 def swap(x):
@@ -325,23 +334,30 @@
     other = swap(send)
     keep = call(third_kernel, both, [], 4 * work, 2**19, smem=1)(core, win, shifts, even, keep_z)
     other, keep = lax.optimization_barrier((other, keep))
-    payload = redistribute(keep + other, "chip", CHIP_ORDER)
+    groups = [[2 * chip + place for chip in CHIP_ORDERS[place]] for place in range(2)]
+    payload = redistribute(keep + other, ("chip", "core"), groups)
     payload = call(
         middle_kernel,
         jax.ShapeDtypeStruct((2 * chips, 4, HALF), f32),
         [],
         2 * 96 * PUPIL * 2 * FREQ,
         5 * 2**20,
-    )(payload, g_high, g_low, s_high, s_low)
-    payload = redistribute(payload, ("chip", "core"), TILE_ORDER)
+        smem=1,
+    )(core, payload, g_high, g_low, s_high, s_low)
+    payload = redistribute(payload, ("chip", "core"), [list(TILE_ORDER)])
     parts = call(
         phase_kernel,
         jax.ShapeDtypeStruct((depths, rows, width), f32),
         [],
         2 * 192 * PUPIL * 2 * FREQ,
         3 * 2**20,
-    )(payload.reshape(HALF, HALF), field_re, field_im, r_high, r_low)
-    parts = redistribute(parts, "depth", DEPTH_ORDER)
+        smem=1,
+    )(core, payload.reshape(HALF, HALF), field_re, field_im, r_high, r_low)
+    groups = [
+        [(depths - 1 - place + 4 * tile) % depths * 2 * chips + tile for place in range(depths)]
+        for tile in range(2 * chips)
+    ]
+    parts = redistribute(parts, ("depth", "chip", "core"), groups)
     return jnp.sum(parts, axis=0)
 
 

time: 64.9 us -> 65.4 us (level)
  no operation moved by 1% of the time
where the time goes in v4:
time: 65.4 us; the launch traced here: 65.1 us
  blocking collectives  39.6 us (61%)
  starting transfers between devices  12.8 us (20%)
  Pallas kernels  9.47 us (14%)
  local copies, waits for them, and re-layouts  0.87 us (1%)
  between operations  0.84 us (1%)
  waiting for transfers between devices  0.83 us (1%)
  other arithmetic  0.66 us (1%)
    all_to_all x3, blocking collectives, redistribute(): return lax.all_to_all(x, axis, 0, 0, tiled=True, axis_index_groups=groups)  39.6 us
    pallas_call x7, Pallas kernels, run(): pl.pallas_call(kernel, out_shape=outs, in_specs=[pl.BlockSpec(memory_spac...  9.47 us
    ppermute x1, starting transfers between devices, beside(): return lax.ppermute(x, ('chip', 'core'), pairs + [(j, i) for i, j in pairs])  6.68 us
    ppermute x3, starting transfers between devices, over_depth(): return lax.ppermute(x, 'depth', [(i, i ^ mask) for i in range(count)])  5.97 us
  transfers between devices with their start and end apart: 6, of which 2 were waited for; matrix products, arithmetic and copies ran while one was open for 0% of the time, Pallas kernels for 11%

profile of v4, /device:TPU:16, one launch (start us, length us, event | category | flops | bytes accessed | tf_op | source)
XLA Modules:
  0.0 65.1 jit_solution(6539227413334300930)
XLA Ops:
  0.0 0.0 copy-start.8
  0.0 1.5 %collective-permute-start = (f32[32,128]{1,0:T(8,128)}, f32[32,128]{1,0:T(8,128)S(1)}, u32[]{:S(2)}, u32[]{:S(2)}) collective-permute-start(f32[32,128]{1,0:T(8,128)} %param.12), channel_id=1, source_target_pairs={{0,64},{32,96},{64,0},{96,32},{128,192},{160,224},{192,128},{224,1... | collective-permute-start | bytes 49160 | tf_op jit(solution)/shard_map/ppermute | solution.py:263
  1.5 6.7 %collective-permute-start.2 = (bf16[128,256]{1,0:T(8,128)(2,1)}, bf16[128,256]{1,0:T(8,128)(2,1)S(1)}, u32[]{:S(2)}, u32[]{:S(2)}) collective-permute-start(bf16[128,256]{1,0:T(8,128)(2,1)} %bitcast.8), channel_id=1, source_target_pairs={{1,2},{3,4},{5,6},{7,8},{9,10},{11,12},{13,14},{15,16},{17,18},{19... | collective-permute-start | bytes 196616 | tf_op jit(solution)/shard_map/ppermute | solution.py:268
  8.8 0.0 copy-start.6
  8.9 0.8 %copy-done.6 = bf16[128,256]{1,0:T(8,128)(2,1)S(1)} copy-done((bf16[128,256]{1,0:T(8,128)(2,1)S(1)}, bf16[128,256]{1,0:T(8,128)(2,1)}, u32[]{:S(2)}) %copy-start.6) | copy-done | bytes 65560
  9.7 0.0 copy-start.7
  9.7 1.1 %shard_map.100.shifts = bf16[8,512,256]{2,1,0:T(8,128)(2,1)S(1)} custom-call(bf16[128,256]{1,0:T(8,128)(2,1)S(1)} %copy-done.6), custom_call_target="tpu_custom_call" | custom-call | flops 268435456 | bytes 4194304 | tf_op jit(solution)/shard_map/pallas_call | solution.py:248
  10.8 0.0 collective-permute-done
  10.8 0.0 copy-done.7
  10.8 0.1 collective-permute-start.3
  10.9 0.0 copy-done.8
  10.9 2.3 %collective-permute-start.1 = (f32[2,32,128]{2,1,0:T(8,128)S(1)}, f32[2,32,128]{2,1,0:T(8,128)S(1)}, u32[]{:S(2)}, u32[]{:S(2)}) collective-permute-start(f32[2,32,128]{2,1,0:T(8,128)S(1)} %pad_maximum_fusion.2), channel_id=1, source_target_pairs={{0,32},{32,0},{64,96},{96,64},{128,160},{160,128},{192,224},{224,1... | collective-permute-start | bytes 98312 | tf_op jit(solution)/shard_map/ppermute | solution.py:263
  13.2 0.0 collective-permute-done.2.far
  13.2 0.0 collective-permute-done.3.near
  13.3 1.6 %shard_map.101 = (bf16[272,2048]{1,0:T(8,128)(2,1)S(1)}, f32[256,128]{1,0:T(8,128)S(1)}) custom-call(s32[1]{0:T(128)} %bitcast.core, bf16[128,256]{1,0:T(8,128)(2,1)S(1)} %collective-permute-done.2.far, bf16[128,256]{1,0:T(8,128)(2,1)S(1)} %collective-permute-done.3.near, bf16[128,256]{1,0:T(8,128)(2,1)S(1)} %bitcast.10, ...), custom_call_target="tpu_custom_call" | custom-call | flops 1140850688 | bytes 524288 | tf_op jit(solution)/shard_map/pallas_call | solution.py:248
  14.9 0.3 collective-permute-done.1
  15.2 0.0 copy-start
  15.2 0.0 copy-start.1
  15.2 2.2 %collective-permute-start.4 = (f32[4,32,128]{2,1,0:T(8,128)S(1)}, f32[4,32,128]{2,1,0:T(8,128)S(1)}, u32[]{:S(2)}, u32[]{:S(2)}) collective-permute-start(f32[4,32,128]{2,1,0:T(8,128)S(1)} %pad_maximum_fusion.1), channel_id=1, source_target_pairs={{0,192},{32,224},{64,128},{96,160},{128,64},{160,96},{192,0},{224,... | collective-permute-start | bytes 196616 | tf_op jit(solution)/shard_map/ppermute | solution.py:263
  17.4 2.9 %shard_map.102 = (f32[16,16,128]{2,1,0:T(8,128)S(1)}, f32[256,128]{1,0:T(8,128)S(1)}) custom-call(s32[1]{0:T(128)} %bitcast.core, bf16[272,2048]{1,0:T(8,128)(2,1)S(1)} %get-tuple-element.46.win, bf16[8,512,256]{2,1,0:T(8,128)(2,1)S(1)} %shard_map.100.shifts, f32[256,128]{1,0:T(8,128)S(1)} %get-tuple-element.39.even), custom_call_target="tpu_custom_call" | custom-call | flops 2281701376 | bytes 524288 | tf_op jit(solution)/shard_map/pallas_call | solution.py:248
  20.2 0.5 collective-permute-done.4
  20.8 0.0 copy-done
  20.8 0.0 copy-done.1
  20.8 0.7 %shard_map.103 = (f32[16,8,128]{2,1,0:T(8,128)S(1)}, f32[16,24,128]{2,1,0:T(8,128)S(1)}, f32[32,1024]{1,0:T(8,128)S(1)}, f32[32,1024]{1,0:T(8,128)S(1)}) custom-call(s32[1]{0:T(128)} %bitcast.1.first, s32[1]{0:T(128)} %bitcast.2.depth, s32[1]{0:T(128)} %bitcast.core, s32[1]{0:T(128)S(6)} %copy.11.defocus, f32[8,32,128]{2,1,0:T(8,128)S(1)} %pad_maximum_fusion.phase, ...), custom_call_target="tpu_custom_call" | custom-call | flops 201326592 | bytes 3145728 | tf_op jit(solution)/shard_map/pallas_call | solution.py:248
  21.5 0.1 collective-permute-start.5
  21.6 0.0 copy-start.2
  21.6 0.0 copy-start.3
  21.6 1.7 %shard_map.104 = f32[16,24,128]{2,1,0:T(8,128)S(1)} custom-call(s32[1]{0:T(128)} %bitcast.core, bf16[272,2048]{1,0:T(8,128)(2,1)S(1)} %get-tuple-element.46.win, bf16[8,512,256]{2,1,0:T(8,128)(2,1)S(1)} %shard_map.100.shifts, f32[256,128]{1,0:T(8,128)S(1)} %get-tuple-element.47.kept, f32[16,8,128]{2,1,0:T(8,128)S(1)} %get-tuple-element.48.keep_z), custom_call_target="tpu_custom_call" | custom-call | flops 1140850688 | bytes 524288 | tf_op jit(solution)/shard_map/pallas_call | solution.py:248
  23.3 0.0 collective-permute-done.5
  23.4 15.9 %all_to_all.15.payload = f32[16,24,128]{2,1,0:T(8,128)S(1)} all-to-all(f32[16,24,128]{2,1,0:T(8,128)S(1)} %add.7), channel_id=1, replica_groups={{30,14,28,12,26,10,24,8,22,6,20,4,18,2,16,0},{23,7,21,5,19,3,17,1,31,15..., dimensions={0} | all-to-all | bytes 393216 | tf_op jit(solution)/shard_map/all_to_all | solution.py:272
  39.2 0.0 copy-done.2
  39.2 0.0 copy-done.3
  39.2 0.0 copy-start.4
  39.2 0.0 copy-start.5
  39.3 1.0 %shard_map.105 = f32[32,4,128]{2,1,0:T(4,128)S(1)} custom-call(s32[1]{0:T(128)} %bitcast.core, f32[16,24,128]{2,1,0:T(8,128)S(1)} %all_to_all.15.payload, bf16[1024,512]{1,0:T(8,128)(2,1)S(1)} %copy-done.1, bf16[1024,512]{1,0:T(8,128)(2,1)S(1)} %copy-done, bf16[256,2048]{1,0:T(8,128)(2,1)S(1)} %copy-done.3, bf16[256,2048]{1,0:T(8,128)(2,1)S(1)} %copy-done.2), custom_call_target="tpu_custom_call" | custom-call | flops 100663296 | bytes 5242880 | tf_op jit(solution)/shard_map/pallas_call | solution.py:248
  40.3 13.7 %all_to_all.16 = f32[32,4,128]{2,1,0:T(4,128)S(1)} all-to-all(f32[32,4,128]{2,1,0:T(4,128)S(1)} %shard_map.105), channel_id=1, replica_groups={{30,15,28,13,31,14,26,11,29,12,24,9,27,10,22,7,25,8,20,5,23,6,18,3,21,4..., dimensions={0} | all-to-all | bytes 131072 | tf_op jit(solution)/shard_map/all_to_all | solution.py:272
  54.0 0.0 copy-done.4
  54.0 0.0 copy-done.5
  54.0 0.5 shard_map.106
  54.5 10.0 %all_to_all.17 = f32[8,32,128]{2,1,0:T(8,128)S(1)} all-to-all(f32[8,32,128]{2,1,0:T(8,128)S(1)} %shard_map.106), channel_id=1, replica_groups={{224,192,160,128,96,64,32,0},{97,65,33,1,225,193,161,129},{226,194,162,..., dimensions={0} | all-to-all | bytes 262144 | tf_op jit(solution)/shard_map/all_to_all | solution.py:272
  64.5 0.6 reduce_sum.9
  (4 shorter events, 0.0 us)
Async XLA Ops:
  0.0 10.9 %copy-start.8 = (f32[32,128]{1,0:T(8,128)S(1)}, f32[32,128]{1,0:T(8,128)}, u32[]{:S(2)}) copy-start(f32[32,128]{1,0:T(8,128)} %param.12) | copy-start | bytes 49156
  0.0 10.8 %collective-permute-start = (f32[32,128]{1,0:T(8,128)}, f32[32,128]{1,0:T(8,128)S(1)}, u32[]{:S(2)}, u32[]{:S(2)}) collective-permute-start(f32[32,128]{1,0:T(8,128)} %param.12), channel_id=1, source_target_pairs={{0,64},{32,96},{64,0},{96,32},{128,192},{160,224},{192,128},{224,1... | collective-permute-start | bytes 49160 | tf_op jit(solution)/shard_map/ppermute | solution.py:263
  1.5 11.8 %collective-permute-start.2 = (bf16[128,256]{1,0:T(8,128)(2,1)}, bf16[128,256]{1,0:T(8,128)(2,1)S(1)}, u32[]{:S(2)}, u32[]{:S(2)}) collective-permute-start(bf16[128,256]{1,0:T(8,128)(2,1)} %bitcast.8), channel_id=1, source_target_pairs={{1,2},{3,4},{5,6},{7,8},{9,10},{11,12},{13,14},{15,16},{17,18},{19... | collective-permute-start | bytes 196616 | tf_op jit(solution)/shard_map/ppermute | solution.py:268
  8.8 0.8 %copy-start.6 = (bf16[128,256]{1,0:T(8,128)(2,1)S(1)}, bf16[128,256]{1,0:T(8,128)(2,1)}, u32[]{:S(2)}) copy-start(bf16[128,256]{1,0:T(8,128)(2,1)} %grad.1) | copy-start | bytes 196612
  9.7 1.1 %copy-start.7 = (bf16[1,128,256]{2,1,0:T(8,128)(2,1)S(1)}, bf16[1,128,256]{2,1,0:T(8,128)(2,1)}, u32[]{:S(2)}) copy-start(bf16[1,128,256]{2,1,0:T(8,128)(2,1)} %param.10) | copy-start | bytes 196612
  10.8 2.4 %collective-permute-start.3 = (bf16[128,256]{1,0:T(8,128)(2,1)S(1)}, bf16[128,256]{1,0:T(8,128)(2,1)S(1)}, u32[]{:S(2)}, u32[]{:S(2)}) collective-permute-start(bf16[128,256]{1,0:T(8,128)(2,1)S(1)} %bitcast.9), channel_id=1, source_target_pairs={{0,1},{1,0},{2,3},{3,2},{4,5},{5,4},{6,7},{7,6},{8,9},{9,8},{10,11... | collective-permute-start | bytes 196616 | tf_op jit(solution)/shard_map/ppermute | solution.py:276
  10.9 4.2 %collective-permute-start.1 = (f32[2,32,128]{2,1,0:T(8,128)S(1)}, f32[2,32,128]{2,1,0:T(8,128)S(1)}, u32[]{:S(2)}, u32[]{:S(2)}) collective-permute-start(f32[2,32,128]{2,1,0:T(8,128)S(1)} %pad_maximum_fusion.2), channel_id=1, source_target_pairs={{0,32},{32,0},{64,96},{96,64},{128,160},{160,128},{192,224},{224,1... | collective-permute-start | bytes 98312 | tf_op jit(solution)/shard_map/ppermute | solution.py:263
  15.2 5.6 %copy-start = (bf16[1024,512]{1,0:T(8,128)(2,1)S(1)}, bf16[1024,512]{1,0:T(8,128)(2,1)}, u32[]{:S(2)}) copy-start(bf16[1024,512]{1,0:T(8,128)(2,1)} %constant.34.clone.low.g_low) | copy-start | bytes 3145732
  15.2 5.6 %copy-start.1 = (bf16[1024,512]{1,0:T(8,128)(2,1)S(1)}, bf16[1024,512]{1,0:T(8,128)(2,1)}, u32[]{:S(2)}) copy-start(bf16[1024,512]{1,0:T(8,128)(2,1)} %constant.33.clone.high.g_high) | copy-start | bytes 3145732
  15.2 5.6 %collective-permute-start.4 = (f32[4,32,128]{2,1,0:T(8,128)S(1)}, f32[4,32,128]{2,1,0:T(8,128)S(1)}, u32[]{:S(2)}, u32[]{:S(2)}) collective-permute-start(f32[4,32,128]{2,1,0:T(8,128)S(1)} %pad_maximum_fusion.1), channel_id=1, source_target_pairs={{0,192},{32,224},{64,128},{96,160},{128,64},{160,96},{192,0},{224,... | collective-permute-start | bytes 196616 | tf_op jit(solution)/shard_map/ppermute | solution.py:263
  21.5 1.8 %collective-permute-start.5 = (f32[16,24,128]{2,1,0:T(8,128)S(1)}, f32[16,24,128]{2,1,0:T(8,128)S(1)}, u32[]{:S(2)}, u32[]{:S(2)}) collective-permute-start(f32[16,24,128]{2,1,0:T(8,128)S(1)} %get-tuple-element.45), channel_id=1, source_target_pairs={{0,1},{1,0},{2,3},{3,2},{4,5},{5,4},{6,7},{7,6},{8,9},{9,8},{10,11... | collective-permute-start | bytes 589832 | tf_op jit(solution)/shard_map/ppermute | solution.py:276
  21.6 17.6 %copy-start.2 = (bf16[256,2048]{1,0:T(8,128)(2,1)S(1)}, bf16[256,2048]{1,0:T(8,128)(2,1)}, u32[]{:S(2)}) copy-start(bf16[256,2048]{1,0:T(8,128)(2,1)} %constant.36.clone.s_low) | copy-start | bytes 3145732
  21.6 17.6 %copy-start.3 = (bf16[256,2048]{1,0:T(8,128)(2,1)S(1)}, bf16[256,2048]{1,0:T(8,128)(2,1)}, u32[]{:S(2)}) copy-start(bf16[256,2048]{1,0:T(8,128)(2,1)} %constant.35.clone.s_high) | copy-start | bytes 3145732
  39.2 14.8 %copy-start.4 = (bf16[256,2048]{1,0:T(8,128)(2,1)S(1)}, bf16[256,2048]{1,0:T(8,128)(2,1)}, u32[]{:S(2)}) copy-start(bf16[256,2048]{1,0:T(8,128)(2,1)} %constant.38.clone.low) | copy-start | bytes 3145732
  39.2 14.8 %copy-start.5 = (bf16[256,2048]{1,0:T(8,128)(2,1)S(1)}, bf16[256,2048]{1,0:T(8,128)(2,1)}, u32[]{:S(2)}) copy-start(bf16[256,2048]{1,0:T(8,128)(2,1)} %constant.37.clone.high) | copy-start | bytes 3145732

commit v5 on v4

--- a/solution.py
+++ b/solution.py
@@ -14,13 +14,7 @@
 GATHER_MASKS = (0, 2, 1, 3, 6, 4, 7, 5)
 CHIPS = tuple(8 * y + z for z in reversed(range(8)) for y in (1, 0))
 CHIP_ORDERS = (CHIPS, CHIPS[8:] + CHIPS[:8])
-TILE_ORDER = tuple(
-    16 * y + 2 * z + core
-    for _, z, y, core in sorted(
-        ((z + 1.5 * (y ^ core), z, y, core) for z in range(8) for y in (0, 1) for core in (0, 1)),
-        reverse=True,
-    )
-)
+TILE_ORDER = tuple(2 * chip + core for chip in CHIPS for core in (1, 0))
 EVEN, ODD = (0, 2, 4, 6), (1, 3, 5, 7)
 WINDOW = FREQ + GROUP
 defocus_step = 0.5
@@ -227,7 +221,7 @@
         out[TILE_ORDER.index(tile)] = jnp.concatenate(rows_of, axis=1)
 
 
-def phase_kernel(core, payload, field_re, field_im, high, low, out):
+def phase_kernel(payload, field_re, field_im, high, low, out):
     rows = field_re.shape[0]
     gz = payload[...].T
     gz_re = jnp.concatenate([gz[:rows], gz[2 * rows : 3 * rows]], axis=1)
@@ -238,8 +232,7 @@
     phase = field_re[...] * ge_im - field_im[...] * ge_re
     width = out.shape[2]
     for block in range(out.shape[0]):
-        place = (out.shape[0] - 1 - block + 4 * core[0]) & (out.shape[0] - 1)
-        out[place] = phase[:, width * block : width * (block + 1)]
+        out[out.shape[0] - 1 - block] = phase[:, width * block : width * (block + 1)]
 
 
 def call(kernel, outs, scratch, flops, moved, smem=0):
@@ -351,13 +344,9 @@
         [],
         2 * 192 * PUPIL * 2 * FREQ,
         3 * 2**20,
-        smem=1,
-    )(core, payload.reshape(HALF, HALF), field_re, field_im, r_high, r_low)
-    groups = [
-        [(depths - 1 - place + 4 * tile) % depths * 2 * chips + tile for place in range(depths)]
-        for tile in range(2 * chips)
-    ]
-    parts = redistribute(parts, ("depth", "chip", "core"), groups)
+    )(payload.reshape(HALF, HALF), field_re, field_im, r_high, r_low)
+    groups = [list(reversed(range(depths)))]
+    parts = redistribute(parts, "depth", groups)
     return jnp.sum(parts, axis=0)
 
 

time: 65.4 us -> 65 us (level)
  no operation moved by 1% of the time
where the time goes in v5:
time: 65 us; the launch traced here: 64.7 us
  blocking collectives  39.1 us (60%)
  starting transfers between devices  12.8 us (20%)
  Pallas kernels  9.47 us (15%)
  local copies, waits for them, and re-layouts  0.87 us (1%)
  waiting for transfers between devices  0.83 us (1%)
  between operations  0.83 us (1%)
  other arithmetic  0.67 us (1%)
    all_to_all x3, blocking collectives, redistribute(): return lax.all_to_all(x, axis, 0, 0, tiled=True, axis_index_groups=groups)  39.1 us
    pallas_call x7, Pallas kernels, run(): pl.pallas_call(kernel, out_shape=outs, in_specs=[pl.BlockSpec(memory_spac...  9.47 us
    ppermute x1, starting transfers between devices, beside(): return lax.ppermute(x, ('chip', 'core'), pairs + [(j, i) for i, j in pairs])  6.68 us
    ppermute x3, starting transfers between devices, over_depth(): return lax.ppermute(x, 'depth', [(i, i ^ mask) for i in range(count)])  5.97 us
  transfers between devices with their start and end apart: 6, of which 2 were waited for; matrix products, arithmetic and copies ran while one was open for 0% of the time, Pallas kernels for 11%

profile of v5, /device:TPU:16, one launch (start us, length us, event | category | flops | bytes accessed | tf_op | source)
XLA Modules:
  0.0 64.7 jit_solution(3493514492012492832)
XLA Ops:
  0.0 0.0 copy-start.8
  0.0 1.5 %collective-permute-start = (f32[32,128]{1,0:T(8,128)}, f32[32,128]{1,0:T(8,128)S(1)}, u32[]{:S(2)}, u32[]{:S(2)}) collective-permute-start(f32[32,128]{1,0:T(8,128)} %param.12), channel_id=1, source_target_pairs={{0,64},{32,96},{64,0},{96,32},{128,192},{160,224},{192,128},{224,1... | collective-permute-start | bytes 49160 | tf_op jit(solution)/shard_map/ppermute | solution.py:256
  1.5 6.7 %collective-permute-start.2 = (bf16[128,256]{1,0:T(8,128)(2,1)}, bf16[128,256]{1,0:T(8,128)(2,1)S(1)}, u32[]{:S(2)}, u32[]{:S(2)}) collective-permute-start(bf16[128,256]{1,0:T(8,128)(2,1)} %bitcast.8), channel_id=1, source_target_pairs={{1,2},{3,4},{5,6},{7,8},{9,10},{11,12},{13,14},{15,16},{17,18},{19... | collective-permute-start | bytes 196616 | tf_op jit(solution)/shard_map/ppermute | solution.py:261
  8.8 0.0 copy-start.6
  8.9 0.8 %copy-done.6 = bf16[128,256]{1,0:T(8,128)(2,1)S(1)} copy-done((bf16[128,256]{1,0:T(8,128)(2,1)S(1)}, bf16[128,256]{1,0:T(8,128)(2,1)}, u32[]{:S(2)}) %copy-start.6) | copy-done | bytes 65560
  9.7 0.0 copy-start.7
  9.7 1.1 %shard_map.100.shifts = bf16[8,512,256]{2,1,0:T(8,128)(2,1)S(1)} custom-call(bf16[128,256]{1,0:T(8,128)(2,1)S(1)} %copy-done.6), custom_call_target="tpu_custom_call" | custom-call | flops 268435456 | bytes 4194304 | tf_op jit(solution)/shard_map/pallas_call | solution.py:241
  10.8 0.0 collective-permute-done
  10.8 0.0 copy-done.7
  10.8 0.1 collective-permute-start.3
  10.9 0.0 copy-done.8
  10.9 2.3 %collective-permute-start.1 = (f32[2,32,128]{2,1,0:T(8,128)S(1)}, f32[2,32,128]{2,1,0:T(8,128)S(1)}, u32[]{:S(2)}, u32[]{:S(2)}) collective-permute-start(f32[2,32,128]{2,1,0:T(8,128)S(1)} %pad_maximum_fusion.2), channel_id=1, source_target_pairs={{0,32},{32,0},{64,96},{96,64},{128,160},{160,128},{192,224},{224,1... | collective-permute-start | bytes 98312 | tf_op jit(solution)/shard_map/ppermute | solution.py:256
  13.2 0.0 collective-permute-done.2.far
  13.2 0.0 collective-permute-done.3.near
  13.3 1.6 %shard_map.101 = (bf16[272,2048]{1,0:T(8,128)(2,1)S(1)}, f32[256,128]{1,0:T(8,128)S(1)}) custom-call(s32[1]{0:T(128)} %bitcast.core, bf16[128,256]{1,0:T(8,128)(2,1)S(1)} %collective-permute-done.2.far, bf16[128,256]{1,0:T(8,128)(2,1)S(1)} %collective-permute-done.3.near, bf16[128,256]{1,0:T(8,128)(2,1)S(1)} %bitcast.10, ...), custom_call_target="tpu_custom_call" | custom-call | flops 1140850688 | bytes 524288 | tf_op jit(solution)/shard_map/pallas_call | solution.py:241
  14.9 0.3 collective-permute-done.1
  15.2 0.0 copy-start
  15.2 0.0 copy-start.1
  15.2 2.2 %collective-permute-start.4 = (f32[4,32,128]{2,1,0:T(8,128)S(1)}, f32[4,32,128]{2,1,0:T(8,128)S(1)}, u32[]{:S(2)}, u32[]{:S(2)}) collective-permute-start(f32[4,32,128]{2,1,0:T(8,128)S(1)} %pad_maximum_fusion.1), channel_id=1, source_target_pairs={{0,192},{32,224},{64,128},{96,160},{128,64},{160,96},{192,0},{224,... | collective-permute-start | bytes 196616 | tf_op jit(solution)/shard_map/ppermute | solution.py:256
  17.4 2.9 %shard_map.102 = (f32[16,16,128]{2,1,0:T(8,128)S(1)}, f32[256,128]{1,0:T(8,128)S(1)}) custom-call(s32[1]{0:T(128)} %bitcast.core, bf16[272,2048]{1,0:T(8,128)(2,1)S(1)} %get-tuple-element.46.win, bf16[8,512,256]{2,1,0:T(8,128)(2,1)S(1)} %shard_map.100.shifts, f32[256,128]{1,0:T(8,128)S(1)} %get-tuple-element.39.even), custom_call_target="tpu_custom_call" | custom-call | flops 2281701376 | bytes 524288 | tf_op jit(solution)/shard_map/pallas_call | solution.py:241
  20.2 0.5 collective-permute-done.4
  20.8 0.0 copy-done
  20.8 0.0 copy-done.1
  20.8 0.7 %shard_map.103 = (f32[16,8,128]{2,1,0:T(8,128)S(1)}, f32[16,24,128]{2,1,0:T(8,128)S(1)}, f32[32,1024]{1,0:T(8,128)S(1)}, f32[32,1024]{1,0:T(8,128)S(1)}) custom-call(s32[1]{0:T(128)} %bitcast.1.first, s32[1]{0:T(128)} %bitcast.2.depth, s32[1]{0:T(128)} %bitcast.core, s32[1]{0:T(128)S(6)} %copy.11.defocus, f32[8,32,128]{2,1,0:T(8,128)S(1)} %pad_maximum_fusion.phase, ...), custom_call_target="tpu_custom_call" | custom-call | flops 201326592 | bytes 3145728 | tf_op jit(solution)/shard_map/pallas_call | solution.py:241
  21.5 0.1 collective-permute-start.5
  21.6 0.0 copy-start.2
  21.6 0.0 copy-start.3
  21.6 1.7 %shard_map.104 = f32[16,24,128]{2,1,0:T(8,128)S(1)} custom-call(s32[1]{0:T(128)} %bitcast.core, bf16[272,2048]{1,0:T(8,128)(2,1)S(1)} %get-tuple-element.46.win, bf16[8,512,256]{2,1,0:T(8,128)(2,1)S(1)} %shard_map.100.shifts, f32[256,128]{1,0:T(8,128)S(1)} %get-tuple-element.47.kept, f32[16,8,128]{2,1,0:T(8,128)S(1)} %get-tuple-element.48.keep_z), custom_call_target="tpu_custom_call" | custom-call | flops 1140850688 | bytes 524288 | tf_op jit(solution)/shard_map/pallas_call | solution.py:241
  23.3 0.0 collective-permute-done.5
  23.4 15.9 %all_to_all.15.payload = f32[16,24,128]{2,1,0:T(8,128)S(1)} all-to-all(f32[16,24,128]{2,1,0:T(8,128)S(1)} %add.7), channel_id=1, replica_groups={{30,14,28,12,26,10,24,8,22,6,20,4,18,2,16,0},{23,7,21,5,19,3,17,1,31,15..., dimensions={0} | all-to-all | bytes 393216 | tf_op jit(solution)/shard_map/all_to_all | solution.py:265
  39.2 0.0 copy-done.2
  39.2 0.0 copy-done.3
  39.2 0.0 copy-start.4
  39.2 0.0 copy-start.5
  39.3 1.0 %shard_map.105 = f32[32,4,128]{2,1,0:T(4,128)S(1)} custom-call(s32[1]{0:T(128)} %bitcast.core, f32[16,24,128]{2,1,0:T(8,128)S(1)} %all_to_all.15.payload, bf16[1024,512]{1,0:T(8,128)(2,1)S(1)} %copy-done.1, bf16[1024,512]{1,0:T(8,128)(2,1)S(1)} %copy-done, bf16[256,2048]{1,0:T(8,128)(2,1)S(1)} %copy-done.3, bf16[256,2048]{1,0:T(8,128)(2,1)S(1)} %copy-done.2), custom_call_target="tpu_custom_call" | custom-call | flops 100663296 | bytes 5242880 | tf_op jit(solution)/shard_map/pallas_call | solution.py:241
  40.3 13.3 %all_to_all.16 = f32[32,4,128]{2,1,0:T(4,128)S(1)} all-to-all(f32[32,4,128]{2,1,0:T(4,128)S(1)} %shard_map.105), channel_id=1, replica_groups={{31,30,15,14,29,28,13,12,27,26,11,10,25,24,9,8,23,22,7,6,21,20,5,4,19,1..., dimensions={0} | all-to-all | bytes 131072 | tf_op jit(solution)/shard_map/all_to_all | solution.py:265
  53.5 0.0 copy-done.4
  53.5 0.0 copy-done.5
  53.5 0.5 shard_map.106
  54.0 10.0 %all_to_all.17 = f32[8,32,128]{2,1,0:T(8,128)S(1)} all-to-all(f32[8,32,128]{2,1,0:T(8,128)S(1)} %shard_map.106), channel_id=1, replica_groups={{224,192,160,128,96,64,32,0},{225,193,161,129,97,65,33,1},{226,194,162,..., dimensions={0} | all-to-all | bytes 262144 | tf_op jit(solution)/shard_map/all_to_all | solution.py:265
  64.0 0.6 reduce_sum.9
  (4 shorter events, 0.1 us)
Async XLA Ops:
  0.0 10.9 %copy-start.8 = (f32[32,128]{1,0:T(8,128)S(1)}, f32[32,128]{1,0:T(8,128)}, u32[]{:S(2)}) copy-start(f32[32,128]{1,0:T(8,128)} %param.12) | copy-start | bytes 49156
  0.0 10.8 %collective-permute-start = (f32[32,128]{1,0:T(8,128)}, f32[32,128]{1,0:T(8,128)S(1)}, u32[]{:S(2)}, u32[]{:S(2)}) collective-permute-start(f32[32,128]{1,0:T(8,128)} %param.12), channel_id=1, source_target_pairs={{0,64},{32,96},{64,0},{96,32},{128,192},{160,224},{192,128},{224,1... | collective-permute-start | bytes 49160 | tf_op jit(solution)/shard_map/ppermute | solution.py:256
  1.5 11.8 %collective-permute-start.2 = (bf16[128,256]{1,0:T(8,128)(2,1)}, bf16[128,256]{1,0:T(8,128)(2,1)S(1)}, u32[]{:S(2)}, u32[]{:S(2)}) collective-permute-start(bf16[128,256]{1,0:T(8,128)(2,1)} %bitcast.8), channel_id=1, source_target_pairs={{1,2},{3,4},{5,6},{7,8},{9,10},{11,12},{13,14},{15,16},{17,18},{19... | collective-permute-start | bytes 196616 | tf_op jit(solution)/shard_map/ppermute | solution.py:261
  8.8 0.8 %copy-start.6 = (bf16[128,256]{1,0:T(8,128)(2,1)S(1)}, bf16[128,256]{1,0:T(8,128)(2,1)}, u32[]{:S(2)}) copy-start(bf16[128,256]{1,0:T(8,128)(2,1)} %grad.1) | copy-start | bytes 196612
  9.7 1.1 %copy-start.7 = (bf16[1,128,256]{2,1,0:T(8,128)(2,1)S(1)}, bf16[1,128,256]{2,1,0:T(8,128)(2,1)}, u32[]{:S(2)}) copy-start(bf16[1,128,256]{2,1,0:T(8,128)(2,1)} %param.10) | copy-start | bytes 196612
  10.8 2.4 %collective-permute-start.3 = (bf16[128,256]{1,0:T(8,128)(2,1)S(1)}, bf16[128,256]{1,0:T(8,128)(2,1)S(1)}, u32[]{:S(2)}, u32[]{:S(2)}) collective-permute-start(bf16[128,256]{1,0:T(8,128)(2,1)S(1)} %bitcast.9), channel_id=1, source_target_pairs={{0,1},{1,0},{2,3},{3,2},{4,5},{5,4},{6,7},{7,6},{8,9},{9,8},{10,11... | collective-permute-start | bytes 196616 | tf_op jit(solution)/shard_map/ppermute | solution.py:269
  10.9 4.2 %collective-permute-start.1 = (f32[2,32,128]{2,1,0:T(8,128)S(1)}, f32[2,32,128]{2,1,0:T(8,128)S(1)}, u32[]{:S(2)}, u32[]{:S(2)}) collective-permute-start(f32[2,32,128]{2,1,0:T(8,128)S(1)} %pad_maximum_fusion.2), channel_id=1, source_target_pairs={{0,32},{32,0},{64,96},{96,64},{128,160},{160,128},{192,224},{224,1... | collective-permute-start | bytes 98312 | tf_op jit(solution)/shard_map/ppermute | solution.py:256
  15.2 5.6 %copy-start = (bf16[1024,512]{1,0:T(8,128)(2,1)S(1)}, bf16[1024,512]{1,0:T(8,128)(2,1)}, u32[]{:S(2)}) copy-start(bf16[1024,512]{1,0:T(8,128)(2,1)} %constant.34.clone.low.g_low) | copy-start | bytes 3145732
  15.2 5.6 %copy-start.1 = (bf16[1024,512]{1,0:T(8,128)(2,1)S(1)}, bf16[1024,512]{1,0:T(8,128)(2,1)}, u32[]{:S(2)}) copy-start(bf16[1024,512]{1,0:T(8,128)(2,1)} %constant.33.clone.high.g_high) | copy-start | bytes 3145732
  15.2 5.6 %collective-permute-start.4 = (f32[4,32,128]{2,1,0:T(8,128)S(1)}, f32[4,32,128]{2,1,0:T(8,128)S(1)}, u32[]{:S(2)}, u32[]{:S(2)}) collective-permute-start(f32[4,32,128]{2,1,0:T(8,128)S(1)} %pad_maximum_fusion.1), channel_id=1, source_target_pairs={{0,192},{32,224},{64,128},{96,160},{128,64},{160,96},{192,0},{224,... | collective-permute-start | bytes 196616 | tf_op jit(solution)/shard_map/ppermute | solution.py:256
  21.5 1.8 %collective-permute-start.5 = (f32[16,24,128]{2,1,0:T(8,128)S(1)}, f32[16,24,128]{2,1,0:T(8,128)S(1)}, u32[]{:S(2)}, u32[]{:S(2)}) collective-permute-start(f32[16,24,128]{2,1,0:T(8,128)S(1)} %get-tuple-element.45), channel_id=1, source_target_pairs={{0,1},{1,0},{2,3},{3,2},{4,5},{5,4},{6,7},{7,6},{8,9},{9,8},{10,11... | collective-permute-start | bytes 589832 | tf_op jit(solution)/shard_map/ppermute | solution.py:269
  21.6 17.6 %copy-start.2 = (bf16[256,2048]{1,0:T(8,128)(2,1)S(1)}, bf16[256,2048]{1,0:T(8,128)(2,1)}, u32[]{:S(2)}) copy-start(bf16[256,2048]{1,0:T(8,128)(2,1)} %constant.36.clone.s_low) | copy-start | bytes 3145732
  21.6 17.6 %copy-start.3 = (bf16[256,2048]{1,0:T(8,128)(2,1)S(1)}, bf16[256,2048]{1,0:T(8,128)(2,1)}, u32[]{:S(2)}) copy-start(bf16[256,2048]{1,0:T(8,128)(2,1)} %constant.35.clone.s_high) | copy-start | bytes 3145732
  39.2 14.3 %copy-start.4 = (bf16[256,2048]{1,0:T(8,128)(2,1)S(1)}, bf16[256,2048]{1,0:T(8,128)(2,1)}, u32[]{:S(2)}) copy-start(bf16[256,2048]{1,0:T(8,128)(2,1)} %constant.38.clone.low) | copy-start | bytes 3145732
  39.2 14.3 %copy-start.5 = (bf16[256,2048]{1,0:T(8,128)(2,1)S(1)}, bf16[256,2048]{1,0:T(8,128)(2,1)}, u32[]{:S(2)}) copy-start(bf16[256,2048]{1,0:T(8,128)(2,1)} %constant.37.clone.high) | copy-start | bytes 3145732

commit v6 on v5

--- a/solution.py
+++ b/solution.py
@@ -14,7 +14,7 @@
 GATHER_MASKS = (0, 2, 1, 3, 6, 4, 7, 5)
 CHIPS = tuple(8 * y + z for z in reversed(range(8)) for y in (1, 0))
 CHIP_ORDERS = (CHIPS, CHIPS[8:] + CHIPS[:8])
-TILE_ORDER = tuple(2 * chip + core for chip in CHIPS for core in (1, 0))
+TILE_ORDER = tuple(2 * chip + core for chip in CHIPS[:-2] for core in (1, 0)) + (1, 17, 0, 16)
 EVEN, ODD = (0, 2, 4, 6), (1, 3, 5, 7)
 WINDOW = FREQ + GROUP
 defocus_step = 0.5

time: 65 us -> 64.8 us (level)
  no operation moved by 1% of the time
where the time goes in v6:
time: 64.8 us; the launch traced here: 64.5 us
  blocking collectives  39 us (60%)
  starting transfers between devices  12.8 us (20%)
  Pallas kernels  9.47 us (15%)
  local copies, waits for them, and re-layouts  0.87 us (1%)
  waiting for transfers between devices  0.83 us (1%)
  between operations  0.83 us (1%)
  other arithmetic  0.67 us (1%)
    all_to_all x3, blocking collectives, redistribute(): return lax.all_to_all(x, axis, 0, 0, tiled=True, axis_index_groups=groups)  39 us
    pallas_call x7, Pallas kernels, run(): pl.pallas_call(kernel, out_shape=outs, in_specs=[pl.BlockSpec(memory_spac...  9.47 us
    ppermute x1, starting transfers between devices, beside(): return lax.ppermute(x, ('chip', 'core'), pairs + [(j, i) for i, j in pairs])  6.68 us
    ppermute x3, starting transfers between devices, over_depth(): return lax.ppermute(x, 'depth', [(i, i ^ mask) for i in range(count)])  5.97 us
  transfers between devices with their start and end apart: 6, of which 2 were waited for; matrix products, arithmetic and copies ran while one was open for 0% of the time, Pallas kernels for 11%

profile of v6, /device:TPU:16, one launch (start us, length us, event | category | flops | bytes accessed | tf_op | source)
XLA Modules:
  0.0 64.5 jit_solution(3526365471883820050)
XLA Ops:
  0.0 0.0 copy-start.8
  0.0 1.5 %collective-permute-start = (f32[32,128]{1,0:T(8,128)}, f32[32,128]{1,0:T(8,128)S(1)}, u32[]{:S(2)}, u32[]{:S(2)}) collective-permute-start(f32[32,128]{1,0:T(8,128)} %param.12), channel_id=1, source_target_pairs={{0,64},{32,96},{64,0},{96,32},{128,192},{160,224},{192,128},{224,1... | collective-permute-start | bytes 49160 | tf_op jit(solution)/shard_map/ppermute | solution.py:256
  1.5 6.7 %collective-permute-start.2 = (bf16[128,256]{1,0:T(8,128)(2,1)}, bf16[128,256]{1,0:T(8,128)(2,1)S(1)}, u32[]{:S(2)}, u32[]{:S(2)}) collective-permute-start(bf16[128,256]{1,0:T(8,128)(2,1)} %bitcast.8), channel_id=1, source_target_pairs={{1,2},{3,4},{5,6},{7,8},{9,10},{11,12},{13,14},{15,16},{17,18},{19... | collective-permute-start | bytes 196616 | tf_op jit(solution)/shard_map/ppermute | solution.py:261
  8.8 0.0 copy-start.6
  8.9 0.8 %copy-done.6 = bf16[128,256]{1,0:T(8,128)(2,1)S(1)} copy-done((bf16[128,256]{1,0:T(8,128)(2,1)S(1)}, bf16[128,256]{1,0:T(8,128)(2,1)}, u32[]{:S(2)}) %copy-start.6) | copy-done | bytes 65560
  9.7 0.0 copy-start.7
  9.7 1.1 %shard_map.100.shifts = bf16[8,512,256]{2,1,0:T(8,128)(2,1)S(1)} custom-call(bf16[128,256]{1,0:T(8,128)(2,1)S(1)} %copy-done.6), custom_call_target="tpu_custom_call" | custom-call | flops 268435456 | bytes 4194304 | tf_op jit(solution)/shard_map/pallas_call | solution.py:241
  10.8 0.0 collective-permute-done
  10.8 0.0 copy-done.7
  10.8 0.1 collective-permute-start.3
  10.9 0.0 copy-done.8
  10.9 2.3 %collective-permute-start.1 = (f32[2,32,128]{2,1,0:T(8,128)S(1)}, f32[2,32,128]{2,1,0:T(8,128)S(1)}, u32[]{:S(2)}, u32[]{:S(2)}) collective-permute-start(f32[2,32,128]{2,1,0:T(8,128)S(1)} %pad_maximum_fusion.2), channel_id=1, source_target_pairs={{0,32},{32,0},{64,96},{96,64},{128,160},{160,128},{192,224},{224,1... | collective-permute-start | bytes 98312 | tf_op jit(solution)/shard_map/ppermute | solution.py:256
  13.2 0.0 collective-permute-done.2.far
  13.2 0.0 collective-permute-done.3.near
  13.3 1.6 %shard_map.101 = (bf16[272,2048]{1,0:T(8,128)(2,1)S(1)}, f32[256,128]{1,0:T(8,128)S(1)}) custom-call(s32[1]{0:T(128)} %bitcast.core, bf16[128,256]{1,0:T(8,128)(2,1)S(1)} %collective-permute-done.2.far, bf16[128,256]{1,0:T(8,128)(2,1)S(1)} %collective-permute-done.3.near, bf16[128,256]{1,0:T(8,128)(2,1)S(1)} %bitcast.10, ...), custom_call_target="tpu_custom_call" | custom-call | flops 1140850688 | bytes 524288 | tf_op jit(solution)/shard_map/pallas_call | solution.py:241
  14.9 0.3 collective-permute-done.1
  15.2 0.0 copy-start
  15.2 0.0 copy-start.1
  15.2 2.2 %collective-permute-start.4 = (f32[4,32,128]{2,1,0:T(8,128)S(1)}, f32[4,32,128]{2,1,0:T(8,128)S(1)}, u32[]{:S(2)}, u32[]{:S(2)}) collective-permute-start(f32[4,32,128]{2,1,0:T(8,128)S(1)} %pad_maximum_fusion.1), channel_id=1, source_target_pairs={{0,192},{32,224},{64,128},{96,160},{128,64},{160,96},{192,0},{224,... | collective-permute-start | bytes 196616 | tf_op jit(solution)/shard_map/ppermute | solution.py:256
  17.4 2.9 %shard_map.102 = (f32[16,16,128]{2,1,0:T(8,128)S(1)}, f32[256,128]{1,0:T(8,128)S(1)}) custom-call(s32[1]{0:T(128)} %bitcast.core, bf16[272,2048]{1,0:T(8,128)(2,1)S(1)} %get-tuple-element.46.win, bf16[8,512,256]{2,1,0:T(8,128)(2,1)S(1)} %shard_map.100.shifts, f32[256,128]{1,0:T(8,128)S(1)} %get-tuple-element.39.even), custom_call_target="tpu_custom_call" | custom-call | flops 2281701376 | bytes 524288 | tf_op jit(solution)/shard_map/pallas_call | solution.py:241
  20.2 0.5 collective-permute-done.4
  20.8 0.0 copy-done
  20.8 0.0 copy-done.1
  20.8 0.7 %shard_map.103 = (f32[16,8,128]{2,1,0:T(8,128)S(1)}, f32[16,24,128]{2,1,0:T(8,128)S(1)}, f32[32,1024]{1,0:T(8,128)S(1)}, f32[32,1024]{1,0:T(8,128)S(1)}) custom-call(s32[1]{0:T(128)} %bitcast.1.first, s32[1]{0:T(128)} %bitcast.2.depth, s32[1]{0:T(128)} %bitcast.core, s32[1]{0:T(128)S(6)} %copy.11.defocus, f32[8,32,128]{2,1,0:T(8,128)S(1)} %pad_maximum_fusion.phase, ...), custom_call_target="tpu_custom_call" | custom-call | flops 201326592 | bytes 3145728 | tf_op jit(solution)/shard_map/pallas_call | solution.py:241
  21.5 0.1 collective-permute-start.5
  21.6 0.0 copy-start.2
  21.6 0.0 copy-start.3
  21.6 1.7 %shard_map.104 = f32[16,24,128]{2,1,0:T(8,128)S(1)} custom-call(s32[1]{0:T(128)} %bitcast.core, bf16[272,2048]{1,0:T(8,128)(2,1)S(1)} %get-tuple-element.46.win, bf16[8,512,256]{2,1,0:T(8,128)(2,1)S(1)} %shard_map.100.shifts, f32[256,128]{1,0:T(8,128)S(1)} %get-tuple-element.47.kept, f32[16,8,128]{2,1,0:T(8,128)S(1)} %get-tuple-element.48.keep_z), custom_call_target="tpu_custom_call" | custom-call | flops 1140850688 | bytes 524288 | tf_op jit(solution)/shard_map/pallas_call | solution.py:241
  23.3 0.0 collective-permute-done.5
  23.4 15.9 %all_to_all.15.payload = f32[16,24,128]{2,1,0:T(8,128)S(1)} all-to-all(f32[16,24,128]{2,1,0:T(8,128)S(1)} %add.7), channel_id=1, replica_groups={{30,14,28,12,26,10,24,8,22,6,20,4,18,2,16,0},{23,7,21,5,19,3,17,1,31,15..., dimensions={0} | all-to-all | bytes 393216 | tf_op jit(solution)/shard_map/all_to_all | solution.py:265
  39.2 0.0 copy-done.2
  39.2 0.0 copy-done.3
  39.2 0.0 copy-start.4
  39.2 0.0 copy-start.5
  39.3 1.0 %shard_map.105 = f32[32,4,128]{2,1,0:T(4,128)S(1)} custom-call(s32[1]{0:T(128)} %bitcast.core, f32[16,24,128]{2,1,0:T(8,128)S(1)} %all_to_all.15.payload, bf16[1024,512]{1,0:T(8,128)(2,1)S(1)} %copy-done.1, bf16[1024,512]{1,0:T(8,128)(2,1)S(1)} %copy-done, bf16[256,2048]{1,0:T(8,128)(2,1)S(1)} %copy-done.3, bf16[256,2048]{1,0:T(8,128)(2,1)S(1)} %copy-done.2), custom_call_target="tpu_custom_call" | custom-call | flops 100663296 | bytes 5242880 | tf_op jit(solution)/shard_map/pallas_call | solution.py:241
  40.3 13.2 %all_to_all.16 = f32[32,4,128]{2,1,0:T(4,128)S(1)} all-to-all(f32[32,4,128]{2,1,0:T(4,128)S(1)} %shard_map.105), channel_id=1, replica_groups={{31,30,15,14,29,28,13,12,27,26,11,10,25,24,9,8,23,22,7,6,21,20,5,4,19,1..., dimensions={0} | all-to-all | bytes 131072 | tf_op jit(solution)/shard_map/all_to_all | solution.py:265
  53.4 0.0 copy-done.4
  53.4 0.0 copy-done.5
  53.4 0.5 shard_map.106
  53.9 10.0 %all_to_all.17 = f32[8,32,128]{2,1,0:T(8,128)S(1)} all-to-all(f32[8,32,128]{2,1,0:T(8,128)S(1)} %shard_map.106), channel_id=1, replica_groups={{224,192,160,128,96,64,32,0},{225,193,161,129,97,65,33,1},{226,194,162,..., dimensions={0} | all-to-all | bytes 262144 | tf_op jit(solution)/shard_map/all_to_all | solution.py:265
  63.9 0.6 reduce_sum.9
  (4 shorter events, 0.1 us)
Async XLA Ops:
  0.0 10.9 %copy-start.8 = (f32[32,128]{1,0:T(8,128)S(1)}, f32[32,128]{1,0:T(8,128)}, u32[]{:S(2)}) copy-start(f32[32,128]{1,0:T(8,128)} %param.12) | copy-start | bytes 49156
  0.0 10.8 %collective-permute-start = (f32[32,128]{1,0:T(8,128)}, f32[32,128]{1,0:T(8,128)S(1)}, u32[]{:S(2)}, u32[]{:S(2)}) collective-permute-start(f32[32,128]{1,0:T(8,128)} %param.12), channel_id=1, source_target_pairs={{0,64},{32,96},{64,0},{96,32},{128,192},{160,224},{192,128},{224,1... | collective-permute-start | bytes 49160 | tf_op jit(solution)/shard_map/ppermute | solution.py:256
  1.5 11.8 %collective-permute-start.2 = (bf16[128,256]{1,0:T(8,128)(2,1)}, bf16[128,256]{1,0:T(8,128)(2,1)S(1)}, u32[]{:S(2)}, u32[]{:S(2)}) collective-permute-start(bf16[128,256]{1,0:T(8,128)(2,1)} %bitcast.8), channel_id=1, source_target_pairs={{1,2},{3,4},{5,6},{7,8},{9,10},{11,12},{13,14},{15,16},{17,18},{19... | collective-permute-start | bytes 196616 | tf_op jit(solution)/shard_map/ppermute | solution.py:261
  8.8 0.8 %copy-start.6 = (bf16[128,256]{1,0:T(8,128)(2,1)S(1)}, bf16[128,256]{1,0:T(8,128)(2,1)}, u32[]{:S(2)}) copy-start(bf16[128,256]{1,0:T(8,128)(2,1)} %grad.1) | copy-start | bytes 196612
  9.7 1.1 %copy-start.7 = (bf16[1,128,256]{2,1,0:T(8,128)(2,1)S(1)}, bf16[1,128,256]{2,1,0:T(8,128)(2,1)}, u32[]{:S(2)}) copy-start(bf16[1,128,256]{2,1,0:T(8,128)(2,1)} %param.10) | copy-start | bytes 196612
  10.8 2.4 %collective-permute-start.3 = (bf16[128,256]{1,0:T(8,128)(2,1)S(1)}, bf16[128,256]{1,0:T(8,128)(2,1)S(1)}, u32[]{:S(2)}, u32[]{:S(2)}) collective-permute-start(bf16[128,256]{1,0:T(8,128)(2,1)S(1)} %bitcast.9), channel_id=1, source_target_pairs={{0,1},{1,0},{2,3},{3,2},{4,5},{5,4},{6,7},{7,6},{8,9},{9,8},{10,11... | collective-permute-start | bytes 196616 | tf_op jit(solution)/shard_map/ppermute | solution.py:269
  10.9 4.2 %collective-permute-start.1 = (f32[2,32,128]{2,1,0:T(8,128)S(1)}, f32[2,32,128]{2,1,0:T(8,128)S(1)}, u32[]{:S(2)}, u32[]{:S(2)}) collective-permute-start(f32[2,32,128]{2,1,0:T(8,128)S(1)} %pad_maximum_fusion.2), channel_id=1, source_target_pairs={{0,32},{32,0},{64,96},{96,64},{128,160},{160,128},{192,224},{224,1... | collective-permute-start | bytes 98312 | tf_op jit(solution)/shard_map/ppermute | solution.py:256
  15.2 5.6 %copy-start = (bf16[1024,512]{1,0:T(8,128)(2,1)S(1)}, bf16[1024,512]{1,0:T(8,128)(2,1)}, u32[]{:S(2)}) copy-start(bf16[1024,512]{1,0:T(8,128)(2,1)} %constant.34.clone.low.g_low) | copy-start | bytes 3145732
  15.2 5.6 %copy-start.1 = (bf16[1024,512]{1,0:T(8,128)(2,1)S(1)}, bf16[1024,512]{1,0:T(8,128)(2,1)}, u32[]{:S(2)}) copy-start(bf16[1024,512]{1,0:T(8,128)(2,1)} %constant.33.clone.high.g_high) | copy-start | bytes 3145732
  15.2 5.6 %collective-permute-start.4 = (f32[4,32,128]{2,1,0:T(8,128)S(1)}, f32[4,32,128]{2,1,0:T(8,128)S(1)}, u32[]{:S(2)}, u32[]{:S(2)}) collective-permute-start(f32[4,32,128]{2,1,0:T(8,128)S(1)} %pad_maximum_fusion.1), channel_id=1, source_target_pairs={{0,192},{32,224},{64,128},{96,160},{128,64},{160,96},{192,0},{224,... | collective-permute-start | bytes 196616 | tf_op jit(solution)/shard_map/ppermute | solution.py:256
  21.5 1.8 %collective-permute-start.5 = (f32[16,24,128]{2,1,0:T(8,128)S(1)}, f32[16,24,128]{2,1,0:T(8,128)S(1)}, u32[]{:S(2)}, u32[]{:S(2)}) collective-permute-start(f32[16,24,128]{2,1,0:T(8,128)S(1)} %get-tuple-element.45), channel_id=1, source_target_pairs={{0,1},{1,0},{2,3},{3,2},{4,5},{5,4},{6,7},{7,6},{8,9},{9,8},{10,11... | collective-permute-start | bytes 589832 | tf_op jit(solution)/shard_map/ppermute | solution.py:269
  21.6 17.6 %copy-start.2 = (bf16[256,2048]{1,0:T(8,128)(2,1)S(1)}, bf16[256,2048]{1,0:T(8,128)(2,1)}, u32[]{:S(2)}) copy-start(bf16[256,2048]{1,0:T(8,128)(2,1)} %constant.36.clone.s_low) | copy-start | bytes 3145732
  21.6 17.6 %copy-start.3 = (bf16[256,2048]{1,0:T(8,128)(2,1)S(1)}, bf16[256,2048]{1,0:T(8,128)(2,1)}, u32[]{:S(2)}) copy-start(bf16[256,2048]{1,0:T(8,128)(2,1)} %constant.35.clone.s_high) | copy-start | bytes 3145732
  39.2 14.2 %copy-start.4 = (bf16[256,2048]{1,0:T(8,128)(2,1)S(1)}, bf16[256,2048]{1,0:T(8,128)(2,1)}, u32[]{:S(2)}) copy-start(bf16[256,2048]{1,0:T(8,128)(2,1)} %constant.38.clone.low) | copy-start | bytes 3145732
  39.2 14.2 %copy-start.5 = (bf16[256,2048]{1,0:T(8,128)(2,1)S(1)}, bf16[256,2048]{1,0:T(8,128)(2,1)}, u32[]{:S(2)}) copy-start(bf16[256,2048]{1,0:T(8,128)(2,1)} %constant.37.clone.high) | copy-start | bytes 3145732

commit v7 on v5

--- a/solution.py
+++ b/solution.py
@@ -13,7 +13,8 @@
 GROUP = 16
 GATHER_MASKS = (0, 2, 1, 3, 6, 4, 7, 5)
 CHIPS = tuple(8 * y + z for z in reversed(range(8)) for y in (1, 0))
-CHIP_ORDERS = (CHIPS, CHIPS[8:] + CHIPS[:8])
+FLIPPED = tuple(chip ^ 8 for chip in CHIPS)
+CHIP_ORDERS = (FLIPPED, FLIPPED[8:] + FLIPPED[:8])
 TILE_ORDER = tuple(2 * chip + core for chip in CHIPS for core in (1, 0))
 EVEN, ODD = (0, 2, 4, 6), (1, 3, 5, 7)
 WINDOW = FREQ + GROUP

time: 65 us -> 66.5 us (1.023)
  blocking collectives: 39.1 us -> 40.7 us
    all_to_all x3, blocking collectives: 39.1 us -> 40.7 us  [redistribute(): return lax.all_to_all(x, axis, 0, 0, tiled=True, axis_index_groups=groups)]
where the time goes in v7:
time: 66.5 us; the launch traced here: 66.2 us
  blocking collectives  40.7 us (61%)
  starting transfers between devices  12.8 us (19%)
  Pallas kernels  9.48 us (14%)
  local copies, waits for them, and re-layouts  0.87 us (1%)
  waiting for transfers between devices  0.83 us (1%)
  between operations  0.83 us (1%)
  other arithmetic  0.67 us (1%)
    all_to_all x3, blocking collectives, redistribute(): return lax.all_to_all(x, axis, 0, 0, tiled=True, axis_index_groups=groups)  40.7 us
    pallas_call x7, Pallas kernels, run(): pl.pallas_call(kernel, out_shape=outs, in_specs=[pl.BlockSpec(memory_spac...  9.48 us
    ppermute x1, starting transfers between devices, beside(): return lax.ppermute(x, ('chip', 'core'), pairs + [(j, i) for i, j in pairs])  6.68 us
    ppermute x3, starting transfers between devices, over_depth(): return lax.ppermute(x, 'depth', [(i, i ^ mask) for i in range(count)])  5.97 us
  transfers between devices with their start and end apart: 6, of which 2 were waited for; matrix products, arithmetic and copies ran while one was open for 0% of the time, Pallas kernels for 11%

profile of v7, /device:TPU:16, one launch (start us, length us, event | category | flops | bytes accessed | tf_op | source)
XLA Modules:
  0.0 66.2 jit_solution(16217756432460702015)
XLA Ops:
  0.0 0.0 copy-start.8
  0.0 1.5 %collective-permute-start = (f32[32,128]{1,0:T(8,128)}, f32[32,128]{1,0:T(8,128)S(1)}, u32[]{:S(2)}, u32[]{:S(2)}) collective-permute-start(f32[32,128]{1,0:T(8,128)} %param.12), channel_id=1, source_target_pairs={{0,64},{32,96},{64,0},{96,32},{128,192},{160,224},{192,128},{224,1... | collective-permute-start | bytes 49160 | tf_op jit(solution)/shard_map/ppermute | solution.py:257
  1.5 6.7 %collective-permute-start.2 = (bf16[128,256]{1,0:T(8,128)(2,1)}, bf16[128,256]{1,0:T(8,128)(2,1)S(1)}, u32[]{:S(2)}, u32[]{:S(2)}) collective-permute-start(bf16[128,256]{1,0:T(8,128)(2,1)} %bitcast.8), channel_id=1, source_target_pairs={{1,2},{3,4},{5,6},{7,8},{9,10},{11,12},{13,14},{15,16},{17,18},{19... | collective-permute-start | bytes 196616 | tf_op jit(solution)/shard_map/ppermute | solution.py:262
  8.8 0.0 copy-start.6
  8.9 0.8 %copy-done.6 = bf16[128,256]{1,0:T(8,128)(2,1)S(1)} copy-done((bf16[128,256]{1,0:T(8,128)(2,1)S(1)}, bf16[128,256]{1,0:T(8,128)(2,1)}, u32[]{:S(2)}) %copy-start.6) | copy-done | bytes 65560
  9.7 0.0 copy-start.7
  9.7 1.1 %shard_map.100.shifts = bf16[8,512,256]{2,1,0:T(8,128)(2,1)S(1)} custom-call(bf16[128,256]{1,0:T(8,128)(2,1)S(1)} %copy-done.6), custom_call_target="tpu_custom_call" | custom-call | flops 268435456 | bytes 4194304 | tf_op jit(solution)/shard_map/pallas_call | solution.py:242
  10.8 0.0 collective-permute-done
  10.8 0.0 copy-done.7
  10.8 0.1 collective-permute-start.3
  10.9 0.0 copy-done.8
  10.9 2.3 %collective-permute-start.1 = (f32[2,32,128]{2,1,0:T(8,128)S(1)}, f32[2,32,128]{2,1,0:T(8,128)S(1)}, u32[]{:S(2)}, u32[]{:S(2)}) collective-permute-start(f32[2,32,128]{2,1,0:T(8,128)S(1)} %pad_maximum_fusion.2), channel_id=1, source_target_pairs={{0,32},{32,0},{64,96},{96,64},{128,160},{160,128},{192,224},{224,1... | collective-permute-start | bytes 98312 | tf_op jit(solution)/shard_map/ppermute | solution.py:257
  13.2 0.0 collective-permute-done.2.far
  13.2 0.0 collective-permute-done.3.near
  13.3 1.6 %shard_map.101 = (bf16[272,2048]{1,0:T(8,128)(2,1)S(1)}, f32[256,128]{1,0:T(8,128)S(1)}) custom-call(s32[1]{0:T(128)} %bitcast.core, bf16[128,256]{1,0:T(8,128)(2,1)S(1)} %collective-permute-done.2.far, bf16[128,256]{1,0:T(8,128)(2,1)S(1)} %collective-permute-done.3.near, bf16[128,256]{1,0:T(8,128)(2,1)S(1)} %bitcast.10, ...), custom_call_target="tpu_custom_call" | custom-call | flops 1140850688 | bytes 524288 | tf_op jit(solution)/shard_map/pallas_call | solution.py:242
  14.9 0.3 collective-permute-done.1
  15.2 0.0 copy-start
  15.2 0.0 copy-start.1
  15.2 2.2 %collective-permute-start.4 = (f32[4,32,128]{2,1,0:T(8,128)S(1)}, f32[4,32,128]{2,1,0:T(8,128)S(1)}, u32[]{:S(2)}, u32[]{:S(2)}) collective-permute-start(f32[4,32,128]{2,1,0:T(8,128)S(1)} %pad_maximum_fusion.1), channel_id=1, source_target_pairs={{0,192},{32,224},{64,128},{96,160},{128,64},{160,96},{192,0},{224,... | collective-permute-start | bytes 196616 | tf_op jit(solution)/shard_map/ppermute | solution.py:257
  17.4 2.9 %shard_map.102 = (f32[16,16,128]{2,1,0:T(8,128)S(1)}, f32[256,128]{1,0:T(8,128)S(1)}) custom-call(s32[1]{0:T(128)} %bitcast.core, bf16[272,2048]{1,0:T(8,128)(2,1)S(1)} %get-tuple-element.46.win, bf16[8,512,256]{2,1,0:T(8,128)(2,1)S(1)} %shard_map.100.shifts, f32[256,128]{1,0:T(8,128)S(1)} %get-tuple-element.39.even), custom_call_target="tpu_custom_call" | custom-call | flops 2281701376 | bytes 524288 | tf_op jit(solution)/shard_map/pallas_call | solution.py:242
  20.2 0.5 collective-permute-done.4
  20.8 0.0 copy-done
  20.8 0.0 copy-done.1
  20.8 0.7 %shard_map.103 = (f32[16,8,128]{2,1,0:T(8,128)S(1)}, f32[16,24,128]{2,1,0:T(8,128)S(1)}, f32[32,1024]{1,0:T(8,128)S(1)}, f32[32,1024]{1,0:T(8,128)S(1)}) custom-call(s32[1]{0:T(128)} %bitcast.1.first, s32[1]{0:T(128)} %bitcast.2.depth, s32[1]{0:T(128)} %bitcast.core, s32[1]{0:T(128)S(6)} %copy.11.defocus, f32[8,32,128]{2,1,0:T(8,128)S(1)} %pad_maximum_fusion.phase, ...), custom_call_target="tpu_custom_call" | custom-call | flops 201326592 | bytes 3145728 | tf_op jit(solution)/shard_map/pallas_call | solution.py:242
  21.5 0.1 collective-permute-start.5
  21.6 0.0 copy-start.2
  21.6 0.0 copy-start.3
  21.6 1.7 %shard_map.104 = f32[16,24,128]{2,1,0:T(8,128)S(1)} custom-call(s32[1]{0:T(128)} %bitcast.core, bf16[272,2048]{1,0:T(8,128)(2,1)S(1)} %get-tuple-element.46.win, bf16[8,512,256]{2,1,0:T(8,128)(2,1)S(1)} %shard_map.100.shifts, f32[256,128]{1,0:T(8,128)S(1)} %get-tuple-element.47.kept, f32[16,8,128]{2,1,0:T(8,128)S(1)} %get-tuple-element.48.keep_z), custom_call_target="tpu_custom_call" | custom-call | flops 1140850688 | bytes 524288 | tf_op jit(solution)/shard_map/pallas_call | solution.py:242
  23.3 0.0 collective-permute-done.5
  23.4 15.8 %all_to_all.15.payload = f32[16,24,128]{2,1,0:T(8,128)S(1)} all-to-all(f32[16,24,128]{2,1,0:T(8,128)S(1)} %add.7), channel_id=1, replica_groups={{14,30,12,28,10,26,8,24,6,22,4,20,2,18,0,16},{7,23,5,21,3,19,1,17,15,31..., dimensions={0} | all-to-all | bytes 393216 | tf_op jit(solution)/shard_map/all_to_all | solution.py:266
  39.2 0.0 copy-done.2
  39.2 0.0 copy-done.3
  39.2 0.0 copy-start.4
  39.2 0.0 copy-start.5
  39.2 1.0 %shard_map.105 = f32[32,4,128]{2,1,0:T(4,128)S(1)} custom-call(s32[1]{0:T(128)} %bitcast.core, f32[16,24,128]{2,1,0:T(8,128)S(1)} %all_to_all.15.payload, bf16[1024,512]{1,0:T(8,128)(2,1)S(1)} %copy-done.1, bf16[1024,512]{1,0:T(8,128)(2,1)S(1)} %copy-done, bf16[256,2048]{1,0:T(8,128)(2,1)S(1)} %copy-done.3, bf16[256,2048]{1,0:T(8,128)(2,1)S(1)} %copy-done.2), custom_call_target="tpu_custom_call" | custom-call | flops 100663296 | bytes 5242880 | tf_op jit(solution)/shard_map/pallas_call | solution.py:242
  40.2 15.7 %all_to_all.16 = f32[32,4,128]{2,1,0:T(4,128)S(1)} all-to-all(f32[32,4,128]{2,1,0:T(4,128)S(1)} %shard_map.105), channel_id=1, replica_groups={{31,30,15,14,29,28,13,12,27,26,11,10,25,24,9,8,23,22,7,6,21,20,5,4,19,1..., dimensions={0} | all-to-all | bytes 131072 | tf_op jit(solution)/shard_map/all_to_all | solution.py:266
  55.9 0.0 copy-done.4
  55.9 0.0 copy-done.5
  55.9 0.5 shard_map.106
  56.5 9.1 %all_to_all.17 = f32[8,32,128]{2,1,0:T(8,128)S(1)} all-to-all(f32[8,32,128]{2,1,0:T(8,128)S(1)} %shard_map.106), channel_id=1, replica_groups={{224,192,160,128,96,64,32,0},{225,193,161,129,97,65,33,1},{226,194,162,..., dimensions={0} | all-to-all | bytes 262144 | tf_op jit(solution)/shard_map/all_to_all | solution.py:266
  65.6 0.6 reduce_sum.9
  (4 shorter events, 0.1 us)
Async XLA Ops:
  0.0 10.9 %copy-start.8 = (f32[32,128]{1,0:T(8,128)S(1)}, f32[32,128]{1,0:T(8,128)}, u32[]{:S(2)}) copy-start(f32[32,128]{1,0:T(8,128)} %param.12) | copy-start | bytes 49156
  0.0 10.8 %collective-permute-start = (f32[32,128]{1,0:T(8,128)}, f32[32,128]{1,0:T(8,128)S(1)}, u32[]{:S(2)}, u32[]{:S(2)}) collective-permute-start(f32[32,128]{1,0:T(8,128)} %param.12), channel_id=1, source_target_pairs={{0,64},{32,96},{64,0},{96,32},{128,192},{160,224},{192,128},{224,1... | collective-permute-start | bytes 49160 | tf_op jit(solution)/shard_map/ppermute | solution.py:257
  1.5 11.8 %collective-permute-start.2 = (bf16[128,256]{1,0:T(8,128)(2,1)}, bf16[128,256]{1,0:T(8,128)(2,1)S(1)}, u32[]{:S(2)}, u32[]{:S(2)}) collective-permute-start(bf16[128,256]{1,0:T(8,128)(2,1)} %bitcast.8), channel_id=1, source_target_pairs={{1,2},{3,4},{5,6},{7,8},{9,10},{11,12},{13,14},{15,16},{17,18},{19... | collective-permute-start | bytes 196616 | tf_op jit(solution)/shard_map/ppermute | solution.py:262
  8.8 0.8 %copy-start.6 = (bf16[128,256]{1,0:T(8,128)(2,1)S(1)}, bf16[128,256]{1,0:T(8,128)(2,1)}, u32[]{:S(2)}) copy-start(bf16[128,256]{1,0:T(8,128)(2,1)} %grad.1) | copy-start | bytes 196612
  9.7 1.1 %copy-start.7 = (bf16[1,128,256]{2,1,0:T(8,128)(2,1)S(1)}, bf16[1,128,256]{2,1,0:T(8,128)(2,1)}, u32[]{:S(2)}) copy-start(bf16[1,128,256]{2,1,0:T(8,128)(2,1)} %param.10) | copy-start | bytes 196612
  10.8 2.4 %collective-permute-start.3 = (bf16[128,256]{1,0:T(8,128)(2,1)S(1)}, bf16[128,256]{1,0:T(8,128)(2,1)S(1)}, u32[]{:S(2)}, u32[]{:S(2)}) collective-permute-start(bf16[128,256]{1,0:T(8,128)(2,1)S(1)} %bitcast.9), channel_id=1, source_target_pairs={{0,1},{1,0},{2,3},{3,2},{4,5},{5,4},{6,7},{7,6},{8,9},{9,8},{10,11... | collective-permute-start | bytes 196616 | tf_op jit(solution)/shard_map/ppermute | solution.py:270
  10.9 4.2 %collective-permute-start.1 = (f32[2,32,128]{2,1,0:T(8,128)S(1)}, f32[2,32,128]{2,1,0:T(8,128)S(1)}, u32[]{:S(2)}, u32[]{:S(2)}) collective-permute-start(f32[2,32,128]{2,1,0:T(8,128)S(1)} %pad_maximum_fusion.2), channel_id=1, source_target_pairs={{0,32},{32,0},{64,96},{96,64},{128,160},{160,128},{192,224},{224,1... | collective-permute-start | bytes 98312 | tf_op jit(solution)/shard_map/ppermute | solution.py:257
  15.2 5.6 %copy-start = (bf16[1024,512]{1,0:T(8,128)(2,1)S(1)}, bf16[1024,512]{1,0:T(8,128)(2,1)}, u32[]{:S(2)}) copy-start(bf16[1024,512]{1,0:T(8,128)(2,1)} %constant.34.clone.low.g_low) | copy-start | bytes 3145732
  15.2 5.6 %copy-start.1 = (bf16[1024,512]{1,0:T(8,128)(2,1)S(1)}, bf16[1024,512]{1,0:T(8,128)(2,1)}, u32[]{:S(2)}) copy-start(bf16[1024,512]{1,0:T(8,128)(2,1)} %constant.33.clone.high.g_high) | copy-start | bytes 3145732
  15.2 5.6 %collective-permute-start.4 = (f32[4,32,128]{2,1,0:T(8,128)S(1)}, f32[4,32,128]{2,1,0:T(8,128)S(1)}, u32[]{:S(2)}, u32[]{:S(2)}) collective-permute-start(f32[4,32,128]{2,1,0:T(8,128)S(1)} %pad_maximum_fusion.1), channel_id=1, source_target_pairs={{0,192},{32,224},{64,128},{96,160},{128,64},{160,96},{192,0},{224,... | collective-permute-start | bytes 196616 | tf_op jit(solution)/shard_map/ppermute | solution.py:257
  21.5 1.8 %collective-permute-start.5 = (f32[16,24,128]{2,1,0:T(8,128)S(1)}, f32[16,24,128]{2,1,0:T(8,128)S(1)}, u32[]{:S(2)}, u32[]{:S(2)}) collective-permute-start(f32[16,24,128]{2,1,0:T(8,128)S(1)} %get-tuple-element.45), channel_id=1, source_target_pairs={{0,1},{1,0},{2,3},{3,2},{4,5},{5,4},{6,7},{7,6},{8,9},{9,8},{10,11... | collective-permute-start | bytes 589832 | tf_op jit(solution)/shard_map/ppermute | solution.py:270
  21.6 17.6 %copy-start.2 = (bf16[256,2048]{1,0:T(8,128)(2,1)S(1)}, bf16[256,2048]{1,0:T(8,128)(2,1)}, u32[]{:S(2)}) copy-start(bf16[256,2048]{1,0:T(8,128)(2,1)} %constant.36.clone.s_low) | copy-start | bytes 3145732
  21.6 17.6 %copy-start.3 = (bf16[256,2048]{1,0:T(8,128)(2,1)S(1)}, bf16[256,2048]{1,0:T(8,128)(2,1)}, u32[]{:S(2)}) copy-start(bf16[256,2048]{1,0:T(8,128)(2,1)} %constant.35.clone.s_high) | copy-start | bytes 3145732
  39.2 16.7 %copy-start.4 = (bf16[256,2048]{1,0:T(8,128)(2,1)S(1)}, bf16[256,2048]{1,0:T(8,128)(2,1)}, u32[]{:S(2)}) copy-start(bf16[256,2048]{1,0:T(8,128)(2,1)} %constant.38.clone.low) | copy-start | bytes 3145732
  39.2 16.7 %copy-start.5 = (bf16[256,2048]{1,0:T(8,128)(2,1)S(1)}, bf16[256,2048]{1,0:T(8,128)(2,1)}, u32[]{:S(2)}) copy-start(bf16[256,2048]{1,0:T(8,128)(2,1)} %constant.37.clone.high) | copy-start | bytes 3145732

commit v8 on v5

--- a/solution.py
+++ b/solution.py
@@ -13,7 +13,8 @@
 GROUP = 16
 GATHER_MASKS = (0, 2, 1, 3, 6, 4, 7, 5)
 CHIPS = tuple(8 * y + z for z in reversed(range(8)) for y in (1, 0))
-CHIP_ORDERS = (CHIPS, CHIPS[8:] + CHIPS[:8])
+BY_HALF = tuple(reversed(range(16)))
+CHIP_ORDERS = (BY_HALF, BY_HALF[8:] + BY_HALF[:8])
 TILE_ORDER = tuple(2 * chip + core for chip in CHIPS for core in (1, 0))
 EVEN, ODD = (0, 2, 4, 6), (1, 3, 5, 7)
 WINDOW = FREQ + GROUP

time: 65 us -> 65 us (level)
  no operation moved by 1% of the time
where the time goes in v8:
time: 65 us; the launch traced here: 64.7 us
  blocking collectives  39.2 us (60%)
  starting transfers between devices  12.8 us (20%)
  Pallas kernels  9.48 us (15%)
  local copies, waits for them, and re-layouts  0.87 us (1%)
  waiting for transfers between devices  0.83 us (1%)
  between operations  0.83 us (1%)
  other arithmetic  0.67 us (1%)
    all_to_all x3, blocking collectives, redistribute(): return lax.all_to_all(x, axis, 0, 0, tiled=True, axis_index_groups=groups)  39.2 us
    pallas_call x7, Pallas kernels, run(): pl.pallas_call(kernel, out_shape=outs, in_specs=[pl.BlockSpec(memory_spac...  9.48 us
    ppermute x1, starting transfers between devices, beside(): return lax.ppermute(x, ('chip', 'core'), pairs + [(j, i) for i, j in pairs])  6.68 us
    ppermute x3, starting transfers between devices, over_depth(): return lax.ppermute(x, 'depth', [(i, i ^ mask) for i in range(count)])  5.97 us
  transfers between devices with their start and end apart: 6, of which 2 were waited for; matrix products, arithmetic and copies ran while one was open for 0% of the time, Pallas kernels for 11%

profile of v8, /device:TPU:16, one launch (start us, length us, event | category | flops | bytes accessed | tf_op | source)
XLA Modules:
  0.0 64.7 jit_solution(17484053159913286165)
XLA Ops:
  0.0 0.0 copy-start.8
  0.0 1.5 %collective-permute-start = (f32[32,128]{1,0:T(8,128)}, f32[32,128]{1,0:T(8,128)S(1)}, u32[]{:S(2)}, u32[]{:S(2)}) collective-permute-start(f32[32,128]{1,0:T(8,128)} %param.12), channel_id=1, source_target_pairs={{0,64},{32,96},{64,0},{96,32},{128,192},{160,224},{192,128},{224,1... | collective-permute-start | bytes 49160 | tf_op jit(solution)/shard_map/ppermute | solution.py:257
  1.5 6.7 %collective-permute-start.2 = (bf16[128,256]{1,0:T(8,128)(2,1)}, bf16[128,256]{1,0:T(8,128)(2,1)S(1)}, u32[]{:S(2)}, u32[]{:S(2)}) collective-permute-start(bf16[128,256]{1,0:T(8,128)(2,1)} %bitcast.8), channel_id=1, source_target_pairs={{1,2},{3,4},{5,6},{7,8},{9,10},{11,12},{13,14},{15,16},{17,18},{19... | collective-permute-start | bytes 196616 | tf_op jit(solution)/shard_map/ppermute | solution.py:262
  8.8 0.0 copy-start.6
  8.9 0.8 %copy-done.6 = bf16[128,256]{1,0:T(8,128)(2,1)S(1)} copy-done((bf16[128,256]{1,0:T(8,128)(2,1)S(1)}, bf16[128,256]{1,0:T(8,128)(2,1)}, u32[]{:S(2)}) %copy-start.6) | copy-done | bytes 65560
  9.7 0.0 copy-start.7
  9.7 1.1 %shard_map.100.shifts = bf16[8,512,256]{2,1,0:T(8,128)(2,1)S(1)} custom-call(bf16[128,256]{1,0:T(8,128)(2,1)S(1)} %copy-done.6), custom_call_target="tpu_custom_call" | custom-call | flops 268435456 | bytes 4194304 | tf_op jit(solution)/shard_map/pallas_call | solution.py:242
  10.8 0.0 collective-permute-done
  10.8 0.0 copy-done.7
  10.8 0.1 collective-permute-start.3
  10.9 0.0 copy-done.8
  10.9 2.3 %collective-permute-start.1 = (f32[2,32,128]{2,1,0:T(8,128)S(1)}, f32[2,32,128]{2,1,0:T(8,128)S(1)}, u32[]{:S(2)}, u32[]{:S(2)}) collective-permute-start(f32[2,32,128]{2,1,0:T(8,128)S(1)} %pad_maximum_fusion.2), channel_id=1, source_target_pairs={{0,32},{32,0},{64,96},{96,64},{128,160},{160,128},{192,224},{224,1... | collective-permute-start | bytes 98312 | tf_op jit(solution)/shard_map/ppermute | solution.py:257
  13.2 0.0 collective-permute-done.2.far
  13.2 0.0 collective-permute-done.3.near
  13.3 1.6 %shard_map.101 = (bf16[272,2048]{1,0:T(8,128)(2,1)S(1)}, f32[256,128]{1,0:T(8,128)S(1)}) custom-call(s32[1]{0:T(128)} %bitcast.core, bf16[128,256]{1,0:T(8,128)(2,1)S(1)} %collective-permute-done.2.far, bf16[128,256]{1,0:T(8,128)(2,1)S(1)} %collective-permute-done.3.near, bf16[128,256]{1,0:T(8,128)(2,1)S(1)} %bitcast.10, ...), custom_call_target="tpu_custom_call" | custom-call | flops 1140850688 | bytes 524288 | tf_op jit(solution)/shard_map/pallas_call | solution.py:242
  14.9 0.3 collective-permute-done.1
  15.2 0.0 copy-start
  15.2 0.0 copy-start.1
  15.2 2.2 %collective-permute-start.4 = (f32[4,32,128]{2,1,0:T(8,128)S(1)}, f32[4,32,128]{2,1,0:T(8,128)S(1)}, u32[]{:S(2)}, u32[]{:S(2)}) collective-permute-start(f32[4,32,128]{2,1,0:T(8,128)S(1)} %pad_maximum_fusion.1), channel_id=1, source_target_pairs={{0,192},{32,224},{64,128},{96,160},{128,64},{160,96},{192,0},{224,... | collective-permute-start | bytes 196616 | tf_op jit(solution)/shard_map/ppermute | solution.py:257
  17.4 2.9 %shard_map.102 = (f32[16,16,128]{2,1,0:T(8,128)S(1)}, f32[256,128]{1,0:T(8,128)S(1)}) custom-call(s32[1]{0:T(128)} %bitcast.core, bf16[272,2048]{1,0:T(8,128)(2,1)S(1)} %get-tuple-element.46.win, bf16[8,512,256]{2,1,0:T(8,128)(2,1)S(1)} %shard_map.100.shifts, f32[256,128]{1,0:T(8,128)S(1)} %get-tuple-element.39.even), custom_call_target="tpu_custom_call" | custom-call | flops 2281701376 | bytes 524288 | tf_op jit(solution)/shard_map/pallas_call | solution.py:242
  20.2 0.5 collective-permute-done.4
  20.8 0.0 copy-done
  20.8 0.0 copy-done.1
  20.8 0.7 %shard_map.103 = (f32[16,8,128]{2,1,0:T(8,128)S(1)}, f32[16,24,128]{2,1,0:T(8,128)S(1)}, f32[32,1024]{1,0:T(8,128)S(1)}, f32[32,1024]{1,0:T(8,128)S(1)}) custom-call(s32[1]{0:T(128)} %bitcast.1.first, s32[1]{0:T(128)} %bitcast.2.depth, s32[1]{0:T(128)} %bitcast.core, s32[1]{0:T(128)S(6)} %copy.11.defocus, f32[8,32,128]{2,1,0:T(8,128)S(1)} %pad_maximum_fusion.phase, ...), custom_call_target="tpu_custom_call" | custom-call | flops 201326592 | bytes 3145728 | tf_op jit(solution)/shard_map/pallas_call | solution.py:242
  21.5 0.1 collective-permute-start.5
  21.6 0.0 copy-start.2
  21.6 0.0 copy-start.3
  21.6 1.7 %shard_map.104 = f32[16,24,128]{2,1,0:T(8,128)S(1)} custom-call(s32[1]{0:T(128)} %bitcast.core, bf16[272,2048]{1,0:T(8,128)(2,1)S(1)} %get-tuple-element.46.win, bf16[8,512,256]{2,1,0:T(8,128)(2,1)S(1)} %shard_map.100.shifts, f32[256,128]{1,0:T(8,128)S(1)} %get-tuple-element.47.kept, f32[16,8,128]{2,1,0:T(8,128)S(1)} %get-tuple-element.48.keep_z), custom_call_target="tpu_custom_call" | custom-call | flops 1140850688 | bytes 524288 | tf_op jit(solution)/shard_map/pallas_call | solution.py:242
  23.3 0.0 collective-permute-done.5
  23.4 17.2 %all_to_all.15.payload = f32[16,24,128]{2,1,0:T(8,128)S(1)} all-to-all(f32[16,24,128]{2,1,0:T(8,128)S(1)} %add.7), channel_id=1, replica_groups={{30,28,26,24,22,20,18,16,14,12,10,8,6,4,2,0},{15,13,11,9,7,5,3,1,31,29,..., dimensions={0} | all-to-all | bytes 393216 | tf_op jit(solution)/shard_map/all_to_all | solution.py:266
  40.6 0.0 copy-done.2
  40.6 0.0 copy-done.3
  40.6 0.0 copy-start.4
  40.6 0.0 copy-start.5
  40.6 1.0 %shard_map.105 = f32[32,4,128]{2,1,0:T(4,128)S(1)} custom-call(s32[1]{0:T(128)} %bitcast.core, f32[16,24,128]{2,1,0:T(8,128)S(1)} %all_to_all.15.payload, bf16[1024,512]{1,0:T(8,128)(2,1)S(1)} %copy-done.1, bf16[1024,512]{1,0:T(8,128)(2,1)S(1)} %copy-done, bf16[256,2048]{1,0:T(8,128)(2,1)S(1)} %copy-done.3, bf16[256,2048]{1,0:T(8,128)(2,1)S(1)} %copy-done.2), custom_call_target="tpu_custom_call" | custom-call | flops 100663296 | bytes 5242880 | tf_op jit(solution)/shard_map/pallas_call | solution.py:242
  41.6 12.2 %all_to_all.16 = f32[32,4,128]{2,1,0:T(4,128)S(1)} all-to-all(f32[32,4,128]{2,1,0:T(4,128)S(1)} %shard_map.105), channel_id=1, replica_groups={{31,30,15,14,29,28,13,12,27,26,11,10,25,24,9,8,23,22,7,6,21,20,5,4,19,1..., dimensions={0} | all-to-all | bytes 131072 | tf_op jit(solution)/shard_map/all_to_all | solution.py:266
  53.8 0.0 copy-done.4
  53.8 0.0 copy-done.5
  53.8 0.5 shard_map.106
  54.3 9.8 %all_to_all.17 = f32[8,32,128]{2,1,0:T(8,128)S(1)} all-to-all(f32[8,32,128]{2,1,0:T(8,128)S(1)} %shard_map.106), channel_id=1, replica_groups={{224,192,160,128,96,64,32,0},{225,193,161,129,97,65,33,1},{226,194,162,..., dimensions={0} | all-to-all | bytes 262144 | tf_op jit(solution)/shard_map/all_to_all | solution.py:266
  64.1 0.6 reduce_sum.9
  (4 shorter events, 0.1 us)
Async XLA Ops:
  0.0 10.9 %copy-start.8 = (f32[32,128]{1,0:T(8,128)S(1)}, f32[32,128]{1,0:T(8,128)}, u32[]{:S(2)}) copy-start(f32[32,128]{1,0:T(8,128)} %param.12) | copy-start | bytes 49156
  0.0 10.8 %collective-permute-start = (f32[32,128]{1,0:T(8,128)}, f32[32,128]{1,0:T(8,128)S(1)}, u32[]{:S(2)}, u32[]{:S(2)}) collective-permute-start(f32[32,128]{1,0:T(8,128)} %param.12), channel_id=1, source_target_pairs={{0,64},{32,96},{64,0},{96,32},{128,192},{160,224},{192,128},{224,1... | collective-permute-start | bytes 49160 | tf_op jit(solution)/shard_map/ppermute | solution.py:257
  1.5 11.8 %collective-permute-start.2 = (bf16[128,256]{1,0:T(8,128)(2,1)}, bf16[128,256]{1,0:T(8,128)(2,1)S(1)}, u32[]{:S(2)}, u32[]{:S(2)}) collective-permute-start(bf16[128,256]{1,0:T(8,128)(2,1)} %bitcast.8), channel_id=1, source_target_pairs={{1,2},{3,4},{5,6},{7,8},{9,10},{11,12},{13,14},{15,16},{17,18},{19... | collective-permute-start | bytes 196616 | tf_op jit(solution)/shard_map/ppermute | solution.py:262
  8.8 0.8 %copy-start.6 = (bf16[128,256]{1,0:T(8,128)(2,1)S(1)}, bf16[128,256]{1,0:T(8,128)(2,1)}, u32[]{:S(2)}) copy-start(bf16[128,256]{1,0:T(8,128)(2,1)} %grad.1) | copy-start | bytes 196612
  9.7 1.1 %copy-start.7 = (bf16[1,128,256]{2,1,0:T(8,128)(2,1)S(1)}, bf16[1,128,256]{2,1,0:T(8,128)(2,1)}, u32[]{:S(2)}) copy-start(bf16[1,128,256]{2,1,0:T(8,128)(2,1)} %param.10) | copy-start | bytes 196612
  10.8 2.4 %collective-permute-start.3 = (bf16[128,256]{1,0:T(8,128)(2,1)S(1)}, bf16[128,256]{1,0:T(8,128)(2,1)S(1)}, u32[]{:S(2)}, u32[]{:S(2)}) collective-permute-start(bf16[128,256]{1,0:T(8,128)(2,1)S(1)} %bitcast.9), channel_id=1, source_target_pairs={{0,1},{1,0},{2,3},{3,2},{4,5},{5,4},{6,7},{7,6},{8,9},{9,8},{10,11... | collective-permute-start | bytes 196616 | tf_op jit(solution)/shard_map/ppermute | solution.py:270
  10.9 4.2 %collective-permute-start.1 = (f32[2,32,128]{2,1,0:T(8,128)S(1)}, f32[2,32,128]{2,1,0:T(8,128)S(1)}, u32[]{:S(2)}, u32[]{:S(2)}) collective-permute-start(f32[2,32,128]{2,1,0:T(8,128)S(1)} %pad_maximum_fusion.2), channel_id=1, source_target_pairs={{0,32},{32,0},{64,96},{96,64},{128,160},{160,128},{192,224},{224,1... | collective-permute-start | bytes 98312 | tf_op jit(solution)/shard_map/ppermute | solution.py:257
  15.2 5.6 %copy-start = (bf16[1024,512]{1,0:T(8,128)(2,1)S(1)}, bf16[1024,512]{1,0:T(8,128)(2,1)}, u32[]{:S(2)}) copy-start(bf16[1024,512]{1,0:T(8,128)(2,1)} %constant.34.clone.low.g_low) | copy-start | bytes 3145732
  15.2 5.6 %copy-start.1 = (bf16[1024,512]{1,0:T(8,128)(2,1)S(1)}, bf16[1024,512]{1,0:T(8,128)(2,1)}, u32[]{:S(2)}) copy-start(bf16[1024,512]{1,0:T(8,128)(2,1)} %constant.33.clone.high.g_high) | copy-start | bytes 3145732
  15.2 5.6 %collective-permute-start.4 = (f32[4,32,128]{2,1,0:T(8,128)S(1)}, f32[4,32,128]{2,1,0:T(8,128)S(1)}, u32[]{:S(2)}, u32[]{:S(2)}) collective-permute-start(f32[4,32,128]{2,1,0:T(8,128)S(1)} %pad_maximum_fusion.1), channel_id=1, source_target_pairs={{0,192},{32,224},{64,128},{96,160},{128,64},{160,96},{192,0},{224,... | collective-permute-start | bytes 196616 | tf_op jit(solution)/shard_map/ppermute | solution.py:257
  21.5 1.8 %collective-permute-start.5 = (f32[16,24,128]{2,1,0:T(8,128)S(1)}, f32[16,24,128]{2,1,0:T(8,128)S(1)}, u32[]{:S(2)}, u32[]{:S(2)}) collective-permute-start(f32[16,24,128]{2,1,0:T(8,128)S(1)} %get-tuple-element.45), channel_id=1, source_target_pairs={{0,1},{1,0},{2,3},{3,2},{4,5},{5,4},{6,7},{7,6},{8,9},{9,8},{10,11... | collective-permute-start | bytes 589832 | tf_op jit(solution)/shard_map/ppermute | solution.py:270
  21.6 19.0 %copy-start.2 = (bf16[256,2048]{1,0:T(8,128)(2,1)S(1)}, bf16[256,2048]{1,0:T(8,128)(2,1)}, u32[]{:S(2)}) copy-start(bf16[256,2048]{1,0:T(8,128)(2,1)} %constant.36.clone.s_low) | copy-start | bytes 3145732
  21.6 19.0 %copy-start.3 = (bf16[256,2048]{1,0:T(8,128)(2,1)S(1)}, bf16[256,2048]{1,0:T(8,128)(2,1)}, u32[]{:S(2)}) copy-start(bf16[256,2048]{1,0:T(8,128)(2,1)} %constant.35.clone.s_high) | copy-start | bytes 3145732
  40.6 13.2 %copy-start.4 = (bf16[256,2048]{1,0:T(8,128)(2,1)S(1)}, bf16[256,2048]{1,0:T(8,128)(2,1)}, u32[]{:S(2)}) copy-start(bf16[256,2048]{1,0:T(8,128)(2,1)} %constant.38.clone.low) | copy-start | bytes 3145732
  40.6 13.2 %copy-start.5 = (bf16[256,2048]{1,0:T(8,128)(2,1)S(1)}, bf16[256,2048]{1,0:T(8,128)(2,1)}, u32[]{:S(2)}) copy-start(bf16[256,2048]{1,0:T(8,128)(2,1)} %constant.37.clone.high) | copy-start | bytes 3145732

commit v9 on v3

--- a/solution.py
+++ b/solution.py
@@ -289,7 +289,7 @@
         2 * scene.shape[0] * FREQ * FREQ * GROUP,
         2**22,
     )(sensor_grad)
-    other, shifts, edge = lax.optimization_barrier((other, shifts, scene))
+    other, shifts, edge, index = lax.optimization_barrier((other, shifts, scene, defocus_index))
     near = swap(edge)
     gathered = jnp.stack([pupil_phase, other])
     beyond = over_depth(gathered, GATHER_MASKS[2])
@@ -320,7 +320,7 @@
         2 * 192 * PUPIL * 2 * FREQ,
         3 * 2**20,
         smem=4,
-    )(first_row, depth, core, defocus_index, gathered, send_k, g_high, g_low)
+    )(first_row, depth, core, index, gathered, send_k, g_high, g_low)
     send, win = lax.optimization_barrier((send, win))
     other = swap(send)
     keep = call(third_kernel, both, [], 4 * work, 2**19, smem=1)(core, win, shifts, even, keep_z)

time: 64.9 us -> 64.9 us (level)
  no operation moved by 1% of the time
where the time goes in v9:
time: 64.9 us; the launch traced here: 64.6 us
  blocking collectives  39.1 us (60%)
  starting transfers between devices  12.8 us (20%)
  Pallas kernels  9.45 us (15%)
  local copies, waits for them, and re-layouts  0.87 us (1%)
  between operations  0.84 us (1%)
  waiting for transfers between devices  0.83 us (1%)
  other arithmetic  0.66 us (1%)
    all_to_all x3, blocking collectives, redistribute(): lax.all_to_all(x, axis, 0, 0, tiled=True, axis_index_groups=[list(order)])  39.1 us
    pallas_call x7, Pallas kernels, run(): pl.pallas_call(kernel, out_shape=outs, in_specs=[pl.BlockSpec(memory_spac...  9.45 us
    ppermute x1, starting transfers between devices, beside(): return lax.ppermute(x, ('chip', 'core'), pairs + [(j, i) for i, j in pairs])  6.68 us
    ppermute x3, starting transfers between devices, over_depth(): return lax.ppermute(x, 'depth', [(i, i ^ mask) for i in range(count)])  5.97 us
  transfers between devices with their start and end apart: 6, of which 2 were waited for; matrix products, arithmetic and copies ran while one was open for 0% of the time, Pallas kernels for 11%

profile of v9, /device:TPU:16, one launch (start us, length us, event | category | flops | bytes accessed | tf_op | source)
XLA Modules:
  0.0 64.6 jit_solution(15140980954086773788)
XLA Ops:
  0.0 0.0 copy-start.8
  0.0 1.5 %collective-permute-start = (f32[32,128]{1,0:T(8,128)}, f32[32,128]{1,0:T(8,128)S(1)}, u32[]{:S(2)}, u32[]{:S(2)}) collective-permute-start(f32[32,128]{1,0:T(8,128)} %param.12), channel_id=1, source_target_pairs={{0,64},{32,96},{64,0},{96,32},{128,192},{160,224},{192,128},{224,1... | collective-permute-start | bytes 49160 | tf_op jit(solution)/shard_map/ppermute | solution.py:254
  1.5 6.7 %collective-permute-start.2 = (bf16[128,256]{1,0:T(8,128)(2,1)}, bf16[128,256]{1,0:T(8,128)(2,1)S(1)}, u32[]{:S(2)}, u32[]{:S(2)}) collective-permute-start(bf16[128,256]{1,0:T(8,128)(2,1)} %bitcast.8), channel_id=1, source_target_pairs={{1,2},{3,4},{5,6},{7,8},{9,10},{11,12},{13,14},{15,16},{17,18},{19... | collective-permute-start | bytes 196616 | tf_op jit(solution)/shard_map/ppermute | solution.py:259
  8.8 0.0 copy-start.6
  8.9 0.8 %copy-done.6 = bf16[128,256]{1,0:T(8,128)(2,1)S(1)} copy-done((bf16[128,256]{1,0:T(8,128)(2,1)S(1)}, bf16[128,256]{1,0:T(8,128)(2,1)}, u32[]{:S(2)}) %copy-start.6) | copy-done | bytes 65560
  9.7 0.0 copy-start.7
  9.7 1.1 %shard_map.100.shifts = bf16[8,512,256]{2,1,0:T(8,128)(2,1)S(1)} custom-call(bf16[128,256]{1,0:T(8,128)(2,1)S(1)} %copy-done.6), custom_call_target="tpu_custom_call" | custom-call | flops 268435456 | bytes 4194304 | tf_op jit(solution)/shard_map/pallas_call | solution.py:239
  10.8 0.0 collective-permute-done
  10.8 0.0 copy-done.7
  10.8 0.1 collective-permute-start.3
  10.9 0.0 copy-done.8
  10.9 2.3 %collective-permute-start.1 = (f32[2,32,128]{2,1,0:T(8,128)S(1)}, f32[2,32,128]{2,1,0:T(8,128)S(1)}, u32[]{:S(2)}, u32[]{:S(2)}) collective-permute-start(f32[2,32,128]{2,1,0:T(8,128)S(1)} %pad_maximum_fusion.2), channel_id=1, source_target_pairs={{0,32},{32,0},{64,96},{96,64},{128,160},{160,128},{192,224},{224,1... | collective-permute-start | bytes 98312 | tf_op jit(solution)/shard_map/ppermute | solution.py:254
  13.2 0.0 collective-permute-done.2.far
  13.2 0.0 collective-permute-done.3.near
  13.3 1.6 %shard_map.101 = (bf16[272,2048]{1,0:T(8,128)(2,1)S(1)}, f32[256,128]{1,0:T(8,128)S(1)}) custom-call(s32[1]{0:T(128)} %bitcast.2.core, bf16[128,256]{1,0:T(8,128)(2,1)S(1)} %collective-permute-done.2.far, bf16[128,256]{1,0:T(8,128)(2,1)S(1)} %collective-permute-done.3.near, bf16[128,256]{1,0:T(8,128)(2,1)S(1)} %bitcast.10, ...), custom_call_target="tpu_custom_call" | custom-call | flops 1140850688 | bytes 524288 | tf_op jit(solution)/shard_map/pallas_call | solution.py:239
  14.9 0.3 collective-permute-done.1
  15.2 0.0 copy-start
  15.2 0.0 copy-start.1
  15.2 2.2 %collective-permute-start.4 = (f32[4,32,128]{2,1,0:T(8,128)S(1)}, f32[4,32,128]{2,1,0:T(8,128)S(1)}, u32[]{:S(2)}, u32[]{:S(2)}) collective-permute-start(f32[4,32,128]{2,1,0:T(8,128)S(1)} %pad_maximum_fusion.1), channel_id=1, source_target_pairs={{0,192},{32,224},{64,128},{96,160},{128,64},{160,96},{192,0},{224,... | collective-permute-start | bytes 196616 | tf_op jit(solution)/shard_map/ppermute | solution.py:254
  17.4 2.9 %shard_map.102 = (f32[16,16,128]{2,1,0:T(8,128)S(1)}, f32[256,128]{1,0:T(8,128)S(1)}) custom-call(s32[1]{0:T(128)} %bitcast.2.core, bf16[272,2048]{1,0:T(8,128)(2,1)S(1)} %get-tuple-element.48.win, bf16[8,512,256]{2,1,0:T(8,128)(2,1)S(1)} %shard_map.100.shifts, f32[256,128]{1,0:T(8,128)S(1)} %get-tuple-element.41.even), custom_call_target="tpu_custom_call" | custom-call | flops 2281701376 | bytes 524288 | tf_op jit(solution)/shard_map/pallas_call | solution.py:239
  20.2 0.5 collective-permute-done.4
  20.8 0.0 copy-done
  20.8 0.0 copy-done.1
  20.8 0.7 %shard_map.103 = (f32[16,8,128]{2,1,0:T(8,128)S(1)}, f32[16,24,128]{2,1,0:T(8,128)S(1)}, f32[32,1024]{1,0:T(8,128)S(1)}, f32[32,1024]{1,0:T(8,128)S(1)}) custom-call(s32[1]{0:T(128)} %bitcast.first, s32[1]{0:T(128)} %bitcast.1.depth, s32[1]{0:T(128)} %bitcast.2.core, s32[1]{0:T(128)S(6)} %copy.11.defocus, f32[8,32,128]{2,1,0:T(8,128)S(1)} %pad_maximum_fusion.phase, ...), custom_call_target="tpu_custom_call" | custom-call | flops 201326592 | bytes 3145728 | tf_op jit(solution)/shard_map/pallas_call | solution.py:239
  21.5 0.1 collective-permute-start.5
  21.6 0.0 copy-start.2
  21.6 0.0 copy-start.3
  21.6 1.7 %shard_map.104 = f32[16,24,128]{2,1,0:T(8,128)S(1)} custom-call(s32[1]{0:T(128)} %bitcast.2.core, bf16[272,2048]{1,0:T(8,128)(2,1)S(1)} %get-tuple-element.48.win, bf16[8,512,256]{2,1,0:T(8,128)(2,1)S(1)} %shard_map.100.shifts, f32[256,128]{1,0:T(8,128)S(1)} %get-tuple-element.49.kept, f32[16,8,128]{2,1,0:T(8,128)S(1)} %get-tuple-element.50.keep_z), custom_call_target="tpu_custom_call" | custom-call | flops 1140850688 | bytes 524288 | tf_op jit(solution)/shard_map/pallas_call | solution.py:239
  23.3 0.0 collective-permute-done.5
  23.4 16.5 %all_to_all.15.payload = f32[16,24,128]{2,1,0:T(8,128)S(1)} all-to-all(f32[16,24,128]{2,1,0:T(8,128)S(1)} %add.7), channel_id=1, replica_groups={{30,14,28,12,26,10,24,8,22,6,20,4,18,2,16,0},{31,15,29,13,27,11,25,9,23..., dimensions={0} | all-to-all | bytes 393216 | tf_op jit(solution)/shard_map/all_to_all | solution.py:263
  39.9 0.0 copy-done.2
  39.9 0.0 copy-done.3
  39.9 0.0 copy-start.4
  39.9 0.0 copy-start.5
  39.9 1.0 %shard_map.105 = f32[32,4,128]{2,1,0:T(4,128)S(1)} custom-call(f32[16,24,128]{2,1,0:T(8,128)S(1)} %all_to_all.15.payload, bf16[1024,512]{1,0:T(8,128)(2,1)S(1)} %copy-done.1, bf16[1024,512]{1,0:T(8,128)(2,1)S(1)} %copy-done, bf16[256,2048]{1,0:T(8,128)(2,1)S(1)} %copy-done.3, bf16[256,2048]{1,0:T(8,128)(2,1)S(1)} %copy-done.2), custom_call_target="tpu_custom_call" | custom-call | flops 100663296 | bytes 5242880 | tf_op jit(solution)/shard_map/pallas_call | solution.py:239
  40.9 12.8 %all_to_all.16 = f32[32,4,128]{2,1,0:T(4,128)S(1)} all-to-all(f32[32,4,128]{2,1,0:T(4,128)S(1)} %shard_map.105), channel_id=1, replica_groups={{31,30,15,14,29,28,13,12,27,26,11,10,25,24,9,8,23,22,7,6,21,20,5,4,19,1..., dimensions={0} | all-to-all | bytes 131072 | tf_op jit(solution)/shard_map/all_to_all | solution.py:263
  53.7 0.0 copy-done.4
  53.7 0.0 copy-done.5
  53.7 0.5 shard_map.106
  54.2 9.8 %all_to_all.17 = f32[8,32,128]{2,1,0:T(8,128)S(1)} all-to-all(f32[8,32,128]{2,1,0:T(8,128)S(1)} %shard_map.106), channel_id=1, replica_groups={{224,192,160,128,96,64,32,0},{225,193,161,129,97,65,33,1},{226,194,162,..., dimensions={0} | all-to-all | bytes 262144 | tf_op jit(solution)/shard_map/all_to_all | solution.py:263
  64.0 0.6 reduce_sum.9
  (4 shorter events, 0.0 us)
Async XLA Ops:
  0.0 10.9 %copy-start.8 = (f32[32,128]{1,0:T(8,128)S(1)}, f32[32,128]{1,0:T(8,128)}, u32[]{:S(2)}) copy-start(f32[32,128]{1,0:T(8,128)} %param.12) | copy-start | bytes 49156
  0.0 10.8 %collective-permute-start = (f32[32,128]{1,0:T(8,128)}, f32[32,128]{1,0:T(8,128)S(1)}, u32[]{:S(2)}, u32[]{:S(2)}) collective-permute-start(f32[32,128]{1,0:T(8,128)} %param.12), channel_id=1, source_target_pairs={{0,64},{32,96},{64,0},{96,32},{128,192},{160,224},{192,128},{224,1... | collective-permute-start | bytes 49160 | tf_op jit(solution)/shard_map/ppermute | solution.py:254
  1.5 11.8 %collective-permute-start.2 = (bf16[128,256]{1,0:T(8,128)(2,1)}, bf16[128,256]{1,0:T(8,128)(2,1)S(1)}, u32[]{:S(2)}, u32[]{:S(2)}) collective-permute-start(bf16[128,256]{1,0:T(8,128)(2,1)} %bitcast.8), channel_id=1, source_target_pairs={{1,2},{3,4},{5,6},{7,8},{9,10},{11,12},{13,14},{15,16},{17,18},{19... | collective-permute-start | bytes 196616 | tf_op jit(solution)/shard_map/ppermute | solution.py:259
  8.8 0.8 %copy-start.6 = (bf16[128,256]{1,0:T(8,128)(2,1)S(1)}, bf16[128,256]{1,0:T(8,128)(2,1)}, u32[]{:S(2)}) copy-start(bf16[128,256]{1,0:T(8,128)(2,1)} %grad.1) | copy-start | bytes 196612
  9.7 1.1 %copy-start.7 = (bf16[1,128,256]{2,1,0:T(8,128)(2,1)S(1)}, bf16[1,128,256]{2,1,0:T(8,128)(2,1)}, u32[]{:S(2)}) copy-start(bf16[1,128,256]{2,1,0:T(8,128)(2,1)} %param.10) | copy-start | bytes 196612
  10.8 2.4 %collective-permute-start.3 = (bf16[128,256]{1,0:T(8,128)(2,1)S(1)}, bf16[128,256]{1,0:T(8,128)(2,1)S(1)}, u32[]{:S(2)}, u32[]{:S(2)}) collective-permute-start(bf16[128,256]{1,0:T(8,128)(2,1)S(1)} %bitcast.9), channel_id=1, source_target_pairs={{0,1},{1,0},{2,3},{3,2},{4,5},{5,4},{6,7},{7,6},{8,9},{9,8},{10,11... | collective-permute-start | bytes 196616 | tf_op jit(solution)/shard_map/ppermute | solution.py:267
  10.9 4.2 %collective-permute-start.1 = (f32[2,32,128]{2,1,0:T(8,128)S(1)}, f32[2,32,128]{2,1,0:T(8,128)S(1)}, u32[]{:S(2)}, u32[]{:S(2)}) collective-permute-start(f32[2,32,128]{2,1,0:T(8,128)S(1)} %pad_maximum_fusion.2), channel_id=1, source_target_pairs={{0,32},{32,0},{64,96},{96,64},{128,160},{160,128},{192,224},{224,1... | collective-permute-start | bytes 98312 | tf_op jit(solution)/shard_map/ppermute | solution.py:254
  15.2 5.6 %copy-start = (bf16[1024,512]{1,0:T(8,128)(2,1)S(1)}, bf16[1024,512]{1,0:T(8,128)(2,1)}, u32[]{:S(2)}) copy-start(bf16[1024,512]{1,0:T(8,128)(2,1)} %constant.34.clone.low.g_low) | copy-start | bytes 3145732
  15.2 5.6 %copy-start.1 = (bf16[1024,512]{1,0:T(8,128)(2,1)S(1)}, bf16[1024,512]{1,0:T(8,128)(2,1)}, u32[]{:S(2)}) copy-start(bf16[1024,512]{1,0:T(8,128)(2,1)} %constant.33.clone.high.g_high) | copy-start | bytes 3145732
  15.2 5.6 %collective-permute-start.4 = (f32[4,32,128]{2,1,0:T(8,128)S(1)}, f32[4,32,128]{2,1,0:T(8,128)S(1)}, u32[]{:S(2)}, u32[]{:S(2)}) collective-permute-start(f32[4,32,128]{2,1,0:T(8,128)S(1)} %pad_maximum_fusion.1), channel_id=1, source_target_pairs={{0,192},{32,224},{64,128},{96,160},{128,64},{160,96},{192,0},{224,... | collective-permute-start | bytes 196616 | tf_op jit(solution)/shard_map/ppermute | solution.py:254
  21.5 1.8 %collective-permute-start.5 = (f32[16,24,128]{2,1,0:T(8,128)S(1)}, f32[16,24,128]{2,1,0:T(8,128)S(1)}, u32[]{:S(2)}, u32[]{:S(2)}) collective-permute-start(f32[16,24,128]{2,1,0:T(8,128)S(1)} %get-tuple-element.47), channel_id=1, source_target_pairs={{0,1},{1,0},{2,3},{3,2},{4,5},{5,4},{6,7},{7,6},{8,9},{9,8},{10,11... | collective-permute-start | bytes 589832 | tf_op jit(solution)/shard_map/ppermute | solution.py:267
  21.6 18.3 %copy-start.2 = (bf16[256,2048]{1,0:T(8,128)(2,1)S(1)}, bf16[256,2048]{1,0:T(8,128)(2,1)}, u32[]{:S(2)}) copy-start(bf16[256,2048]{1,0:T(8,128)(2,1)} %constant.36.clone.s_low) | copy-start | bytes 3145732
  21.6 18.3 %copy-start.3 = (bf16[256,2048]{1,0:T(8,128)(2,1)S(1)}, bf16[256,2048]{1,0:T(8,128)(2,1)}, u32[]{:S(2)}) copy-start(bf16[256,2048]{1,0:T(8,128)(2,1)} %constant.35.clone.s_high) | copy-start | bytes 3145732
  39.9 13.8 %copy-start.4 = (bf16[256,2048]{1,0:T(8,128)(2,1)S(1)}, bf16[256,2048]{1,0:T(8,128)(2,1)}, u32[]{:S(2)}) copy-start(bf16[256,2048]{1,0:T(8,128)(2,1)} %constant.38.clone.low) | copy-start | bytes 3145732
  39.9 13.8 %copy-start.5 = (bf16[256,2048]{1,0:T(8,128)(2,1)S(1)}, bf16[256,2048]{1,0:T(8,128)(2,1)}, u32[]{:S(2)}) copy-start(bf16[256,2048]{1,0:T(8,128)(2,1)} %constant.37.clone.high) | copy-start | bytes 3145732

commit v10 on v3

--- a/solution.py
+++ b/solution.py
@@ -12,8 +12,10 @@
 FREQ = 2 * HALF
 GROUP = 16
 GATHER_MASKS = (0, 2, 1, 3, 6, 4, 7, 5)
-CHIP_ORDER = tuple(8 * y + z for z in reversed(range(8)) for y in (1, 0))
-TILE_ORDER = tuple(2 * chip + core for chip in CHIP_ORDER for core in (1, 0))
+CHIP_ORDER = tuple(reversed(range(16)))
+TILE_ORDER = tuple(
+    16 * y + 2 * z + core for z in reversed(range(8)) for y in (1, 0) for core in (1, 0)
+)
 DEPTH_ORDER = tuple(reversed(range(8)))
 EVEN, ODD = (0, 2, 4, 6), (1, 3, 5, 7)
 WINDOW = FREQ + GROUP

time: 64.9 us -> 64.9 us (level)
  no operation moved by 1% of the time
where the time goes in v10:
time: 64.9 us; the launch traced here: 64.6 us
  blocking collectives  39.1 us (60%)
  starting transfers between devices  12.8 us (20%)
  Pallas kernels  9.46 us (15%)
  local copies, waits for them, and re-layouts  0.87 us (1%)
  between operations  0.84 us (1%)
  waiting for transfers between devices  0.83 us (1%)
  other arithmetic  0.66 us (1%)
    all_to_all x3, blocking collectives, redistribute(): lax.all_to_all(x, axis, 0, 0, tiled=True, axis_index_groups=[list(order)])  39.1 us
    pallas_call x7, Pallas kernels, run(): pl.pallas_call(kernel, out_shape=outs, in_specs=[pl.BlockSpec(memory_spac...  9.46 us
    ppermute x1, starting transfers between devices, beside(): return lax.ppermute(x, ('chip', 'core'), pairs + [(j, i) for i, j in pairs])  6.68 us
    ppermute x3, starting transfers between devices, over_depth(): return lax.ppermute(x, 'depth', [(i, i ^ mask) for i in range(count)])  5.97 us
  transfers between devices with their start and end apart: 6, of which 2 were waited for; matrix products, arithmetic and copies ran while one was open for 0% of the time, Pallas kernels for 11%

profile of v10, /device:TPU:16, one launch (start us, length us, event | category | flops | bytes accessed | tf_op | source)
XLA Modules:
  0.0 64.6 jit_solution(7478873023273605455)
XLA Ops:
  0.0 0.0 copy-start.8
  0.0 1.5 %collective-permute-start = (f32[32,128]{1,0:T(8,128)}, f32[32,128]{1,0:T(8,128)S(1)}, u32[]{:S(2)}, u32[]{:S(2)}) collective-permute-start(f32[32,128]{1,0:T(8,128)} %param.12), channel_id=1, source_target_pairs={{0,64},{32,96},{64,0},{96,32},{128,192},{160,224},{192,128},{224,1... | collective-permute-start | bytes 49160 | tf_op jit(solution)/shard_map/ppermute | solution.py:256
  1.5 6.7 %collective-permute-start.2 = (bf16[128,256]{1,0:T(8,128)(2,1)}, bf16[128,256]{1,0:T(8,128)(2,1)S(1)}, u32[]{:S(2)}, u32[]{:S(2)}) collective-permute-start(bf16[128,256]{1,0:T(8,128)(2,1)} %bitcast.8), channel_id=1, source_target_pairs={{1,2},{3,4},{5,6},{7,8},{9,10},{11,12},{13,14},{15,16},{17,18},{19... | collective-permute-start | bytes 196616 | tf_op jit(solution)/shard_map/ppermute | solution.py:261
  8.8 0.0 copy-start.6
  8.9 0.8 %copy-done.6 = bf16[128,256]{1,0:T(8,128)(2,1)S(1)} copy-done((bf16[128,256]{1,0:T(8,128)(2,1)S(1)}, bf16[128,256]{1,0:T(8,128)(2,1)}, u32[]{:S(2)}) %copy-start.6) | copy-done | bytes 65560
  9.7 0.0 copy-start.7
  9.7 1.1 %shard_map.100.shifts = bf16[8,512,256]{2,1,0:T(8,128)(2,1)S(1)} custom-call(bf16[128,256]{1,0:T(8,128)(2,1)S(1)} %copy-done.6), custom_call_target="tpu_custom_call" | custom-call | flops 268435456 | bytes 4194304 | tf_op jit(solution)/shard_map/pallas_call | solution.py:241
  10.8 0.0 collective-permute-done
  10.8 0.0 copy-done.7
  10.8 0.1 collective-permute-start.3
  10.9 0.0 copy-done.8
  10.9 2.3 %collective-permute-start.1 = (f32[2,32,128]{2,1,0:T(8,128)S(1)}, f32[2,32,128]{2,1,0:T(8,128)S(1)}, u32[]{:S(2)}, u32[]{:S(2)}) collective-permute-start(f32[2,32,128]{2,1,0:T(8,128)S(1)} %pad_maximum_fusion.2), channel_id=1, source_target_pairs={{0,32},{32,0},{64,96},{96,64},{128,160},{160,128},{192,224},{224,1... | collective-permute-start | bytes 98312 | tf_op jit(solution)/shard_map/ppermute | solution.py:256
  13.2 0.0 collective-permute-done.2.far
  13.2 0.0 collective-permute-done.3.near
  13.3 1.6 %shard_map.101 = (bf16[272,2048]{1,0:T(8,128)(2,1)S(1)}, f32[256,128]{1,0:T(8,128)S(1)}) custom-call(s32[1]{0:T(128)} %bitcast.2.core, bf16[128,256]{1,0:T(8,128)(2,1)S(1)} %collective-permute-done.2.far, bf16[128,256]{1,0:T(8,128)(2,1)S(1)} %collective-permute-done.3.near, bf16[128,256]{1,0:T(8,128)(2,1)S(1)} %bitcast.10, ...), custom_call_target="tpu_custom_call" | custom-call | flops 1140850688 | bytes 524288 | tf_op jit(solution)/shard_map/pallas_call | solution.py:241
  14.9 0.3 collective-permute-done.1
  15.2 0.0 copy-start
  15.2 0.0 copy-start.1
  15.2 2.2 %collective-permute-start.4 = (f32[4,32,128]{2,1,0:T(8,128)S(1)}, f32[4,32,128]{2,1,0:T(8,128)S(1)}, u32[]{:S(2)}, u32[]{:S(2)}) collective-permute-start(f32[4,32,128]{2,1,0:T(8,128)S(1)} %pad_maximum_fusion.1), channel_id=1, source_target_pairs={{0,192},{32,224},{64,128},{96,160},{128,64},{160,96},{192,0},{224,... | collective-permute-start | bytes 196616 | tf_op jit(solution)/shard_map/ppermute | solution.py:256
  17.4 2.9 %shard_map.102 = (f32[16,16,128]{2,1,0:T(8,128)S(1)}, f32[256,128]{1,0:T(8,128)S(1)}) custom-call(s32[1]{0:T(128)} %bitcast.2.core, bf16[272,2048]{1,0:T(8,128)(2,1)S(1)} %get-tuple-element.46.win, bf16[8,512,256]{2,1,0:T(8,128)(2,1)S(1)} %shard_map.100.shifts, f32[256,128]{1,0:T(8,128)S(1)} %get-tuple-element.39.even), custom_call_target="tpu_custom_call" | custom-call | flops 2281701376 | bytes 524288 | tf_op jit(solution)/shard_map/pallas_call | solution.py:241
  20.2 0.5 collective-permute-done.4
  20.8 0.0 copy-done
  20.8 0.0 copy-done.1
  20.8 0.7 %shard_map.103 = (f32[16,8,128]{2,1,0:T(8,128)S(1)}, f32[16,24,128]{2,1,0:T(8,128)S(1)}, f32[32,1024]{1,0:T(8,128)S(1)}, f32[32,1024]{1,0:T(8,128)S(1)}) custom-call(s32[1]{0:T(128)} %bitcast.first, s32[1]{0:T(128)} %bitcast.1.depth, s32[1]{0:T(128)} %bitcast.2.core, s32[1]{0:T(128)S(6)} %copy.11.defocus, f32[8,32,128]{2,1,0:T(8,128)S(1)} %pad_maximum_fusion.phase, ...), custom_call_target="tpu_custom_call" | custom-call | flops 201326592 | bytes 3145728 | tf_op jit(solution)/shard_map/pallas_call | solution.py:241
  21.5 0.1 collective-permute-start.5
  21.6 0.0 copy-start.2
  21.6 0.0 copy-start.3
  21.6 1.7 %shard_map.104 = f32[16,24,128]{2,1,0:T(8,128)S(1)} custom-call(s32[1]{0:T(128)} %bitcast.2.core, bf16[272,2048]{1,0:T(8,128)(2,1)S(1)} %get-tuple-element.46.win, bf16[8,512,256]{2,1,0:T(8,128)(2,1)S(1)} %shard_map.100.shifts, f32[256,128]{1,0:T(8,128)S(1)} %get-tuple-element.47.kept, f32[16,8,128]{2,1,0:T(8,128)S(1)} %get-tuple-element.48.keep_z), custom_call_target="tpu_custom_call" | custom-call | flops 1140850688 | bytes 524288 | tf_op jit(solution)/shard_map/pallas_call | solution.py:241
  23.3 0.0 collective-permute-done.5
  23.4 17.1 %all_to_all.15.payload = f32[16,24,128]{2,1,0:T(8,128)S(1)} all-to-all(f32[16,24,128]{2,1,0:T(8,128)S(1)} %add.7), channel_id=1, replica_groups={{30,28,26,24,22,20,18,16,14,12,10,8,6,4,2,0},{31,29,27,25,23,21,19,17,1..., dimensions={0} | all-to-all | bytes 393216 | tf_op jit(solution)/shard_map/all_to_all | solution.py:265
  40.5 0.0 copy-done.2
  40.5 0.0 copy-done.3
  40.5 0.0 copy-start.4
  40.5 0.0 copy-start.5
  40.5 1.0 %shard_map.105 = f32[32,4,128]{2,1,0:T(4,128)S(1)} custom-call(f32[16,24,128]{2,1,0:T(8,128)S(1)} %all_to_all.15.payload, bf16[1024,512]{1,0:T(8,128)(2,1)S(1)} %copy-done.1, bf16[1024,512]{1,0:T(8,128)(2,1)S(1)} %copy-done, bf16[256,2048]{1,0:T(8,128)(2,1)S(1)} %copy-done.3, bf16[256,2048]{1,0:T(8,128)(2,1)S(1)} %copy-done.2), custom_call_target="tpu_custom_call" | custom-call | flops 100663296 | bytes 5242880 | tf_op jit(solution)/shard_map/pallas_call | solution.py:241
  41.5 12.2 %all_to_all.16 = f32[32,4,128]{2,1,0:T(4,128)S(1)} all-to-all(f32[32,4,128]{2,1,0:T(4,128)S(1)} %shard_map.105), channel_id=1, replica_groups={{31,30,15,14,29,28,13,12,27,26,11,10,25,24,9,8,23,22,7,6,21,20,5,4,19,1..., dimensions={0} | all-to-all | bytes 131072 | tf_op jit(solution)/shard_map/all_to_all | solution.py:265
  53.7 0.0 copy-done.4
  53.7 0.0 copy-done.5
  53.7 0.5 shard_map.106
  54.2 9.8 %all_to_all.17 = f32[8,32,128]{2,1,0:T(8,128)S(1)} all-to-all(f32[8,32,128]{2,1,0:T(8,128)S(1)} %shard_map.106), channel_id=1, replica_groups={{224,192,160,128,96,64,32,0},{225,193,161,129,97,65,33,1},{226,194,162,..., dimensions={0} | all-to-all | bytes 262144 | tf_op jit(solution)/shard_map/all_to_all | solution.py:265
  64.0 0.6 reduce_sum.9
  (4 shorter events, 0.0 us)
Async XLA Ops:
  0.0 10.9 %copy-start.8 = (f32[32,128]{1,0:T(8,128)S(1)}, f32[32,128]{1,0:T(8,128)}, u32[]{:S(2)}) copy-start(f32[32,128]{1,0:T(8,128)} %param.12) | copy-start | bytes 49156
  0.0 10.8 %collective-permute-start = (f32[32,128]{1,0:T(8,128)}, f32[32,128]{1,0:T(8,128)S(1)}, u32[]{:S(2)}, u32[]{:S(2)}) collective-permute-start(f32[32,128]{1,0:T(8,128)} %param.12), channel_id=1, source_target_pairs={{0,64},{32,96},{64,0},{96,32},{128,192},{160,224},{192,128},{224,1... | collective-permute-start | bytes 49160 | tf_op jit(solution)/shard_map/ppermute | solution.py:256
  1.5 11.8 %collective-permute-start.2 = (bf16[128,256]{1,0:T(8,128)(2,1)}, bf16[128,256]{1,0:T(8,128)(2,1)S(1)}, u32[]{:S(2)}, u32[]{:S(2)}) collective-permute-start(bf16[128,256]{1,0:T(8,128)(2,1)} %bitcast.8), channel_id=1, source_target_pairs={{1,2},{3,4},{5,6},{7,8},{9,10},{11,12},{13,14},{15,16},{17,18},{19... | collective-permute-start | bytes 196616 | tf_op jit(solution)/shard_map/ppermute | solution.py:261
  8.8 0.8 %copy-start.6 = (bf16[128,256]{1,0:T(8,128)(2,1)S(1)}, bf16[128,256]{1,0:T(8,128)(2,1)}, u32[]{:S(2)}) copy-start(bf16[128,256]{1,0:T(8,128)(2,1)} %grad.1) | copy-start | bytes 196612
  9.7 1.1 %copy-start.7 = (bf16[1,128,256]{2,1,0:T(8,128)(2,1)S(1)}, bf16[1,128,256]{2,1,0:T(8,128)(2,1)}, u32[]{:S(2)}) copy-start(bf16[1,128,256]{2,1,0:T(8,128)(2,1)} %param.10) | copy-start | bytes 196612
  10.8 2.4 %collective-permute-start.3 = (bf16[128,256]{1,0:T(8,128)(2,1)S(1)}, bf16[128,256]{1,0:T(8,128)(2,1)S(1)}, u32[]{:S(2)}, u32[]{:S(2)}) collective-permute-start(bf16[128,256]{1,0:T(8,128)(2,1)S(1)} %bitcast.9), channel_id=1, source_target_pairs={{0,1},{1,0},{2,3},{3,2},{4,5},{5,4},{6,7},{7,6},{8,9},{9,8},{10,11... | collective-permute-start | bytes 196616 | tf_op jit(solution)/shard_map/ppermute | solution.py:269
  10.9 4.2 %collective-permute-start.1 = (f32[2,32,128]{2,1,0:T(8,128)S(1)}, f32[2,32,128]{2,1,0:T(8,128)S(1)}, u32[]{:S(2)}, u32[]{:S(2)}) collective-permute-start(f32[2,32,128]{2,1,0:T(8,128)S(1)} %pad_maximum_fusion.2), channel_id=1, source_target_pairs={{0,32},{32,0},{64,96},{96,64},{128,160},{160,128},{192,224},{224,1... | collective-permute-start | bytes 98312 | tf_op jit(solution)/shard_map/ppermute | solution.py:256
  15.2 5.6 %copy-start = (bf16[1024,512]{1,0:T(8,128)(2,1)S(1)}, bf16[1024,512]{1,0:T(8,128)(2,1)}, u32[]{:S(2)}) copy-start(bf16[1024,512]{1,0:T(8,128)(2,1)} %constant.34.clone.low.g_low) | copy-start | bytes 3145732
  15.2 5.6 %copy-start.1 = (bf16[1024,512]{1,0:T(8,128)(2,1)S(1)}, bf16[1024,512]{1,0:T(8,128)(2,1)}, u32[]{:S(2)}) copy-start(bf16[1024,512]{1,0:T(8,128)(2,1)} %constant.33.clone.high.g_high) | copy-start | bytes 3145732
  15.2 5.6 %collective-permute-start.4 = (f32[4,32,128]{2,1,0:T(8,128)S(1)}, f32[4,32,128]{2,1,0:T(8,128)S(1)}, u32[]{:S(2)}, u32[]{:S(2)}) collective-permute-start(f32[4,32,128]{2,1,0:T(8,128)S(1)} %pad_maximum_fusion.1), channel_id=1, source_target_pairs={{0,192},{32,224},{64,128},{96,160},{128,64},{160,96},{192,0},{224,... | collective-permute-start | bytes 196616 | tf_op jit(solution)/shard_map/ppermute | solution.py:256
  21.5 1.8 %collective-permute-start.5 = (f32[16,24,128]{2,1,0:T(8,128)S(1)}, f32[16,24,128]{2,1,0:T(8,128)S(1)}, u32[]{:S(2)}, u32[]{:S(2)}) collective-permute-start(f32[16,24,128]{2,1,0:T(8,128)S(1)} %get-tuple-element.45), channel_id=1, source_target_pairs={{0,1},{1,0},{2,3},{3,2},{4,5},{5,4},{6,7},{7,6},{8,9},{9,8},{10,11... | collective-permute-start | bytes 589832 | tf_op jit(solution)/shard_map/ppermute | solution.py:269
  21.6 18.9 %copy-start.2 = (bf16[256,2048]{1,0:T(8,128)(2,1)S(1)}, bf16[256,2048]{1,0:T(8,128)(2,1)}, u32[]{:S(2)}) copy-start(bf16[256,2048]{1,0:T(8,128)(2,1)} %constant.36.clone.s_low) | copy-start | bytes 3145732
  21.6 18.9 %copy-start.3 = (bf16[256,2048]{1,0:T(8,128)(2,1)S(1)}, bf16[256,2048]{1,0:T(8,128)(2,1)}, u32[]{:S(2)}) copy-start(bf16[256,2048]{1,0:T(8,128)(2,1)} %constant.35.clone.s_high) | copy-start | bytes 3145732
  40.5 13.2 %copy-start.4 = (bf16[256,2048]{1,0:T(8,128)(2,1)S(1)}, bf16[256,2048]{1,0:T(8,128)(2,1)}, u32[]{:S(2)}) copy-start(bf16[256,2048]{1,0:T(8,128)(2,1)} %constant.38.clone.low) | copy-start | bytes 3145732
  40.5 13.2 %copy-start.5 = (bf16[256,2048]{1,0:T(8,128)(2,1)S(1)}, bf16[256,2048]{1,0:T(8,128)(2,1)}, u32[]{:S(2)}) copy-start(bf16[256,2048]{1,0:T(8,128)(2,1)} %constant.37.clone.high) | copy-start | bytes 3145732
